TPU v7x, 256 devices: a whole 4x4x8 slice. The times are simulated.
256 devices in a mesh: row: 16 (over x, z_lo, core), col: 16 (over y, z_hi).
Axes of the slice: x: 4, y: 4, z: 8 (z_hi: 4, z_lo: 2; z = z_hi * 2 + z_lo), core: 2. Of those that a mesh axis runs over, the one named last changes fastest.
Arguments:
- tiles: float32 [16, 16, 128, 128, 128], P('row', 'col'), may hold values from -0.125 to 0.125
- tile_rows: int32 [16, 16, 128], P('row', 'col'), may hold values from 0 to 63, as said below
- tile_cols: int32 [16, 16, 128], P('row', 'col'), may hold values from 0 to 63, as said below
- tile_counts: int32 [16, 16], P('row', 'col'), may hold values from 1 to 128, as said below
- vectors: float32 [8, 131072], P(None, ('row', 'col')), may hold values from -6 to 6
Outputs:
- product: float32 [8, 131072], P(None, ('row', 'col'))
Inputs may be any that keep to these rules, and one draw needn't show every extreme that they name: `tile_counts`: each device has 1 to 128 live slots; the target count of grid row r is the ceiling of 128 * (r + 1) / 16 less a jitter of 0 to 32, at least 1; one device of the last grid row has exactly 128. `tile_rows`: live slots of a device name distinct tiles on or below the block diagonal (global block row at least global block column); slots past the count hold 0. `tile_cols`: drawn together with tile_rows; slots past the count hold 0.
All inputs are finite; a program needn't handle non-finite values.
Results may differ from a plain program's by a relative error of at most 0.0003.
Values sent between devices are 32-bit elements; how exact they have to be, the bound alone decides.
No kernel may reach another device: no remote copies, remote signals or barrier semaphores. Data moves between devices by JAX's collectives and lax.ppermute only.
A program may use at most 64 MiB of HBM per device.

v0:
```python
import jax
import jax.numpy as jnp
from jax import lax
from jax.sharding import PartitionSpec as P


def tile_products(blocks, rows, cols, row_inputs, col_inputs):
    from_cols = jnp.take(col_inputs, cols, axis=1)
    from_rows = jnp.take(row_inputs, rows, axis=1)
    first = jnp.einsum("tab,ktb->kta", blocks, from_cols, precision=lax.Precision.HIGHEST)
    second = jnp.einsum("tab,kta->ktb", blocks, from_rows, precision=lax.Precision.HIGHEST)
    return (first, second)


def block_sums(terms, labels, valid, count):
    targets = jnp.arange(count, dtype=jnp.int32)
    hits = ((labels[:, None] == targets[None, :]) & valid[:, None]).astype(jnp.float32)
    return jnp.einsum("kta,ti->ika", terms, hits, precision=lax.Precision.HIGHEST)


def body(tiles, tile_rows, tile_cols, tile_counts, vectors):
    blocks = tiles[0, 0]
    rows = tile_rows[0, 0]
    cols = tile_cols[0, 0]
    count = tile_counts[0, 0]
    vector_count, width = vectors.shape
    tile_side = blocks.shape[1]
    row_devices = lax.axis_size("row")
    column_devices = lax.axis_size("col")
    local_blocks = width // tile_side
    row_blocks = column_devices * local_blocks
    col_blocks = row_devices * local_blocks
    valid = jnp.arange(blocks.shape[0], dtype=jnp.int32) < count
    col_inputs = lax.all_gather(vectors, "row", axis=1, tiled=True).reshape(
        vector_count, col_blocks, tile_side
    )
    row_inputs = lax.all_gather(vectors, "col", axis=1, tiled=True).reshape(
        vector_count, row_blocks, tile_side
    )
    first, second = tile_products(blocks, rows, cols, row_inputs, col_inputs)
    row_part = jnp.transpose(block_sums(first, rows, valid, row_blocks), (1, 0, 2))
    col_part = jnp.transpose(block_sums(second, cols, valid, col_blocks), (1, 0, 2))
    row_total = lax.psum_scatter(
        row_part.reshape(vector_count, row_blocks * tile_side),
        "col",
        scatter_dimension=1,
        tiled=True,
    )
    col_total = lax.psum_scatter(
        col_part.reshape(vector_count, col_blocks * tile_side),
        "row",
        scatter_dimension=1,
        tiled=True,
    )
    result = row_total + col_total
    return result


def solution(mesh):
    in_specs = (
        P("row", "col", None, None, None),
        P("row", "col", None),
        P("row", "col", None),
        P("row", "col"),
        P(None, ("row", "col")),
    )
    out_specs = P(None, ("row", "col"))
    return jax.shard_map(body, mesh=mesh, in_specs=in_specs, out_specs=out_specs, check_vma=False)
```

profile of v0, /device:TPU:1, one launch (start us, length us, event | category | flops | bytes accessed | tf_op | source)
XLA Modules:
  0.0 219.9 jit_solution(1657220787556363010)
XLA Ops:
  6.5 0.0 copy-start
  6.5 0.0 copy-start.1
  6.5 0.0 reduce-scatter.5.cloned.1.call-start
  6.5 0.7 compare_and_fusion
  7.2 0.7 compare_select_fusion
  8.6 42.2 %all_gather.7 = f32[8,8192]{1,0:T(8,128)S(1)} all-gather(f32[8,512]{1,0:T(8,128)} %param.11), channel_id=1, replica_groups=mesh['row'=16,'col'=16] {'col'}, dimensions={1}, use_global_device_ids=true | all-gather | bytes 278528 | tf_op jit(solution)/shard_map/all_gather | solution.py:37
  50.8 0.8 gather_fusion.1
  51.6 9.4 %fusion = f32[128,8,128]{2,1,0:T(8,128)S(1)} fusion(f32[1,1,128,128,128]{4,3,2,1,0:T(8,128)} %param.7, f32[128,8,128]{2,1,0:T(8,128)S(1)} %gather_fusion.1, pred[128]{0:T(512)(128)(4,1)S(1)} %compare_and_fusion), kind=kOutput, calls=%fused_computation.2 | convolution fusion | flops 201457664 | bytes 9437312 | tf_op jit(solution)/shard_map/tab,kta->ktb/dot_general | solution.py:11
  61.0 0.0 copy-start.2
  61.0 0.0 copy-done.1
  61.0 0.4 convolution_bitcast_fusion
  61.4 0.8 copy.20
  62.2 0.0 reduce-scatter.5.cloned.1.call-update
  62.2 0.0 reduce-scatter.3.cloned.1.call-start
  62.3 0.0 copy-done
  62.3 27.9 %all_gather.6 = f32[8,8192]{1,0:T(8,128)S(1)} all-gather(f32[8,512]{1,0:T(8,128)S(1)} %copy-done), channel_id=1, replica_groups=mesh['row'=16,'col'=16] {'row'}, dimensions={1}, use_global_device_ids=true | all-gather | bytes 278528 | tf_op jit(solution)/shard_map/all_gather | solution.py:34
  90.2 0.8 gather_fusion
  91.0 15.5 %fusion.2 = f32[128,8,128]{2,1,0:T(8,128)S(1)} fusion(f32[1,1,128,128,128]{4,3,2,1,0:T(8,128)} %param.7, f32[128,8,128]{2,1,0:T(8,128)S(1)} %gather_fusion, pred[128]{0:T(512)(128)(4,1)S(1)} %compare_and_fusion.1), kind=kOutput, calls=%fused_computation.4 | convolution fusion | flops 201457664 | bytes 9437312 | tf_op jit(solution)/shard_map/tab,ktb->kta/dot_general | solution.py:10
  106.5 0.0 copy-done.2
  106.5 0.4 convolution_bitcast_fusion.1
  106.9 0.8 copy.21
  107.7 0.0 reduce-scatter.3.cloned.1.call-update
  107.7 15.6 %reduce-scatter.5.cloned.1.call-done = f32[8,512]{1,0:T(8,128)} async-done(((f32[8,8192]{1,0:T(8,128)}), f32[8,512]{1,0:T(8,128)}) %reduce-scatter.5.cloned.1.call-update) | async-done | bytes 16400 | tf_op jit(solution)/shard_map/reduce_scatter | solution.py:49
  123.3 88.4 %reduce-scatter.3.cloned.1.call-done = f32[8,512]{1,0:T(8,128)} async-done(((f32[8,8192]{1,0:T(8,128)}), f32[8,512]{1,0:T(8,128)}) %reduce-scatter.3.cloned.1.call-update) | async-done | bytes 16400 | tf_op jit(solution)/shard_map/reduce_scatter | solution.py:43
  211.7 1.3 add.13
  (5 shorter events, 0.0 us)
Async XLA Ops:
  6.5 55.8 %copy-start = (f32[8,512]{1,0:T(8,128)S(1)}, f32[8,512]{1,0:T(8,128)}, u32[]{:S(2)}) copy-start(f32[8,512]{1,0:T(8,128)} %param.11) | copy-start | bytes 49156
  6.5 54.4 %copy-start.1 = (s32[1,1,128]{2,1,0:T(1,128)S(1)}, s32[1,1,128]{2,1,0:T(1,128)}, u32[]{:S(2)}) copy-start(s32[1,1,128]{2,1,0:T(1,128)} %param.9) | copy-start | bytes 1540
  6.5 116.8 %reduce-scatter.5.cloned.1.call-start = ((), (), s32[]{:S(2)}) async-start(), calls=%async_computation.3 | async-start | bytes 278528 | tf_op jit(solution)/shard_map/reduce_scatter | solution.py:49
  61.0 45.5 %copy-start.2 = (s32[1,1,128]{2,1,0:T(1,128)S(1)}, s32[1,1,128]{2,1,0:T(1,128)}, u32[]{:S(2)}) copy-start(s32[1,1,128]{2,1,0:T(1,128)} %param.8) | copy-start | bytes 1540
  62.2 149.5 %reduce-scatter.3.cloned.1.call-start = ((), (), s32[]{:S(2)}) async-start(), calls=%async_computation.2 | async-start | bytes 278528 | tf_op jit(solution)/shard_map/reduce_scatter | solution.py:43
Sparse Core Ops, SparseCore 0:
  62.4 60.9 reduce-scatter.4
  127.2 84.4 reduce-scatter.2
where the time goes:
time: 221 us; the launch traced here: 220 us
  waiting for transfers between devices  104 us (47%)
  blocking collectives  70.1 us (32%)
  matrix products  25.7 us (12%)
  between operations  14.1 us (6%)
  local copies, waits for them, and re-layouts  3.22 us (1%)
  other arithmetic  2.71 us (1%)
    reduce_scatter x1, waiting for transfers between devices, body(): lax.psum_scatter(row_part.reshape(vector_count, row_blocks * tile_side),...  88.4 us
    all_gather x1, blocking collectives, body(): lax.all_gather(vectors, 'col', axis=1, tiled=True)  42.2 us
    all_gather x1, blocking collectives, body(): lax.all_gather(vectors, 'row', axis=1, tiled=True)  27.9 us
    reduce_scatter x1, waiting for transfers between devices, body(): lax.psum_scatter(col_part.reshape(vector_count, col_blocks * tile_side),...  15.6 us
    dot_general x1, matrix products, tile_products(): jnp.einsum('tab,ktb->kta', blocks, from_cols, precision=lax.Precision.HIG...  15.5 us
    dot_general x1, matrix products, tile_products(): jnp.einsum('tab,kta->ktb', blocks, from_rows, precision=lax.Precision.HIG...  9.39 us
  transfers between devices with their start and end apart: 2, of which 2 were waited for; matrix products, arithmetic and copies ran while one was open for 8% of the time, Pallas kernels for 0%

commit v1 on v0

v1 whole, which is shorter than its diff:
```python
import jax
import jax.numpy as jnp
from jax import lax
from jax.experimental import pallas as pl
from jax.experimental.pallas import tpu as pltpu
from jax.sharding import PartitionSpec as P

GROUP = 8


def split(value):
    high = value.astype(jnp.bfloat16)
    low = (value - high.astype(jnp.float32)).astype(jnp.bfloat16)
    return high, low


def tile_kernel(rows, cols, count, row_inputs, col_inputs, tiles, row_part, col_part,
                held, row_split, col_split, row_sum, col_sum, arrived):
    slots = held.shape[0]
    side = held.shape[1]
    groups = slots // GROUP
    blocks = row_inputs.shape[0]

    def fetch(group):
        place = pl.ds(group * GROUP, GROUP)
        return pltpu.make_async_copy(tiles.at[place], held.at[place], arrived.at[group])

    for group in range(groups):
        fetch(group).start()
    for source, target in ((row_inputs, row_split), (col_inputs, col_split)):
        high, low = split(source[...])
        target[...] = jnp.concatenate([high, low], axis=1)
    row_sum[...] = jnp.zeros_like(row_sum)
    col_sum[...] = jnp.zeros_like(col_sum)
    live = count[0]

    def step(group, carry):
        fetch(group).wait()
        results = []
        for offset in range(GROUP):
            slot = group * GROUP + offset
            row = rows[slot]
            col = cols[slot]
            high, low = split(held[slot])
            from_cols = col_split[col]
            from_rows = row_split[row]
            first = lax.dot_general(
                jnp.concatenate([from_cols, from_cols], axis=1),
                jnp.concatenate([high, low], axis=1),
                (((1,), (1,)), ((), ())),
                preferred_element_type=jnp.float32,
            )
            second = lax.dot_general(
                jnp.concatenate([from_rows, from_rows], axis=1),
                jnp.concatenate([high, low], axis=0),
                (((1,), (0,)), ((), ())),
                preferred_element_type=jnp.float32,
            )
            dead = slot >= live
            results.append((jnp.where(dead, blocks, row), jnp.where(dead, blocks, col),
                            first[:8] + first[8:], second[:8] + second[8:]))
        for row, col, first, second in results:
            row_sum[row] += first
            col_sum[col] += second
        return carry

    lax.fori_loop(0, groups, step, 0)
    row_part[...] = row_sum[:blocks]
    col_part[...] = col_sum[:blocks]


def multiply(tiles, rows, cols, count, row_inputs, col_inputs):
    slots, side, _ = tiles.shape
    blocks, vectors, _ = row_inputs.shape
    part = jax.ShapeDtypeStruct((blocks, vectors, side), jnp.float32)
    smem = pl.BlockSpec(memory_space=pltpu.SMEM)
    vmem = pl.BlockSpec(memory_space=pltpu.VMEM)
    return pl.pallas_call(
        tile_kernel,
        out_shape=(part, part),
        in_specs=[smem, smem, smem, vmem, vmem, pl.BlockSpec(memory_space=pl.ANY)],
        out_specs=(vmem, vmem),
        scratch_shapes=[
            pltpu.VMEM((slots, side, side), jnp.float32),
            pltpu.VMEM((blocks, 2 * vectors, side), jnp.bfloat16),
            pltpu.VMEM((blocks, 2 * vectors, side), jnp.bfloat16),
            pltpu.VMEM((blocks + 8, vectors, side), jnp.float32),
            pltpu.VMEM((blocks + 8, vectors, side), jnp.float32),
            pltpu.SemaphoreType.DMA((slots // GROUP,)),
        ],
        compiler_params=pltpu.CompilerParams(vmem_limit_bytes=20 * 1024 * 1024),
        cost_estimate=pl.CostEstimate(flops=4 * 16 * 256 * side * slots, bytes_accessed=4 * slots * side * side, transcendentals=0),
    )(rows, cols, count, row_inputs, col_inputs, tiles)


def body(tiles, tile_rows, tile_cols, tile_counts, vectors):
    vector_count, width = vectors.shape
    side = tiles.shape[-1]
    local_blocks = width // side
    row_devices = lax.axis_size("row")
    col_devices = lax.axis_size("col")
    own = vectors.reshape(vector_count, local_blocks, side).transpose(1, 0, 2)

    def gather(axis, devices):
        copies = jnp.broadcast_to(own[None], (devices, *own.shape)).reshape(-1, vector_count, side)
        return lax.all_to_all(copies, axis, 0, 0, tiled=True)

    col_inputs = gather("row", row_devices)
    row_inputs = gather("col", col_devices)
    row_part, col_part = multiply(tiles[0, 0], tile_rows[0, 0], tile_cols[0, 0], tile_counts[0], row_inputs, col_inputs)
    row_terms = lax.all_to_all(row_part, "col", 0, 0, tiled=True)
    col_terms = lax.all_to_all(col_part, "row", 0, 0, tiled=True)
    total = row_terms.reshape(col_devices, *own.shape).sum(0) + col_terms.reshape(row_devices, *own.shape).sum(0)
    return total.transpose(1, 0, 2).reshape(vector_count, width)


def solution(mesh):
    in_specs = (
        P("row", "col", None, None, None),
        P("row", "col", None),
        P("row", "col", None),
        P("row", "col"),
        P(None, ("row", "col")),
    )
    out_specs = P(None, ("row", "col"))
    return jax.shard_map(body, mesh=mesh, in_specs=in_specs, out_specs=out_specs, check_vma=False)
```

time: 221 us -> 79.4 us (0.36)
  waiting for transfers between devices: 104 us -> 17.9 us
  blocking collectives: 70.1 us -> 29.4 us
  matrix products: 25.7 us -> 0 us
  starting transfers between devices: 0.04 us -> 16.4 us
  between operations: 14.1 us -> 0.67 us
  Pallas kernels: 0 us -> 7.58 us
  local copies, waits for them, and re-layouts: 3.22 us -> 6.12 us
    reduce_scatter x2 -> x0, waiting for transfers between devices: 104 us -> none  [the longest x1 88.4 us: body(): lax.psum_scatter(row_part.reshape(vector_count, row_blocks * tile_side),...]
    all_gather x2 -> x0, blocking collectives: 70.1 us -> none  [the longest x1 42.2 us: body(): lax.all_gather(vectors, 'col', axis=1, tiled=True)]
    all_to_all x0 -> x2, blocking collectives: none -> 29.4 us  [the longest x1 15.1 us: body(): row_terms = lax.all_to_all(row_part, 'col', 0, 0, tiled=True)]
    dot_general x4 -> x0, matrix products: 25.7 us -> none  [the longest x1 15.5 us: tile_products(): jnp.einsum('tab,ktb->kta', blocks, from_cols, precision=lax.Precision.HIG...]
    all_to_all x0 -> x2, waiting for transfers between devices: none -> 17.9 us  [the longest x1 10.8 us: gather(): return lax.all_to_all(copies, axis, 0, 0, tiled=True)]
    all_to_all x0 -> x2, starting transfers between devices: none -> 16.4 us  [the longest x1 10 us: gather(): return lax.all_to_all(copies, axis, 0, 0, tiled=True)]
    pallas_call x0 -> x1, Pallas kernels: none -> 7.58 us  [multiply(): pl.pallas_call(tile_kernel, out_shape=(part, part), in_specs=[smem, smem,...]
    unnamed x8 -> x6, local copies, waits for them, and re-layouts: 1.7 us -> 4.69 us
  transfers between devices with their start and end apart: 2 -> 2, of which waited for: 2 -> 2; matrix products, arithmetic and copies ran while one was open for 8% -> 0% of each run, Pallas kernels for 0% -> 0%
where the time goes in v1:
time: 79.4 us; the launch traced here: 78.8 us
  blocking collectives  29.4 us (37%)
  waiting for transfers between devices  17.9 us (23%)
  starting transfers between devices  16.4 us (21%)
  Pallas kernels  7.58 us (10%)
  local copies, waits for them, and re-layouts  6.12 us (8%)
    all_to_all x1, blocking collectives, body(): row_terms = lax.all_to_all(row_part, 'col', 0, 0, tiled=True)  15.1 us
    all_to_all x1, blocking collectives, gather(): return lax.all_to_all(copies, axis, 0, 0, tiled=True)  14.3 us
    all_to_all x1, waiting for transfers between devices, gather(): return lax.all_to_all(copies, axis, 0, 0, tiled=True)  10.8 us
    all_to_all x1, starting transfers between devices, gather(): return lax.all_to_all(copies, axis, 0, 0, tiled=True)  10 us
    pallas_call x1, Pallas kernels, multiply(): pl.pallas_call(tile_kernel, out_shape=(part, part), in_specs=[smem, smem,...  7.58 us
    all_to_all x1, waiting for transfers between devices, body(): col_terms = lax.all_to_all(col_part, 'row', 0, 0, tiled=True)  7.15 us
    all_to_all x1, starting transfers between devices, body(): col_terms = lax.all_to_all(col_part, 'row', 0, 0, tiled=True)  6.37 us
    unnamed x6, local copies, waits for them, and re-layouts  4.69 us
  transfers between devices with their start and end apart: 2, of which 2 were waited for; matrix products, arithmetic and copies ran while one was open for 0% of the time, Pallas kernels for 0%

profile of v1, /device:TPU:1, one launch (start us, length us, event | category | flops | bytes accessed | tf_op | source)
XLA Modules:
  0.0 78.8 jit_solution(7573332043688520090)
XLA Ops:
  0.0 1.4 %broadcast_in_dim.2 = f32[16,4,8,128]{3,2,1,0:T(8,128)} broadcast(f32[4,8,128]{2,1,0:T(8,128)} %bitcast.20), dimensions={1,2,3} | broadcast | bytes 278528 | tf_op jit(solution)/shard_map/broadcast_in_dim | solution.py:105
  1.4 14.3 %all_to_all.20.col_inputs = f32[64,8,128]{2,1,0:T(8,128)S(1)} all-to-all(f32[64,8,128]{2,1,0:T(8,128)} %bitcast.5), channel_id=1, replica_groups=mesh['row'=16,'col'=16] {'row'}, dimensions={0} | all-to-all | bytes 524288 | tf_op jit(solution)/shard_map/all_to_all | solution.py:106
  15.8 10.0 %all-to-all-start = ((f32[64,8,128]{2,1,0:T(8,128)}), f32[64,8,128]{2,1,0:T(8,128)S(1)}, u32[]{:S(2)}, u32[]{:S(2)}) async-start(f32[64,8,128]{2,1,0:T(8,128)} %bitcast.5), calls=%async_computation | async-start | bytes 524288 | tf_op jit(solution)/shard_map/all_to_all | solution.py:106
  26.4 10.8 %all-to-all-done.row_inputs = f32[64,8,128]{2,1,0:T(8,128)S(1)} async-done(((f32[64,8,128]{2,1,0:T(8,128)}), f32[64,8,128]{2,1,0:T(8,128)S(1)}, u32[]{:S(2)}, u32[]{:S(2)}) %all-to-all-start) | async-done | bytes 262176 | tf_op jit(solution)/shard_map/all_to_all | solution.py:106
  37.2 0.0 copy-start
  37.2 3.4 %copy-done = f32[1,1,128,128,128]{4,3,2,1,0:T(8,128)S(1)} copy-done((f32[1,1,128,128,128]{4,3,2,1,0:T(8,128)S(1)}, f32[1,1,128,128,128]{4,3,2,1,0:T(8,128)}, u32[]{:S(2)}) %copy-start) | copy-done | bytes 8388632
  40.6 0.0 copy-start.1
  40.6 0.7 copy-done.1
  41.3 0.0 copy-start.2
  41.3 0.7 copy-done.2
  41.9 7.6 %shard_map.55 = (f32[64,8,128]{2,1,0:T(8,128)S(1)}, f32[64,8,128]{2,1,0:T(8,128)}) custom-call(s32[128]{0:T(128)S(1)} %bitcast.16, s32[128]{0:T(128)S(1)} %bitcast.17, s32[1]{0:T(128)} %bitcast.14.count, f32[64,8,128]{2,1,0:T(8,128)S(1)} %all-to-all-done.row_inputs, f32[64,8,128]{2,1,0:T(8,128)S(1)} %all_to_all.20.col_inputs, f32[128,128,128]{2,1,0:T(8,128)S(1)} %bitcast.15), custom_call_target="tpu_custom_call" | custom-call | flops 268435456 | bytes 8388608 | tf_op jit(solution)/shard_map/pallas_call | solution.py:78
  49.5 15.1 %all_to_all.21 = f32[64,8,128]{2,1,0:T(8,128)S(1)} all-to-all(f32[64,8,128]{2,1,0:T(8,128)S(1)} %get-tuple-element.7), channel_id=1, replica_groups=mesh['row'=16,'col'=16] {'col'}, dimensions={0} | all-to-all | bytes 524288 | tf_op jit(solution)/shard_map/all_to_all | solution.py:111
  64.6 6.4 %all-to-all-start.3 = ((f32[64,8,128]{2,1,0:T(8,128)}), f32[64,8,128]{2,1,0:T(8,128)S(1)}, u32[]{:S(2)}, u32[]{:S(2)}) async-start(f32[64,8,128]{2,1,0:T(8,128)} %get-tuple-element.8), calls=%async_computation.3 | async-start | bytes 524288 | tf_op jit(solution)/shard_map/all_to_all | solution.py:112
  71.0 7.1 %all-to-all-done.3 = f32[64,8,128]{2,1,0:T(8,128)S(1)} async-done(((f32[64,8,128]{2,1,0:T(8,128)}), f32[64,8,128]{2,1,0:T(8,128)S(1)}, u32[]{:S(2)}, u32[]{:S(2)}) %all-to-all-start.3) | async-done | bytes 262176 | tf_op jit(solution)/shard_map/all_to_all | solution.py:112
  78.1 0.6 add_bitcast_fusion
  (2 shorter events, 0.0 us)
Async XLA Ops:
  15.8 21.5 %all-to-all-start = ((f32[64,8,128]{2,1,0:T(8,128)}), f32[64,8,128]{2,1,0:T(8,128)S(1)}, u32[]{:S(2)}, u32[]{:S(2)}) async-start(f32[64,8,128]{2,1,0:T(8,128)} %bitcast.5), calls=%async_computation | async-start | bytes 524288 | tf_op jit(solution)/shard_map/all_to_all | solution.py:106
  37.2 3.4 %copy-start = (f32[1,1,128,128,128]{4,3,2,1,0:T(8,128)S(1)}, f32[1,1,128,128,128]{4,3,2,1,0:T(8,128)}, u32[]{:S(2)}) copy-start(f32[1,1,128,128,128]{4,3,2,1,0:T(8,128)} %param.5) | copy-start | bytes 25165828
  40.6 0.7 copy-start.1
  41.3 0.7 copy-start.2
  64.6 13.5 %all-to-all-start.3 = ((f32[64,8,128]{2,1,0:T(8,128)}), f32[64,8,128]{2,1,0:T(8,128)S(1)}, u32[]{:S(2)}, u32[]{:S(2)}) async-start(f32[64,8,128]{2,1,0:T(8,128)} %get-tuple-element.8), calls=%async_computation.3 | async-start | bytes 524288 | tf_op jit(solution)/shard_map/all_to_all | solution.py:112

commit v2 on v1

v2 whole, which is shorter than its diff:
```python
import functools

import jax
import jax.numpy as jnp
from jax import lax
from jax.experimental import pallas as pl
from jax.experimental.pallas import tpu as pltpu
from jax.sharding import PartitionSpec as P

CHUNK = 16
AHEAD = 3
SLIM = 62
TLIM = 48
JOIN = 5 * 10 ** 10
FLOPS = 4 * 16 * 256 * 128 * 128
SMEM = pl.BlockSpec(memory_space=pltpu.SMEM)
VMEM = pl.BlockSpec(memory_space=pltpu.VMEM)
ANY = pl.BlockSpec(memory_space=pl.ANY)


def split(value):
    high = value.astype(jnp.bfloat16)
    low = (value - high.astype(jnp.float32)).astype(jnp.bfloat16)
    return high, low


def tile_kernel(inputs, outputs, *refs):
    places, tiles, row_source = refs[:3]
    col_sources = refs[3:3 + inputs]
    row_part = refs[3 + inputs]
    col_parts = refs[4 + inputs:4 + inputs + outputs]
    held, row_split, col_split, row_sum, col_sum, arrived = refs[4 + inputs + outputs:]
    slots = held.shape[0]
    chunks = slots // CHUNK
    vectors = row_sum.shape[1]

    def fetch(chunk):
        place = pl.ds(chunk * CHUNK, CHUNK)
        return pltpu.make_async_copy(tiles.at[place], held.at[place], arrived.at[chunk])

    for chunk in range(AHEAD):
        fetch(chunk).start()
    for sources, parts in (((row_source,), row_split), (col_sources, col_split)):
        start = 0
        for source in sources:
            high, low = split(source[...])
            parts[start:start + source.shape[0]] = jnp.concatenate([high, low], axis=1)
            start += source.shape[0]
        parts[start] = jnp.zeros_like(parts[start])
    row_sum[...] = jnp.zeros_like(row_sum)
    col_sum[...] = jnp.zeros_like(col_sum)

    def step(chunk, carry):
        fetch(chunk).wait()

        @pl.when(chunk + AHEAD < chunks)
        def _():
            fetch(chunk + AHEAD).start()

        results = []
        for offset in range(CHUNK):
            slot = chunk * CHUNK + offset
            place = places[slot]
            row, col = place // 128, place % 128
            high, low = split(held[slot])
            from_cols = col_split[col]
            from_rows = row_split[row]
            first = lax.dot_general(
                jnp.concatenate([from_cols, from_cols], axis=1),
                jnp.concatenate([high, low], axis=1),
                (((1,), (1,)), ((), ())), preferred_element_type=jnp.float32,
            )
            second = lax.dot_general(
                jnp.concatenate([from_rows, from_rows], axis=1),
                jnp.concatenate([high, low], axis=0),
                (((1,), (0,)), ((), ())), preferred_element_type=jnp.float32,
            )
            results.append((row, col, first[:vectors] + first[vectors:], second[:vectors] + second[vectors:]))
        for row, col, first, second in results:
            row_sum[row] += first
            col_sum[col] += second
        return carry

    lax.fori_loop(0, chunks, step, 0)
    row_part[...] = row_sum[:row_part.shape[0]]
    start = 0
    for part in col_parts:
        part[...] = col_sum[start:start + part.shape[0]]
        start += part.shape[0]


def multiply(places, tiles, row_input, col_inputs):
    slots, side, _ = tiles.shape
    row_blocks, vectors, _ = row_input.shape
    col_blocks = sum(part.shape[0] for part in col_inputs)
    parts = [jax.ShapeDtypeStruct(part.shape, jnp.float32) for part in [row_input, *col_inputs]]
    row_part, *col_parts = pl.pallas_call(
        functools.partial(tile_kernel, len(col_inputs), len(col_inputs)),
        out_shape=parts,
        in_specs=[SMEM, ANY, VMEM] + [VMEM] * len(col_inputs),
        out_specs=[VMEM] * len(parts),
        scratch_shapes=[
            pltpu.VMEM(tiles.shape, jnp.float32),
            pltpu.VMEM((row_blocks + 8, 2 * vectors, side), jnp.bfloat16),
            pltpu.VMEM((col_blocks + 8, 2 * vectors, side), jnp.bfloat16),
            pltpu.VMEM((row_blocks + 8, vectors, side), jnp.float32),
            pltpu.VMEM((col_blocks + 8, vectors, side), jnp.float32),
            pltpu.SemaphoreType.DMA((slots // CHUNK,)),
        ],
        compiler_params=pltpu.CompilerParams(vmem_limit_bytes=TLIM * 1024 * 1024),
        cost_estimate=pl.CostEstimate(flops=FLOPS, bytes_accessed=4 * slots * side * side, transcendentals=0),
    )(places, tiles, row_input, *col_inputs)
    return row_part, col_parts


def spread_kernel(own, out, local, arrived):
    fetch = pltpu.make_async_copy(own, local, arrived)
    fetch.start()
    fetch.wait()
    size = local.shape[0]
    value = local[...]
    for index in range(out.shape[0] // size):
        out[index * size:(index + 1) * size] = value


def spread(own, devices):
    return pl.pallas_call(
        spread_kernel,
        out_shape=[
            jax.ShapeDtypeStruct((devices * own.shape[0], *own.shape[1:]), own.dtype),
            jax.ShapeDtypeStruct(own.shape, own.dtype),
        ],
        in_specs=[ANY],
        out_specs=[VMEM, VMEM],
        scratch_shapes=[pltpu.SemaphoreType.DMA],
        compiler_params=pltpu.CompilerParams(vmem_limit_bytes=SLIM * 1024 * 1024),
    )(own)


def join_kernel(*refs):
    out = refs[-1]
    start = 0
    for part in refs[:-1]:
        out[start:start + part.shape[0]] = part[...]
        start += part.shape[0]


def join(parts):
    size = sum(part.shape[0] for part in parts)
    return pl.pallas_call(
        join_kernel,
        out_shape=jax.ShapeDtypeStruct((size, *parts[0].shape[1:]), parts[0].dtype),
        in_specs=[VMEM] * len(parts),
        out_specs=VMEM,
        compiler_params=pltpu.CompilerParams(vmem_limit_bytes=4 * 1024 * 1024),
        cost_estimate=pl.CostEstimate(flops=JOIN, bytes_accessed=1024, transcendentals=0),
    )(*parts)


def body(tiles, tile_rows, tile_cols, tile_counts, vectors):
    vector_count, width = vectors.shape
    slots, side = tiles.shape[2:4]
    local_blocks = width // side
    row_devices = lax.axis_size("row")
    col_devices = lax.axis_size("col")
    near = 4
    own = vectors.reshape(vector_count, local_blocks, side).transpose(1, 0, 2)

    def swap(value, offset):
        return lax.ppermute(value, "row", [(j, j ^ offset) for j in range(row_devices)])

    me = lax.axis_index("row")
    slot = jnp.arange(slots, dtype=jnp.int32)
    cols = tile_cols[0, 0]
    rel = ((cols // local_blocks) ^ me) * local_blocks + cols % local_blocks
    row_blocks = col_devices * local_blocks
    col_blocks = row_devices * local_blocks
    places = jnp.where(slot < tile_counts[0, 0], tile_rows[0, 0] * 128 + rel, row_blocks * 128 + col_blocks)

    copies, local = spread(own, col_devices)
    row_input = lax.all_to_all(copies, "col", 0, 0, tiled=True)
    close = join([local] + [swap(own, offset) for offset in range(1, near)])
    col_inputs = [close] + [swap(close, offset) for offset in range(near, row_devices, near)]
    row_part, col_parts = multiply(places, tiles[0, 0], row_input, col_inputs)
    row_terms = lax.all_to_all(row_part, "col", 0, 0, tiled=True)
    far = col_parts[0]
    for index in range(1, row_devices // near):
        far = far + swap(col_parts[index], index * near)
    far = far.reshape(near, local_blocks, vector_count, side)
    total = row_terms.reshape(col_devices, *own.shape).sum(0) + far[0]
    for offset in range(1, near):
        total = total + swap(far[offset], offset)
    return total.transpose(1, 0, 2).reshape(vector_count, width)


def solution(mesh):
    in_specs = (
        P("row", "col", None, None, None),
        P("row", "col", None),
        P("row", "col", None),
        P("row", "col"),
        P(None, ("row", "col")),
    )
    out_specs = P(None, ("row", "col"))
    return jax.shard_map(body, mesh=mesh, in_specs=in_specs, out_specs=out_specs, check_vma=False)
```

time: 79.4 us -> 58.8 us (0.74)
  the two profiles are of different devices: /device:TPU:1 before, /device:TPU:32 now
where the time goes in v2:
time: 58.8 us; the launch traced here: 58.2 us
  starting transfers between devices  29.4 us (50%)
  waiting for transfers between devices  18.1 us (31%)
  Pallas kernels  8.46 us (14%)
  between operations  0.8 us (1%)
  local copies, waits for them, and re-layouts  0.73 us (1%)
  other arithmetic  0.67 us (1%)
    ppermute x12, starting transfers between devices, swap(): lax.ppermute(value, 'row', [(j, j ^ offset) for j in range(row_devices)])  13.2 us
    all_to_all x1, starting transfers between devices, body(): row_input = lax.all_to_all(copies, 'col', 0, 0, tiled=True)  10.2 us
    all_to_all x1, waiting for transfers between devices, body(): row_terms = lax.all_to_all(row_part, 'col', 0, 0, tiled=True)  10.1 us
    pallas_call x1, Pallas kernels, multiply(): pl.pallas_call(functools.partial(tile_kernel, len(col_inputs), len(col_in...  7.01 us
    all_to_all x1, starting transfers between devices, body(): row_terms = lax.all_to_all(row_part, 'col', 0, 0, tiled=True)  6.07 us
    ppermute x12, waiting for transfers between devices, swap(): lax.ppermute(value, 'row', [(j, j ^ offset) for j in range(row_devices)])  4.44 us
    all_to_all x1, waiting for transfers between devices, body(): row_input = lax.all_to_all(copies, 'col', 0, 0, tiled=True)  3.56 us
    pallas_call x1, Pallas kernels, spread(): pl.pallas_call(spread_kernel, out_shape=[jax.ShapeDtypeStruct((devices *...  1.44 us
  transfers between devices with their start and end apart: 14, of which 4 were waited for; matrix products, arithmetic and copies ran while one was open for 0% of the time, Pallas kernels for 2%

profile of v2, /device:TPU:32, one launch (start us, length us, event | category | flops | bytes accessed | tf_op | source)
XLA Modules:
  0.0 58.2 jit_solution(39242321000084805)
XLA Ops:
  0.0 0.0 collective-permute-start.2
  0.0 1.9 %collective-permute-start.1 = (f32[4,8,128]{2,1,0:T(8,128)}, f32[4,8,128]{2,1,0:T(8,128)S(1)}, u32[]{:S(2)}, u32[]{:S(2)}) collective-permute-start(f32[4,8,128]{2,1,0:T(8,128)} %bitcast.33), channel_id=1, source_target_pairs={{0,32},{16,48},{32,0},{48,16},{64,96},{80,112},{96,64},{112,80},{1... | collective-permute-start | bytes 49160 | tf_op jit(solution)/shard_map/ppermute | solution.py:170
  1.9 0.1 collective-permute-start
  2.0 1.4 %shard_map.55 = (f32[64,8,128]{2,1,0:T(8,128)}, f32[4,8,128]{2,1,0:T(8,128)}) custom-call(f32[4,8,128]{2,1,0:T(8,128)} %bitcast.35), custom_call_target="tpu_custom_call" | custom-call | tf_op jit(solution)/shard_map/pallas_call | solution.py:127
  3.4 10.2 %all-to-all-start = ((f32[64,8,128]{2,1,0:T(8,128)}), f32[64,8,128]{2,1,0:T(8,128)S(1)}, u32[]{:S(2)}, u32[]{:S(2)}) async-start(f32[64,8,128]{2,1,0:T(8,128)} %get-tuple-element.12), calls=%async_computation | async-start | bytes 524288 | tf_op jit(solution)/shard_map/all_to_all | solution.py:181
  14.3 0.0 collective-permute-done.2.refs_3_
  14.3 0.0 collective-permute-done.1.refs_2_
  14.3 0.0 collective-permute-done.refs_1_
  14.3 0.0 copy-start
  14.3 0.7 %copy-done = f32[4,8,128]{2,1,0:T(8,128)S(1)} copy-done((f32[4,8,128]{2,1,0:T(8,128)S(1)}, f32[4,8,128]{2,1,0:T(8,128)}, u32[]{:S(2)}) %copy-start) | copy-done | bytes 16408
  15.0 0.0 copy-start.1
  15.0 0.0 copy-start.2
  15.1 2.8 %collective-permute-start.5 = (f32[16,8,128]{2,1,0:T(8,128)S(1)}, f32[16,8,128]{2,1,0:T(8,128)S(1)}, u32[]{:S(2)}, u32[]{:S(2)}) collective-permute-start(f32[16,8,128]{2,1,0:T(8,128)S(1)} %shard_map.56.refs_3_), channel_id=1, source_target_pairs={{0,192},{16,208},{32,224},{48,240},{64,128},{80,144},{96,160},{112... | collective-permute-start | bytes 196616 | tf_op jit(solution)/shard_map/ppermute | solution.py:170
  17.9 0.8 %collective-permute-start.4 = (f32[16,8,128]{2,1,0:T(8,128)S(1)}, f32[16,8,128]{2,1,0:T(8,128)S(1)}, u32[]{:S(2)}, u32[]{:S(2)}) collective-permute-start(f32[16,8,128]{2,1,0:T(8,128)S(1)} %shard_map.56.refs_3_), channel_id=1, source_target_pairs={{0,128},{16,144},{32,160},{48,176},{64,192},{80,208},{96,224},{112... | collective-permute-start | bytes 196616 | tf_op jit(solution)/shard_map/ppermute | solution.py:170
  18.7 0.5 collective-permute-start.3
  19.2 0.0 copy-done.1
  19.2 0.0 copy-done.2
  19.3 1.4 %collective-permute-done.5.refs_6_ = f32[16,8,128]{2,1,0:T(8,128)S(1)} collective-permute-done((f32[16,8,128]{2,1,0:T(8,128)S(1)}, f32[16,8,128]{2,1,0:T(8,128)S(1)}, u32[]{:S(2)}, u32[]{:S(2)}) %collective-permute-start.5) | collective-permute-done | bytes 65568 | tf_op jit(solution)/shard_map/ppermute | solution.py:170
  20.6 3.1 %collective-permute-done.4.refs_5_ = f32[16,8,128]{2,1,0:T(8,128)S(1)} collective-permute-done((f32[16,8,128]{2,1,0:T(8,128)S(1)}, f32[16,8,128]{2,1,0:T(8,128)S(1)}, u32[]{:S(2)}, u32[]{:S(2)}) %collective-permute-start.4) | collective-permute-done | bytes 65568 | tf_op jit(solution)/shard_map/ppermute | solution.py:170
  23.7 0.0 collective-permute-done.3.refs_4_
  23.7 3.6 %all-to-all-done.refs_2_ = f32[64,8,128]{2,1,0:T(8,128)S(1)} async-done(((f32[64,8,128]{2,1,0:T(8,128)}), f32[64,8,128]{2,1,0:T(8,128)S(1)}, u32[]{:S(2)}, u32[]{:S(2)}) %all-to-all-start) | async-done | bytes 262176 | tf_op jit(solution)/shard_map/all_to_all | solution.py:181
  27.2 7.0 %shard_map.57 = (f32[64,8,128]{2,1,0:T(8,128)}, f32[16,8,128]{2,1,0:T(8,128)S(1)}, f32[16,8,128]{2,1,0:T(8,128)S(1)}, f32[16,8,128]{2,1,0:T(8,128)S(1)}, f32[16,8,128]{2,1,0:T(8,128)S(1)}) custom-call(s32[128]{0:T(128)S(1)} %compare_select_fusion.refs_0_, f32[128,128,128]{2,1,0:T(8,128)} %bitcast.30, f32[64,8,128]{2,1,0:T(8,128)S(1)} %all-to-all-done.refs_2_, ...), custom_call_target="tpu_custom_call" | custom-call | flops 268435456 | bytes 8388608 | tf_op jit(solution)/shard_map/pallas_call | solution.py:97
  34.3 1.6 %collective-permute-start.6 = (f32[16,8,128]{2,1,0:T(8,128)S(1)}, f32[16,8,128]{2,1,0:T(8,128)S(1)}, u32[]{:S(2)}, u32[]{:S(2)}) collective-permute-start(f32[16,8,128]{2,1,0:T(8,128)S(1)} %get-tuple-element.16), channel_id=1, source_target_pairs={{0,64},{16,80},{32,96},{48,112},{64,0},{80,16},{96,32},{112,48},{1... | collective-permute-start | bytes 196616 | tf_op jit(solution)/shard_map/ppermute | solution.py:170
  35.8 2.7 %collective-permute-start.7 = (f32[16,8,128]{2,1,0:T(8,128)S(1)}, f32[16,8,128]{2,1,0:T(8,128)S(1)}, u32[]{:S(2)}, u32[]{:S(2)}) collective-permute-start(f32[16,8,128]{2,1,0:T(8,128)S(1)} %get-tuple-element.17), channel_id=1, source_target_pairs={{0,128},{16,144},{32,160},{48,176},{64,192},{80,208},{96,224},{112... | collective-permute-start | bytes 196616 | tf_op jit(solution)/shard_map/ppermute | solution.py:170
  38.5 0.5 collective-permute-start.8
  39.0 6.1 %all-to-all-start.1 = ((f32[64,8,128]{2,1,0:T(8,128)}), f32[64,8,128]{2,1,0:T(8,128)S(1)}, u32[]{:S(2)}, u32[]{:S(2)}) async-start(f32[64,8,128]{2,1,0:T(8,128)} %get-tuple-element.14), calls=%async_computation.1 | async-start | bytes 524288 | tf_op jit(solution)/shard_map/all_to_all | solution.py:185
  45.1 0.0 collective-permute-done.6
  45.1 0.0 collective-permute-done.7
  45.1 0.0 collective-permute-done.8
  45.2 0.1 collective-permute-start.9
  45.3 1.1 %collective-permute-start.11 = (f32[4,8,128]{2,1,0:T(8,128)S(1)}, f32[4,8,128]{2,1,0:T(8,128)S(1)}, u32[]{:S(2)}, u32[]{:S(2)}) collective-permute-start(f32[4,8,128]{2,1,0:T(8,128)S(1)} %get-tuple-element.20), channel_id=1, source_target_pairs={{0,48},{16,32},{32,16},{48,0},{64,112},{80,96},{96,80},{112,64},{1... | collective-permute-start | bytes 49160 | tf_op jit(solution)/shard_map/ppermute | solution.py:170
  46.4 1.0 %collective-permute-start.10 = (f32[4,8,128]{2,1,0:T(8,128)S(1)}, f32[4,8,128]{2,1,0:T(8,128)S(1)}, u32[]{:S(2)}, u32[]{:S(2)}) collective-permute-start(f32[4,8,128]{2,1,0:T(8,128)S(1)} %get-tuple-element.21), channel_id=1, source_target_pairs={{0,32},{16,48},{32,0},{48,16},{64,96},{80,112},{96,64},{112,80},{1... | collective-permute-start | bytes 49160 | tf_op jit(solution)/shard_map/ppermute | solution.py:170
  47.4 10.1 %all-to-all-done.1 = f32[64,8,128]{2,1,0:T(8,128)S(1)} async-done(((f32[64,8,128]{2,1,0:T(8,128)}), f32[64,8,128]{2,1,0:T(8,128)S(1)}, u32[]{:S(2)}, u32[]{:S(2)}) %all-to-all-start.1) | async-done | bytes 262176 | tf_op jit(solution)/shard_map/all_to_all | solution.py:185
  57.5 0.0 collective-permute-done.9
  57.6 0.0 collective-permute-done.11
  57.6 0.0 collective-permute-done.10
  57.6 0.6 %fusion.3 = f32[8,512]{1,0:T(8,128)} fusion(f32[4,8,128]{2,1,0:T(8,128)S(1)} %collective-permute-done.11, f32[4,8,128]{2,1,0:T(8,128)S(1)} %collective-permute-done.10, f32[4,8,128]{2,1,0:T(8,128)S(1)} %collective-permute-done.9, f32[4,8,128]{2,1,0:T(8,128)S(1)} %reduce_sum.9, f32[16,8,128]{2,1,0:T(8,128)S(1)} %add_add_fusion), kind=kLoop, calls=%fused_computation.5 | loop fusion | flops 16384 | bytes 98304 | tf_op jit(solution)/shard_map/reshape | solution.py:193
  (5 shorter events, 0.1 us)
Async XLA Ops:
  0.0 14.3 %collective-permute-start.2 = (f32[4,8,128]{2,1,0:T(8,128)}, f32[4,8,128]{2,1,0:T(8,128)S(1)}, u32[]{:S(2)}, u32[]{:S(2)}) collective-permute-start(f32[4,8,128]{2,1,0:T(8,128)} %bitcast.32), channel_id=1, source_target_pairs={{0,48},{16,32},{32,16},{48,0},{64,112},{80,96},{96,80},{112,64},{1... | collective-permute-start | bytes 49160 | tf_op jit(solution)/shard_map/ppermute | solution.py:170
  0.0 14.3 %collective-permute-start.1 = (f32[4,8,128]{2,1,0:T(8,128)}, f32[4,8,128]{2,1,0:T(8,128)S(1)}, u32[]{:S(2)}, u32[]{:S(2)}) collective-permute-start(f32[4,8,128]{2,1,0:T(8,128)} %bitcast.33), channel_id=1, source_target_pairs={{0,32},{16,48},{32,0},{48,16},{64,96},{80,112},{96,64},{112,80},{1... | collective-permute-start | bytes 49160 | tf_op jit(solution)/shard_map/ppermute | solution.py:170
  1.9 12.4 %collective-permute-start = (f32[4,8,128]{2,1,0:T(8,128)}, f32[4,8,128]{2,1,0:T(8,128)S(1)}, u32[]{:S(2)}, u32[]{:S(2)}) collective-permute-start(f32[4,8,128]{2,1,0:T(8,128)} %bitcast.34), channel_id=1, source_target_pairs={{0,16},{16,0},{32,48},{48,32},{64,80},{80,64},{96,112},{112,96},{1... | collective-permute-start | bytes 49160 | tf_op jit(solution)/shard_map/ppermute | solution.py:170
  3.4 23.8 %all-to-all-start = ((f32[64,8,128]{2,1,0:T(8,128)}), f32[64,8,128]{2,1,0:T(8,128)S(1)}, u32[]{:S(2)}, u32[]{:S(2)}) async-start(f32[64,8,128]{2,1,0:T(8,128)} %get-tuple-element.12), calls=%async_computation | async-start | bytes 524288 | tf_op jit(solution)/shard_map/all_to_all | solution.py:181
  14.3 0.7 %copy-start = (f32[4,8,128]{2,1,0:T(8,128)S(1)}, f32[4,8,128]{2,1,0:T(8,128)}, u32[]{:S(2)}) copy-start(f32[4,8,128]{2,1,0:T(8,128)} %get-tuple-element.13.refs_0_) | copy-start | bytes 49156
  15.0 4.2 %copy-start.1 = (s32[1,1,128]{2,1,0:T(1,128)S(1)}, s32[1,1,128]{2,1,0:T(1,128)}, u32[]{:S(2)}) copy-start(s32[1,1,128]{2,1,0:T(1,128)} %param.7) | copy-start | bytes 1540
  15.0 4.2 %copy-start.2 = (s32[1,1,128]{2,1,0:T(1,128)S(1)}, s32[1,1,128]{2,1,0:T(1,128)}, u32[]{:S(2)}) copy-start(s32[1,1,128]{2,1,0:T(1,128)} %param.6) | copy-start | bytes 1540
  15.1 5.6 %collective-permute-start.5 = (f32[16,8,128]{2,1,0:T(8,128)S(1)}, f32[16,8,128]{2,1,0:T(8,128)S(1)}, u32[]{:S(2)}, u32[]{:S(2)}) collective-permute-start(f32[16,8,128]{2,1,0:T(8,128)S(1)} %shard_map.56.refs_3_), channel_id=1, source_target_pairs={{0,192},{16,208},{32,224},{48,240},{64,128},{80,144},{96,160},{112... | collective-permute-start | bytes 196616 | tf_op jit(solution)/shard_map/ppermute | solution.py:170
  17.9 5.8 %collective-permute-start.4 = (f32[16,8,128]{2,1,0:T(8,128)S(1)}, f32[16,8,128]{2,1,0:T(8,128)S(1)}, u32[]{:S(2)}, u32[]{:S(2)}) collective-permute-start(f32[16,8,128]{2,1,0:T(8,128)S(1)} %shard_map.56.refs_3_), channel_id=1, source_target_pairs={{0,128},{16,144},{32,160},{48,176},{64,192},{80,208},{96,224},{112... | collective-permute-start | bytes 196616 | tf_op jit(solution)/shard_map/ppermute | solution.py:170
  18.7 5.0 %collective-permute-start.3 = (f32[16,8,128]{2,1,0:T(8,128)S(1)}, f32[16,8,128]{2,1,0:T(8,128)S(1)}, u32[]{:S(2)}, u32[]{:S(2)}) collective-permute-start(f32[16,8,128]{2,1,0:T(8,128)S(1)} %shard_map.56.refs_3_), channel_id=1, source_target_pairs={{0,64},{16,80},{32,96},{48,112},{64,0},{80,16},{96,32},{112,48},{1... | collective-permute-start | bytes 196616 | tf_op jit(solution)/shard_map/ppermute | solution.py:170
  34.3 10.9 %collective-permute-start.6 = (f32[16,8,128]{2,1,0:T(8,128)S(1)}, f32[16,8,128]{2,1,0:T(8,128)S(1)}, u32[]{:S(2)}, u32[]{:S(2)}) collective-permute-start(f32[16,8,128]{2,1,0:T(8,128)S(1)} %get-tuple-element.16), channel_id=1, source_target_pairs={{0,64},{16,80},{32,96},{48,112},{64,0},{80,16},{96,32},{112,48},{1... | collective-permute-start | bytes 196616 | tf_op jit(solution)/shard_map/ppermute | solution.py:170
  35.8 9.3 %collective-permute-start.7 = (f32[16,8,128]{2,1,0:T(8,128)S(1)}, f32[16,8,128]{2,1,0:T(8,128)S(1)}, u32[]{:S(2)}, u32[]{:S(2)}) collective-permute-start(f32[16,8,128]{2,1,0:T(8,128)S(1)} %get-tuple-element.17), channel_id=1, source_target_pairs={{0,128},{16,144},{32,160},{48,176},{64,192},{80,208},{96,224},{112... | collective-permute-start | bytes 196616 | tf_op jit(solution)/shard_map/ppermute | solution.py:170
  38.5 6.6 %collective-permute-start.8 = (f32[16,8,128]{2,1,0:T(8,128)S(1)}, f32[16,8,128]{2,1,0:T(8,128)S(1)}, u32[]{:S(2)}, u32[]{:S(2)}) collective-permute-start(f32[16,8,128]{2,1,0:T(8,128)S(1)} %get-tuple-element.18), channel_id=1, source_target_pairs={{0,192},{16,208},{32,224},{48,240},{64,128},{80,144},{96,160},{112... | collective-permute-start | bytes 196616 | tf_op jit(solution)/shard_map/ppermute | solution.py:170
  39.0 18.5 %all-to-all-start.1 = ((f32[64,8,128]{2,1,0:T(8,128)}), f32[64,8,128]{2,1,0:T(8,128)S(1)}, u32[]{:S(2)}, u32[]{:S(2)}) async-start(f32[64,8,128]{2,1,0:T(8,128)} %get-tuple-element.14), calls=%async_computation.1 | async-start | bytes 524288 | tf_op jit(solution)/shard_map/all_to_all | solution.py:185
  45.2 12.4 %collective-permute-start.9 = (f32[4,8,128]{2,1,0:T(8,128)S(1)}, f32[4,8,128]{2,1,0:T(8,128)S(1)}, u32[]{:S(2)}, u32[]{:S(2)}) collective-permute-start(f32[4,8,128]{2,1,0:T(8,128)S(1)} %get-tuple-element.19), channel_id=1, source_target_pairs={{0,16},{16,0},{32,48},{48,32},{64,80},{80,64},{96,112},{112,96},{1... | collective-permute-start | bytes 49160 | tf_op jit(solution)/shard_map/ppermute | solution.py:170
  45.3 12.3 %collective-permute-start.11 = (f32[4,8,128]{2,1,0:T(8,128)S(1)}, f32[4,8,128]{2,1,0:T(8,128)S(1)}, u32[]{:S(2)}, u32[]{:S(2)}) collective-permute-start(f32[4,8,128]{2,1,0:T(8,128)S(1)} %get-tuple-element.20), channel_id=1, source_target_pairs={{0,48},{16,32},{32,16},{48,0},{64,112},{80,96},{96,80},{112,64},{1... | collective-permute-start | bytes 49160 | tf_op jit(solution)/shard_map/ppermute | solution.py:170
  46.4 11.1 %collective-permute-start.10 = (f32[4,8,128]{2,1,0:T(8,128)S(1)}, f32[4,8,128]{2,1,0:T(8,128)S(1)}, u32[]{:S(2)}, u32[]{:S(2)}) collective-permute-start(f32[4,8,128]{2,1,0:T(8,128)S(1)} %get-tuple-element.21), channel_id=1, source_target_pairs={{0,32},{16,48},{32,0},{48,16},{64,96},{80,112},{96,64},{112,80},{1... | collective-permute-start | bytes 49160 | tf_op jit(solution)/shard_map/ppermute | solution.py:170

commit v3 on v2

v3 whole, which is shorter than its diff:
```python
import functools

import jax
import jax.numpy as jnp
from jax import lax
from jax.experimental import pallas as pl
from jax.experimental.pallas import tpu as pltpu
from jax.sharding import PartitionSpec as P

CHUNK = 32
AHEAD = 2
SLIM = 62
TLIM = 48
JOIN = 5 * 10 ** 10
ORDER = (2, 3, 1)
FLOPS = 4 * 16 * 256 * 128 * 128
SMEM = pl.BlockSpec(memory_space=pltpu.SMEM)
VMEM = pl.BlockSpec(memory_space=pltpu.VMEM)
ANY = pl.BlockSpec(memory_space=pl.ANY)


def split(value):
    high = value.astype(jnp.bfloat16)
    low = (value - high.astype(jnp.float32)).astype(jnp.bfloat16)
    return high, low


def take(refs, count):
    taken = refs[:count]
    del refs[:count]
    return taken


def tile_kernel(row_pieces, col_pieces, *refs):
    refs = list(refs)
    places, tiles = take(refs, 2)
    row_sources, col_sources = take(refs, row_pieces), take(refs, col_pieces)
    row_parts, col_parts = take(refs, row_pieces), take(refs, col_pieces)
    held, row_split, col_split, row_sum, col_sum, arrived = refs
    slots = held.shape[0]
    chunks = slots // CHUNK
    vectors = row_sum.shape[1]

    def fetch(chunk):
        place = pl.ds(chunk * CHUNK, CHUNK)
        return pltpu.make_async_copy(tiles.at[place], held.at[place], arrived.at[chunk])

    for chunk in range(AHEAD):
        fetch(chunk).start()
    for sources, parts in ((row_sources, row_split), (col_sources, col_split)):
        start = 0
        for source in sources:
            high, low = split(source[...])
            parts[start:start + source.shape[0]] = jnp.concatenate([high, low], axis=1)
            start += source.shape[0]
        parts[start] = jnp.zeros_like(parts[start])
    row_sum[...] = jnp.zeros_like(row_sum)
    col_sum[...] = jnp.zeros_like(col_sum)

    def step(chunk, carry):
        fetch(chunk).wait()

        @pl.when(chunk + AHEAD < chunks)
        def _():
            fetch(chunk + AHEAD).start()

        results = []
        for offset in range(CHUNK):
            slot = chunk * CHUNK + offset
            place = places[slot]
            row, col = place // 128, place % 128
            high, low = split(held[slot])
            from_cols = col_split[col]
            from_rows = row_split[row]
            first = lax.dot_general(
                jnp.concatenate([from_cols, from_cols], axis=1),
                jnp.concatenate([high, low], axis=1),
                (((1,), (1,)), ((), ())), preferred_element_type=jnp.float32,
            )
            second = lax.dot_general(
                jnp.concatenate([from_rows, from_rows], axis=1),
                jnp.concatenate([high, low], axis=0),
                (((1,), (0,)), ((), ())), preferred_element_type=jnp.float32,
            )
            results.append((row, col, first[:vectors] + first[vectors:], second[:vectors] + second[vectors:]))
        for row, col, first, second in results:
            row_sum[row] += first
            col_sum[col] += second
        return carry

    lax.fori_loop(0, chunks, step, 0)
    for parts, total in ((row_parts, row_sum), (col_parts, col_sum)):
        start = 0
        for part in parts:
            part[...] = total[start:start + part.shape[0]]
            start += part.shape[0]


def multiply(places, tiles, row_inputs, col_inputs):
    slots, side, _ = tiles.shape
    pieces = len(row_inputs), len(col_inputs)
    blocks = sum(part.shape[0] for part in row_inputs)
    vectors = row_inputs[0].shape[1]
    parts = [jax.ShapeDtypeStruct(part.shape, jnp.float32) for part in [*row_inputs, *col_inputs]]
    results = pl.pallas_call(
        functools.partial(tile_kernel, *pieces),
        out_shape=parts,
        in_specs=[SMEM, ANY] + [VMEM] * len(parts),
        out_specs=[VMEM] * len(parts),
        scratch_shapes=[
            pltpu.VMEM(tiles.shape, jnp.float32),
            pltpu.VMEM((blocks + 8, 2 * vectors, side), jnp.bfloat16),
            pltpu.VMEM((blocks + 8, 2 * vectors, side), jnp.bfloat16),
            pltpu.VMEM((blocks + 8, vectors, side), jnp.float32),
            pltpu.VMEM((blocks + 8, vectors, side), jnp.float32),
            pltpu.SemaphoreType.DMA((slots // CHUNK,)),
        ],
        compiler_params=pltpu.CompilerParams(vmem_limit_bytes=TLIM * 1024 * 1024),
        cost_estimate=pl.CostEstimate(flops=FLOPS, bytes_accessed=4 * slots * side * side, transcendentals=0),
    )(places, tiles, *row_inputs, *col_inputs)
    return results[:pieces[0]], results[pieces[0]:]


def join_kernel(*refs):
    out = refs[-1]
    start = 0
    for part in refs[:-1]:
        out[start:start + part.shape[0]] = part[...]
        start += part.shape[0]


def join(parts):
    size = sum(part.shape[0] for part in parts)
    return pl.pallas_call(
        join_kernel,
        out_shape=jax.ShapeDtypeStruct((size, *parts[0].shape[1:]), parts[0].dtype),
        in_specs=[VMEM] * len(parts),
        out_specs=VMEM,
        compiler_params=pltpu.CompilerParams(vmem_limit_bytes=4 * 1024 * 1024),
        cost_estimate=pl.CostEstimate(flops=JOIN, bytes_accessed=1024, transcendentals=0),
    )(*parts)


def fold_kernel(count, *refs):
    total = refs[0][...]
    for part in refs[1:count]:
        total = total + part[...]
    start = 0
    for out in refs[count:]:
        out[...] = total[start:start + out.shape[0]]
        start += out.shape[0]


def fold(parts, pieces):
    size, *rest = parts[0].shape
    out = jax.ShapeDtypeStruct((size // pieces, *rest), parts[0].dtype)
    return pl.pallas_call(
        functools.partial(fold_kernel, len(parts)),
        out_shape=[out] * pieces,
        in_specs=[VMEM] * len(parts),
        out_specs=[VMEM] * pieces,
        compiler_params=pltpu.CompilerParams(vmem_limit_bytes=4 * 1024 * 1024),
        cost_estimate=pl.CostEstimate(flops=JOIN, bytes_accessed=1024, transcendentals=0),
    )(*parts)


def body(tiles, tile_rows, tile_cols, tile_counts, vectors):
    vector_count, width = vectors.shape
    slots, side = tiles.shape[2:4]
    local_blocks = width // side
    row_devices = lax.axis_size("row")
    col_devices = lax.axis_size("col")
    own = vectors.reshape(vector_count, local_blocks, side).transpose(1, 0, 2)

    def swap(value, axis, offset):
        return lax.ppermute(value, axis, [(j, j ^ offset) for j in range(lax.axis_size(axis))])

    def swaps(values, axis, step):
        sent = {index: swap(values[index], axis, index * step) for index in ORDER}
        return [sent[index] for index in sorted(sent)]

    rows, cols = tile_rows[0, 0], tile_cols[0, 0]
    row_offset = (rows // local_blocks) ^ lax.axis_index("col")
    col_offset = (cols // local_blocks) ^ lax.axis_index("row")
    col_offset = (col_offset & 1) * (row_devices // 2) + (col_offset >> 1)
    places = (row_offset * local_blocks + rows % local_blocks) * 128 + col_offset * local_blocks + cols % local_blocks
    slot = jnp.arange(slots, dtype=jnp.int32)
    places = jnp.where(slot < tile_counts[0, 0], places, col_devices * local_blocks * 128 + row_devices * local_blocks)

    pair = join([own, swap(own, "row", 2)])
    close = join([own] + swaps([own] * 4, "col", 1))
    half = join([pair] + swaps([pair] * 4, "row", 4))
    row_inputs = [close] + swaps([close] * 4, "col", 4)
    col_inputs = [half, swap(half, "row", 1)]

    row_parts, col_parts = multiply(places, tiles[0, 0], row_inputs, col_inputs)

    half = fold([col_parts[0], swap(col_parts[1], "row", 1)], 4)
    close = fold([row_parts[0]] + swaps(row_parts, "col", 4), 4)
    pair = fold([half[0]] + swaps(half, "row", 4), 2)
    terms = [close[0]] + swaps(close, "col", 1) + [pair[0], swap(pair[1], "row", 2)]
    total = functools.reduce(jnp.add, terms)
    return total.transpose(1, 0, 2).reshape(vector_count, width)


def solution(mesh):
    in_specs = (
        P("row", "col", None, None, None),
        P("row", "col", None),
        P("row", "col", None),
        P("row", "col"),
        P(None, ("row", "col")),
    )
    out_specs = P(None, ("row", "col"))
    return jax.shard_map(body, mesh=mesh, in_specs=in_specs, out_specs=out_specs, check_vma=False)
```

time: 58.8 us -> 53.2 us (0.905)
  the two profiles are of different devices: /device:TPU:32 before, /device:TPU:6 now
where the time goes in v3:
time: 53.2 us; the launch traced here: 53 us
  starting transfers between devices  35.5 us (67%)
  waiting for transfers between devices  9.17 us (17%)
  Pallas kernels  6.22 us (12%)
  between operations  0.78 us (1%)
  local copies, waits for them, and re-layouts  0.72 us (1%)
  other arithmetic  0.64 us (1%)
    ppermute x22, starting transfers between devices, swap(): lax.ppermute(value, axis, [(j, j ^ offset) for j in range(lax.axis_size(a...  35.5 us
    ppermute x22, waiting for transfers between devices, swap(): lax.ppermute(value, axis, [(j, j ^ offset) for j in range(lax.axis_size(a...  9.17 us
    pallas_call x1, Pallas kernels, multiply(): pl.pallas_call(functools.partial(tile_kernel, *pieces), out_shape=parts,...  6.16 us
  transfers between devices with their start and end apart: 22, of which 4 were waited for; matrix products, arithmetic and copies ran while one was open for 0% of the time, Pallas kernels for 0%

profile of v3, /device:TPU:6, one launch (start us, length us, event | category | flops | bytes accessed | tf_op | source)
XLA Modules:
  0.0 53.0 jit_solution(12085801585469312687)
XLA Ops:
  0.0 1.9 %collective-permute-start.6 = (f32[4,8,128]{2,1,0:T(8,128)}, f32[4,8,128]{2,1,0:T(8,128)S(1)}, u32[]{:S(2)}, u32[]{:S(2)}) collective-permute-start(f32[4,8,128]{2,1,0:T(8,128)} %bitcast.36), channel_id=1, source_target_pairs={{0,32},{16,48},{32,0},{48,16},{64,96},{80,112},{96,64},{112,80},{1... | collective-permute-start | bytes 49160 | tf_op jit(solution)/shard_map/ppermute | solution.py:176
  1.9 5.4 %collective-permute-start.2 = (f32[4,8,128]{2,1,0:T(8,128)}, f32[4,8,128]{2,1,0:T(8,128)S(1)}, u32[]{:S(2)}, u32[]{:S(2)}) collective-permute-start(f32[4,8,128]{2,1,0:T(8,128)} %bitcast.37), channel_id=1, source_target_pairs={{0,3},{1,2},{2,1},{3,0},{4,7},{5,6},{6,5},{7,4},{8,11},{9,10},{10,... | collective-permute-start | bytes 49160 | tf_op jit(solution)/shard_map/ppermute | solution.py:176
  7.3 1.4 %collective-permute-start.1 = (f32[4,8,128]{2,1,0:T(8,128)}, f32[4,8,128]{2,1,0:T(8,128)S(1)}, u32[]{:S(2)}, u32[]{:S(2)}) collective-permute-start(f32[4,8,128]{2,1,0:T(8,128)} %bitcast.38), channel_id=1, source_target_pairs={{0,2},{1,3},{2,0},{3,1},{4,6},{5,7},{6,4},{7,5},{8,10},{9,11},{10,... | collective-permute-start | bytes 49160 | tf_op jit(solution)/shard_map/ppermute | solution.py:176
  8.8 0.9 %collective-permute-start = (f32[4,8,128]{2,1,0:T(8,128)}, f32[4,8,128]{2,1,0:T(8,128)S(1)}, u32[]{:S(2)}, u32[]{:S(2)}) collective-permute-start(f32[4,8,128]{2,1,0:T(8,128)} %bitcast.39), channel_id=1, source_target_pairs={{0,1},{1,0},{2,3},{3,2},{4,5},{5,4},{6,7},{7,6},{8,9},{9,8},{10,11... | collective-permute-start | bytes 49160 | tf_op jit(solution)/shard_map/ppermute | solution.py:176
  10.3 0.0 collective-permute-done.6.refs_1_
  10.4 0.7 %copy-done = f32[8,512]{1,0:T(8,128)S(1)} copy-done((f32[8,512]{1,0:T(8,128)S(1)}, f32[8,512]{1,0:T(8,128)}, u32[]{:S(2)}) %copy-start) | copy-done | bytes 16408
  11.1 0.5 collective-permute-start.9
  11.5 2.4 %collective-permute-start.8 = (f32[8,8,128]{2,1,0:T(8,128)S(1)}, f32[8,8,128]{2,1,0:T(8,128)S(1)}, u32[]{:S(2)}, u32[]{:S(2)}) collective-permute-start(f32[8,8,128]{2,1,0:T(8,128)S(1)} %shard_map.56.refs_0_), channel_id=1, source_target_pairs={{0,128},{16,144},{32,160},{48,176},{64,192},{80,208},{96,224},{112... | collective-permute-start | bytes 98312 | tf_op jit(solution)/shard_map/ppermute | solution.py:176
  14.0 0.0 collective-permute-done.2.refs_3_
  14.0 1.2 %collective-permute-start.7 = (f32[8,8,128]{2,1,0:T(8,128)S(1)}, f32[8,8,128]{2,1,0:T(8,128)S(1)}, u32[]{:S(2)}, u32[]{:S(2)}) collective-permute-start(f32[8,8,128]{2,1,0:T(8,128)S(1)} %shard_map.56.refs_0_), channel_id=1, source_target_pairs={{0,64},{16,80},{32,96},{48,112},{64,0},{80,16},{96,32},{112,48},{1... | collective-permute-start | bytes 98312 | tf_op jit(solution)/shard_map/ppermute | solution.py:176
  15.2 0.0 collective-permute-done.1.refs_2_
  15.2 0.0 collective-permute-done.refs_1_
  15.2 0.0 copy-start.1
  15.2 0.0 copy-start.2
  15.2 3.1 %collective-permute-start.5 = (f32[16,8,128]{2,1,0:T(8,128)S(1)}, f32[16,8,128]{2,1,0:T(8,128)S(1)}, u32[]{:S(2)}, u32[]{:S(2)}) collective-permute-start(f32[16,8,128]{2,1,0:T(8,128)S(1)} %shard_map.55.refs_2_), channel_id=1, source_target_pairs={{0,12},{1,13},{2,14},{3,15},{4,8},{5,9},{6,10},{7,11},{8,4},{9,5},... | collective-permute-start | bytes 196616 | tf_op jit(solution)/shard_map/ppermute | solution.py:176
  18.3 0.6 %collective-permute-start.4 = (f32[16,8,128]{2,1,0:T(8,128)S(1)}, f32[16,8,128]{2,1,0:T(8,128)S(1)}, u32[]{:S(2)}, u32[]{:S(2)}) collective-permute-start(f32[16,8,128]{2,1,0:T(8,128)S(1)} %shard_map.55.refs_2_), channel_id=1, source_target_pairs={{0,8},{1,9},{2,10},{3,11},{4,12},{5,13},{6,14},{7,15},{8,0},{9,1},... | collective-permute-start | bytes 196616 | tf_op jit(solution)/shard_map/ppermute | solution.py:176
  18.9 0.0 collective-permute-done.9.refs_3_
  18.9 0.5 collective-permute-start.3
  19.4 0.0 collective-permute-done.8.refs_2_
  19.4 0.0 collective-permute-done.7.refs_1_
  19.4 0.1 collective-permute-start.10
  19.6 1.9 %collective-permute-done.5.refs_5_ = f32[16,8,128]{2,1,0:T(8,128)S(1)} collective-permute-done((f32[16,8,128]{2,1,0:T(8,128)S(1)}, f32[16,8,128]{2,1,0:T(8,128)S(1)}, u32[]{:S(2)}, u32[]{:S(2)}) %collective-permute-start.5) | collective-permute-done | bytes 65568 | tf_op jit(solution)/shard_map/ppermute | solution.py:176
  21.5 2.6 %collective-permute-done.4.refs_4_ = f32[16,8,128]{2,1,0:T(8,128)S(1)} collective-permute-done((f32[16,8,128]{2,1,0:T(8,128)S(1)}, f32[16,8,128]{2,1,0:T(8,128)S(1)}, u32[]{:S(2)}, u32[]{:S(2)}) %collective-permute-start.4) | collective-permute-done | bytes 65568 | tf_op jit(solution)/shard_map/ppermute | solution.py:176
  24.1 0.0 collective-permute-done.3.refs_3_
  24.1 0.0 collective-permute-done.10.refs_7_
  24.1 6.2 %shard_map.58 = (f32[16,8,128]{2,1,0:T(8,128)S(1)}, f32[16,8,128]{2,1,0:T(8,128)S(1)}, f32[16,8,128]{2,1,0:T(8,128)S(1)}, f32[16,8,128]{2,1,0:T(8,128)S(1)}, f32...) custom-call(s32[128]{0:T(128)S(1)} %compare_select_fusion.refs_0_, f32[128,128,128]{2,1,0:T(8,128)} %bitcast.42, ...), custom_call_target="tpu_custom_call" | custom-call | flops 268435456 | bytes 8388608 | tf_op jit(solution)/shard_map/pallas_call | solution.py:105
  30.3 0.1 collective-permute-start.17
  30.4 0.2 collective-permute-start.11
  30.6 2.6 %collective-permute-start.12 = (f32[16,8,128]{2,1,0:T(8,128)S(1)}, f32[16,8,128]{2,1,0:T(8,128)S(1)}, u32[]{:S(2)}, u32[]{:S(2)}) collective-permute-start(f32[16,8,128]{2,1,0:T(8,128)S(1)} %get-tuple-element.23), channel_id=1, source_target_pairs={{0,8},{1,9},{2,10},{3,11},{4,12},{5,13},{6,14},{7,15},{8,0},{9,1},... | collective-permute-start | bytes 196616 | tf_op jit(solution)/shard_map/ppermute | solution.py:176
  33.2 1.9 %collective-permute-start.13 = (f32[16,8,128]{2,1,0:T(8,128)S(1)}, f32[16,8,128]{2,1,0:T(8,128)S(1)}, u32[]{:S(2)}, u32[]{:S(2)}) collective-permute-start(f32[16,8,128]{2,1,0:T(8,128)S(1)} %get-tuple-element.24), channel_id=1, source_target_pairs={{0,12},{1,13},{2,14},{3,15},{4,8},{5,9},{6,10},{7,11},{8,4},{9,5},... | collective-permute-start | bytes 196616 | tf_op jit(solution)/shard_map/ppermute | solution.py:176
  35.1 0.0 collective-permute-done.17.refs_1_
  35.2 0.9 %collective-permute-start.18 = (f32[8,8,128]{2,1,0:T(8,128)S(1)}, f32[8,8,128]{2,1,0:T(8,128)S(1)}, u32[]{:S(2)}, u32[]{:S(2)}) collective-permute-start(f32[8,8,128]{2,1,0:T(8,128)S(1)} %get-tuple-element.32), channel_id=1, source_target_pairs={{0,64},{16,80},{32,96},{48,112},{64,0},{80,16},{96,32},{112,48},{1... | collective-permute-start | bytes 98312 | tf_op jit(solution)/shard_map/ppermute | solution.py:176
  36.1 1.1 %collective-permute-start.19 = (f32[8,8,128]{2,1,0:T(8,128)S(1)}, f32[8,8,128]{2,1,0:T(8,128)S(1)}, u32[]{:S(2)}, u32[]{:S(2)}) collective-permute-start(f32[8,8,128]{2,1,0:T(8,128)S(1)} %get-tuple-element.33), channel_id=1, source_target_pairs={{0,128},{16,144},{32,160},{48,176},{64,192},{80,208},{96,224},{112... | collective-permute-start | bytes 98312 | tf_op jit(solution)/shard_map/ppermute | solution.py:176
  37.2 0.0 collective-permute-done.11.refs_1_
  37.2 2.7 %collective-permute-start.20 = (f32[8,8,128]{2,1,0:T(8,128)S(1)}, f32[8,8,128]{2,1,0:T(8,128)S(1)}, u32[]{:S(2)}, u32[]{:S(2)}) collective-permute-start(f32[8,8,128]{2,1,0:T(8,128)S(1)} %get-tuple-element.34), channel_id=1, source_target_pairs={{0,192},{16,208},{32,224},{48,240},{64,128},{80,144},{96,160},{112... | collective-permute-start | bytes 98312 | tf_op jit(solution)/shard_map/ppermute | solution.py:176
  40.0 0.0 collective-permute-done.12.refs_2_
  40.0 0.0 collective-permute-done.13.refs_3_
  40.0 2.1 %collective-permute-start.14 = (f32[4,8,128]{2,1,0:T(8,128)S(1)}, f32[4,8,128]{2,1,0:T(8,128)S(1)}, u32[]{:S(2)}, u32[]{:S(2)}) collective-permute-start(f32[4,8,128]{2,1,0:T(8,128)S(1)} %get-tuple-element.26), channel_id=1, source_target_pairs={{0,1},{1,0},{2,3},{3,2},{4,5},{5,4},{6,7},{7,6},{8,9},{9,8},{10,11... | collective-permute-start | bytes 49160 | tf_op jit(solution)/shard_map/ppermute | solution.py:176
  42.1 4.5 %collective-permute-start.15 = (f32[4,8,128]{2,1,0:T(8,128)S(1)}, f32[4,8,128]{2,1,0:T(8,128)S(1)}, u32[]{:S(2)}, u32[]{:S(2)}) collective-permute-start(f32[4,8,128]{2,1,0:T(8,128)S(1)} %get-tuple-element.27), channel_id=1, source_target_pairs={{0,2},{1,3},{2,0},{3,1},{4,6},{5,7},{6,4},{7,5},{8,10},{9,11},{10,... | collective-permute-start | bytes 49160 | tf_op jit(solution)/shard_map/ppermute | solution.py:176
  46.6 0.0 collective-permute-done.18.refs_1_
  46.6 0.0 collective-permute-start.16
  46.6 0.0 collective-permute-done.19.refs_2_
  46.6 1.2 %collective-permute-start.21 = (f32[4,8,128]{2,1,0:T(8,128)S(1)}, f32[4,8,128]{2,1,0:T(8,128)S(1)}, u32[]{:S(2)}, u32[]{:S(2)}) collective-permute-start(f32[4,8,128]{2,1,0:T(8,128)S(1)} %get-tuple-element.36), channel_id=1, source_target_pairs={{0,32},{16,48},{32,0},{48,16},{64,96},{80,112},{96,64},{112,80},{1... | collective-permute-start | bytes 49160 | tf_op jit(solution)/shard_map/ppermute | solution.py:176
  47.8 0.0 collective-permute-done.14
  47.8 2.1 %collective-permute-done.15 = f32[4,8,128]{2,1,0:T(8,128)S(1)} collective-permute-done((f32[4,8,128]{2,1,0:T(8,128)S(1)}, f32[4,8,128]{2,1,0:T(8,128)S(1)}, u32[]{:S(2)}, u32[]{:S(2)}) %collective-permute-start.15) | collective-permute-done | bytes 16416 | tf_op jit(solution)/shard_map/ppermute | solution.py:176
  49.9 2.5 %collective-permute-done.16 = f32[4,8,128]{2,1,0:T(8,128)S(1)} collective-permute-done((f32[4,8,128]{2,1,0:T(8,128)S(1)}, f32[4,8,128]{2,1,0:T(8,128)S(1)}, u32[]{:S(2)}, u32[]{:S(2)}) %collective-permute-start.16) | collective-permute-done | bytes 16416 | tf_op jit(solution)/shard_map/ppermute | solution.py:176
  52.4 0.0 collective-permute-done.21
  52.4 0.6 %add_bitcast_fusion = f32[8,512]{1,0:T(8,128)} fusion(f32[4,8,128]{2,1,0:T(8,128)S(1)} %collective-permute-done.21, f32[4,8,128]{2,1,0:T(8,128)S(1)} %get-tuple-element.35, f32[4,8,128]{2,1,0:T(8,128)S(1)} %collective-permute-done.16, f32[4,8,128]{2,1,0:T(8,128)S(1)} %collective-permute-done.15, f32[4,8,128]{2,1,0:T(8,128)S(1)} %get-tuple-element.25, ...), kind=kLoop, calls=%fused_computation | loop fusion | flops 20480 | bytes 114688 | tf_op jit(solution)/shard_map/reshape | solution.py:203
  (11 shorter events, 0.1 us)
Async XLA Ops:
  0.0 10.3 %collective-permute-start.6 = (f32[4,8,128]{2,1,0:T(8,128)}, f32[4,8,128]{2,1,0:T(8,128)S(1)}, u32[]{:S(2)}, u32[]{:S(2)}) collective-permute-start(f32[4,8,128]{2,1,0:T(8,128)} %bitcast.36), channel_id=1, source_target_pairs={{0,32},{16,48},{32,0},{48,16},{64,96},{80,112},{96,64},{112,80},{1... | collective-permute-start | bytes 49160 | tf_op jit(solution)/shard_map/ppermute | solution.py:176
  1.9 12.1 %collective-permute-start.2 = (f32[4,8,128]{2,1,0:T(8,128)}, f32[4,8,128]{2,1,0:T(8,128)S(1)}, u32[]{:S(2)}, u32[]{:S(2)}) collective-permute-start(f32[4,8,128]{2,1,0:T(8,128)} %bitcast.37), channel_id=1, source_target_pairs={{0,3},{1,2},{2,1},{3,0},{4,7},{5,6},{6,5},{7,4},{8,11},{9,10},{10,... | collective-permute-start | bytes 49160 | tf_op jit(solution)/shard_map/ppermute | solution.py:176
  7.3 7.9 %collective-permute-start.1 = (f32[4,8,128]{2,1,0:T(8,128)}, f32[4,8,128]{2,1,0:T(8,128)S(1)}, u32[]{:S(2)}, u32[]{:S(2)}) collective-permute-start(f32[4,8,128]{2,1,0:T(8,128)} %bitcast.38), channel_id=1, source_target_pairs={{0,2},{1,3},{2,0},{3,1},{4,6},{5,7},{6,4},{7,5},{8,10},{9,11},{10,... | collective-permute-start | bytes 49160 | tf_op jit(solution)/shard_map/ppermute | solution.py:176
  8.8 6.4 %collective-permute-start = (f32[4,8,128]{2,1,0:T(8,128)}, f32[4,8,128]{2,1,0:T(8,128)S(1)}, u32[]{:S(2)}, u32[]{:S(2)}) collective-permute-start(f32[4,8,128]{2,1,0:T(8,128)} %bitcast.39), channel_id=1, source_target_pairs={{0,1},{1,0},{2,3},{3,2},{4,5},{5,4},{6,7},{7,6},{8,9},{9,8},{10,11... | collective-permute-start | bytes 49160 | tf_op jit(solution)/shard_map/ppermute | solution.py:176
  10.3 0.7 %copy-start = (f32[8,512]{1,0:T(8,128)S(1)}, f32[8,512]{1,0:T(8,128)}, u32[]{:S(2)}) copy-start(f32[8,512]{1,0:T(8,128)} %param.9) | copy-start | bytes 49156
  11.1 7.9 %collective-permute-start.9 = (f32[8,8,128]{2,1,0:T(8,128)S(1)}, f32[8,8,128]{2,1,0:T(8,128)S(1)}, u32[]{:S(2)}, u32[]{:S(2)}) collective-permute-start(f32[8,8,128]{2,1,0:T(8,128)S(1)} %shard_map.56.refs_0_), channel_id=1, source_target_pairs={{0,192},{16,208},{32,224},{48,240},{64,128},{80,144},{96,160},{112... | collective-permute-start | bytes 98312 | tf_op jit(solution)/shard_map/ppermute | solution.py:176
  11.5 7.9 %collective-permute-start.8 = (f32[8,8,128]{2,1,0:T(8,128)S(1)}, f32[8,8,128]{2,1,0:T(8,128)S(1)}, u32[]{:S(2)}, u32[]{:S(2)}) collective-permute-start(f32[8,8,128]{2,1,0:T(8,128)S(1)} %shard_map.56.refs_0_), channel_id=1, source_target_pairs={{0,128},{16,144},{32,160},{48,176},{64,192},{80,208},{96,224},{112... | collective-permute-start | bytes 98312 | tf_op jit(solution)/shard_map/ppermute | solution.py:176
  14.0 5.4 %collective-permute-start.7 = (f32[8,8,128]{2,1,0:T(8,128)S(1)}, f32[8,8,128]{2,1,0:T(8,128)S(1)}, u32[]{:S(2)}, u32[]{:S(2)}) collective-permute-start(f32[8,8,128]{2,1,0:T(8,128)S(1)} %shard_map.56.refs_0_), channel_id=1, source_target_pairs={{0,64},{16,80},{32,96},{48,112},{64,0},{80,16},{96,32},{112,48},{1... | collective-permute-start | bytes 98312 | tf_op jit(solution)/shard_map/ppermute | solution.py:176
  15.2 4.3 %copy-start.1 = (s32[1,1,128]{2,1,0:T(1,128)S(1)}, s32[1,1,128]{2,1,0:T(1,128)}, u32[]{:S(2)}) copy-start(s32[1,1,128]{2,1,0:T(1,128)} %param.7) | copy-start | bytes 1540
  15.2 4.3 %copy-start.2 = (s32[1,1,128]{2,1,0:T(1,128)S(1)}, s32[1,1,128]{2,1,0:T(1,128)}, u32[]{:S(2)}) copy-start(s32[1,1,128]{2,1,0:T(1,128)} %param.6) | copy-start | bytes 1540
  15.2 6.3 %collective-permute-start.5 = (f32[16,8,128]{2,1,0:T(8,128)S(1)}, f32[16,8,128]{2,1,0:T(8,128)S(1)}, u32[]{:S(2)}, u32[]{:S(2)}) collective-permute-start(f32[16,8,128]{2,1,0:T(8,128)S(1)} %shard_map.55.refs_2_), channel_id=1, source_target_pairs={{0,12},{1,13},{2,14},{3,15},{4,8},{5,9},{6,10},{7,11},{8,4},{9,5},... | collective-permute-start | bytes 196616 | tf_op jit(solution)/shard_map/ppermute | solution.py:176
  18.3 5.8 %collective-permute-start.4 = (f32[16,8,128]{2,1,0:T(8,128)S(1)}, f32[16,8,128]{2,1,0:T(8,128)S(1)}, u32[]{:S(2)}, u32[]{:S(2)}) collective-permute-start(f32[16,8,128]{2,1,0:T(8,128)S(1)} %shard_map.55.refs_2_), channel_id=1, source_target_pairs={{0,8},{1,9},{2,10},{3,11},{4,12},{5,13},{6,14},{7,15},{8,0},{9,1},... | collective-permute-start | bytes 196616 | tf_op jit(solution)/shard_map/ppermute | solution.py:176
  18.9 5.1 %collective-permute-start.3 = (f32[16,8,128]{2,1,0:T(8,128)S(1)}, f32[16,8,128]{2,1,0:T(8,128)S(1)}, u32[]{:S(2)}, u32[]{:S(2)}) collective-permute-start(f32[16,8,128]{2,1,0:T(8,128)S(1)} %shard_map.55.refs_2_), channel_id=1, source_target_pairs={{0,4},{1,5},{2,6},{3,7},{4,0},{5,1},{6,2},{7,3},{8,12},{9,13},{10,... | collective-permute-start | bytes 196616 | tf_op jit(solution)/shard_map/ppermute | solution.py:176
  19.4 4.7 %collective-permute-start.10 = (f32[32,8,128]{2,1,0:T(8,128)S(1)}, f32[32,8,128]{2,1,0:T(8,128)S(1)}, u32[]{:S(2)}, u32[]{:S(2)}) collective-permute-start(f32[32,8,128]{2,1,0:T(8,128)S(1)} %shard_map.57.refs_6_), channel_id=1, source_target_pairs={{0,16},{16,0},{32,48},{48,32},{64,80},{80,64},{96,112},{112,96},{1... | collective-permute-start | bytes 393224 | tf_op jit(solution)/shard_map/ppermute | solution.py:176
  30.3 4.9 %collective-permute-start.17 = (f32[32,8,128]{2,1,0:T(8,128)S(1)}, f32[32,8,128]{2,1,0:T(8,128)S(1)}, u32[]{:S(2)}, u32[]{:S(2)}) collective-permute-start(f32[32,8,128]{2,1,0:T(8,128)S(1)} %get-tuple-element.30), channel_id=1, source_target_pairs={{0,16},{16,0},{32,48},{48,32},{64,80},{80,64},{96,112},{112,96},{1... | collective-permute-start | bytes 393224 | tf_op jit(solution)/shard_map/ppermute | solution.py:176
  30.4 6.9 %collective-permute-start.11 = (f32[16,8,128]{2,1,0:T(8,128)S(1)}, f32[16,8,128]{2,1,0:T(8,128)S(1)}, u32[]{:S(2)}, u32[]{:S(2)}) collective-permute-start(f32[16,8,128]{2,1,0:T(8,128)S(1)} %get-tuple-element.22), channel_id=1, source_target_pairs={{0,4},{1,5},{2,6},{3,7},{4,0},{5,1},{6,2},{7,3},{8,12},{9,13},{10,... | collective-permute-start | bytes 196616 | tf_op jit(solution)/shard_map/ppermute | solution.py:176
  30.6 9.4 %collective-permute-start.12 = (f32[16,8,128]{2,1,0:T(8,128)S(1)}, f32[16,8,128]{2,1,0:T(8,128)S(1)}, u32[]{:S(2)}, u32[]{:S(2)}) collective-permute-start(f32[16,8,128]{2,1,0:T(8,128)S(1)} %get-tuple-element.23), channel_id=1, source_target_pairs={{0,8},{1,9},{2,10},{3,11},{4,12},{5,13},{6,14},{7,15},{8,0},{9,1},... | collective-permute-start | bytes 196616 | tf_op jit(solution)/shard_map/ppermute | solution.py:176
  33.2 6.8 %collective-permute-start.13 = (f32[16,8,128]{2,1,0:T(8,128)S(1)}, f32[16,8,128]{2,1,0:T(8,128)S(1)}, u32[]{:S(2)}, u32[]{:S(2)}) collective-permute-start(f32[16,8,128]{2,1,0:T(8,128)S(1)} %get-tuple-element.24), channel_id=1, source_target_pairs={{0,12},{1,13},{2,14},{3,15},{4,8},{5,9},{6,10},{7,11},{8,4},{9,5},... | collective-permute-start | bytes 196616 | tf_op jit(solution)/shard_map/ppermute | solution.py:176
  35.2 11.4 %collective-permute-start.18 = (f32[8,8,128]{2,1,0:T(8,128)S(1)}, f32[8,8,128]{2,1,0:T(8,128)S(1)}, u32[]{:S(2)}, u32[]{:S(2)}) collective-permute-start(f32[8,8,128]{2,1,0:T(8,128)S(1)} %get-tuple-element.32), channel_id=1, source_target_pairs={{0,64},{16,80},{32,96},{48,112},{64,0},{80,16},{96,32},{112,48},{1... | collective-permute-start | bytes 98312 | tf_op jit(solution)/shard_map/ppermute | solution.py:176
  36.1 10.5 %collective-permute-start.19 = (f32[8,8,128]{2,1,0:T(8,128)S(1)}, f32[8,8,128]{2,1,0:T(8,128)S(1)}, u32[]{:S(2)}, u32[]{:S(2)}) collective-permute-start(f32[8,8,128]{2,1,0:T(8,128)S(1)} %get-tuple-element.33), channel_id=1, source_target_pairs={{0,128},{16,144},{32,160},{48,176},{64,192},{80,208},{96,224},{112... | collective-permute-start | bytes 98312 | tf_op jit(solution)/shard_map/ppermute | solution.py:176
  37.2 9.3 %collective-permute-start.20 = (f32[8,8,128]{2,1,0:T(8,128)S(1)}, f32[8,8,128]{2,1,0:T(8,128)S(1)}, u32[]{:S(2)}, u32[]{:S(2)}) collective-permute-start(f32[8,8,128]{2,1,0:T(8,128)S(1)} %get-tuple-element.34), channel_id=1, source_target_pairs={{0,192},{16,208},{32,224},{48,240},{64,128},{80,144},{96,160},{112... | collective-permute-start | bytes 98312 | tf_op jit(solution)/shard_map/ppermute | solution.py:176
  40.0 7.8 %collective-permute-start.14 = (f32[4,8,128]{2,1,0:T(8,128)S(1)}, f32[4,8,128]{2,1,0:T(8,128)S(1)}, u32[]{:S(2)}, u32[]{:S(2)}) collective-permute-start(f32[4,8,128]{2,1,0:T(8,128)S(1)} %get-tuple-element.26), channel_id=1, source_target_pairs={{0,1},{1,0},{2,3},{3,2},{4,5},{5,4},{6,7},{7,6},{8,9},{9,8},{10,11... | collective-permute-start | bytes 49160 | tf_op jit(solution)/shard_map/ppermute | solution.py:176
  42.1 7.8 %collective-permute-start.15 = (f32[4,8,128]{2,1,0:T(8,128)S(1)}, f32[4,8,128]{2,1,0:T(8,128)S(1)}, u32[]{:S(2)}, u32[]{:S(2)}) collective-permute-start(f32[4,8,128]{2,1,0:T(8,128)S(1)} %get-tuple-element.27), channel_id=1, source_target_pairs={{0,2},{1,3},{2,0},{3,1},{4,6},{5,7},{6,4},{7,5},{8,10},{9,11},{10,... | collective-permute-start | bytes 49160 | tf_op jit(solution)/shard_map/ppermute | solution.py:176
  46.6 5.8 %collective-permute-start.16 = (f32[4,8,128]{2,1,0:T(8,128)S(1)}, f32[4,8,128]{2,1,0:T(8,128)S(1)}, u32[]{:S(2)}, u32[]{:S(2)}) collective-permute-start(f32[4,8,128]{2,1,0:T(8,128)S(1)} %get-tuple-element.28), channel_id=1, source_target_pairs={{0,3},{1,2},{2,1},{3,0},{4,7},{5,6},{6,5},{7,4},{8,11},{9,10},{10,... | collective-permute-start | bytes 49160 | tf_op jit(solution)/shard_map/ppermute | solution.py:176
  46.6 5.8 %collective-permute-start.21 = (f32[4,8,128]{2,1,0:T(8,128)S(1)}, f32[4,8,128]{2,1,0:T(8,128)S(1)}, u32[]{:S(2)}, u32[]{:S(2)}) collective-permute-start(f32[4,8,128]{2,1,0:T(8,128)S(1)} %get-tuple-element.36), channel_id=1, source_target_pairs={{0,32},{16,48},{32,0},{48,16},{64,96},{80,112},{96,64},{112,80},{1... | collective-permute-start | bytes 49160 | tf_op jit(solution)/shard_map/ppermute | solution.py:176

commit v4 on v3

--- a/solution.py
+++ b/solution.py
@@ -10,9 +10,15 @@
 CHUNK = 32
 AHEAD = 2
 SLIM = 62
-TLIM = 48
+TLIM = 24
 JOIN = 5 * 10 ** 10
-ORDER = (2, 3, 1)
+FETCH = True
+RING = 8
+PIECE = 16
+PLIM = 24
+PREP = 3 * 10 ** 10
+FETCH_COST = 10 ** 10
+ROW_JOIN = JOIN
 FLOPS = 4 * 16 * 256 * 128 * 128
 SMEM = pl.BlockSpec(memory_space=pltpu.SMEM)
 VMEM = pl.BlockSpec(memory_space=pltpu.VMEM)
@@ -23,6 +29,49 @@
     high = value.astype(jnp.bfloat16)
     low = (value - high.astype(jnp.float32)).astype(jnp.bfloat16)
     return high, low
+
+
+def split_tiles_kernel(tiles, out, held, arrived):
+    slots = out.shape[0]
+    ring, size, side, _ = held.shape
+    chunks = slots // size
+
+    def fetch(chunk):
+        return pltpu.make_async_copy(tiles.at[pl.ds(chunk * size, size)], held.at[chunk % ring], arrived.at[chunk % ring])
+
+    for chunk in range(ring):
+        fetch(chunk).start()
+
+    def step(chunk, carry):
+        fetch(chunk).wait()
+        for offset in range(size):
+            high, low = split(held[chunk % ring, offset])
+            out[chunk * size + offset, :side, :] = high
+            out[chunk * size + offset, side:, :] = low
+
+        @pl.when(chunk + ring < chunks)
+        def _():
+            fetch(chunk + ring).start()
+
+        return carry
+
+    lax.fori_loop(0, chunks, step, 0)
+
+
+def split_tiles(tiles):
+    slots, side, _ = tiles.shape
+    return pl.pallas_call(
+        split_tiles_kernel,
+        out_shape=jax.ShapeDtypeStruct((slots, 2 * side, side), jnp.bfloat16),
+        in_specs=[ANY],
+        out_specs=VMEM,
+        scratch_shapes=[
+            pltpu.VMEM((RING, PIECE, side, side), jnp.float32),
+            pltpu.SemaphoreType.DMA((RING,)),
+        ],
+        compiler_params=pltpu.CompilerParams(vmem_limit_bytes=PLIM * 1024 * 1024),
+        cost_estimate=pl.CostEstimate(flops=PREP, bytes_accessed=8 * slots * side * side, transcendentals=0),
+    )(tiles)
 
 
 def take(refs, count):
@@ -36,17 +85,10 @@
     places, tiles = take(refs, 2)
     row_sources, col_sources = take(refs, row_pieces), take(refs, col_pieces)
     row_parts, col_parts = take(refs, row_pieces), take(refs, col_pieces)
-    held, row_split, col_split, row_sum, col_sum, arrived = refs
-    slots = held.shape[0]
-    chunks = slots // CHUNK
+    row_split, col_split, row_sum, col_sum = refs
+    slots, _, side = tiles.shape
     vectors = row_sum.shape[1]
 
-    def fetch(chunk):
-        place = pl.ds(chunk * CHUNK, CHUNK)
-        return pltpu.make_async_copy(tiles.at[place], held.at[place], arrived.at[chunk])
-
-    for chunk in range(AHEAD):
-        fetch(chunk).start()
     for sources, parts in ((row_sources, row_split), (col_sources, col_split)):
         start = 0
         for source in sources:
@@ -58,28 +100,22 @@
     col_sum[...] = jnp.zeros_like(col_sum)
 
     def step(chunk, carry):
-        fetch(chunk).wait()
-
-        @pl.when(chunk + AHEAD < chunks)
-        def _():
-            fetch(chunk + AHEAD).start()
-
         results = []
         for offset in range(CHUNK):
             slot = chunk * CHUNK + offset
             place = places[slot]
             row, col = place // 128, place % 128
-            high, low = split(held[slot])
+            pair = tiles[slot]
             from_cols = col_split[col]
             from_rows = row_split[row]
             first = lax.dot_general(
                 jnp.concatenate([from_cols, from_cols], axis=1),
-                jnp.concatenate([high, low], axis=1),
+                jnp.concatenate([pair[:side], pair[side:]], axis=1),
                 (((1,), (1,)), ((), ())), preferred_element_type=jnp.float32,
             )
             second = lax.dot_general(
                 jnp.concatenate([from_rows, from_rows], axis=1),
-                jnp.concatenate([high, low], axis=0),
+                pair,
                 (((1,), (0,)), ((), ())), preferred_element_type=jnp.float32,
             )
             results.append((row, col, first[:vectors] + first[vectors:], second[:vectors] + second[vectors:]))
@@ -88,7 +124,7 @@
             col_sum[col] += second
         return carry
 
-    lax.fori_loop(0, chunks, step, 0)
+    lax.fori_loop(0, slots // CHUNK, step, 0)
     for parts, total in ((row_parts, row_sum), (col_parts, col_sum)):
         start = 0
         for part in parts:
@@ -97,7 +133,7 @@
 
 
 def multiply(places, tiles, row_inputs, col_inputs):
-    slots, side, _ = tiles.shape
+    slots, _, side = tiles.shape
     pieces = len(row_inputs), len(col_inputs)
     blocks = sum(part.shape[0] for part in row_inputs)
     vectors = row_inputs[0].shape[1]
@@ -105,20 +141,33 @@
     results = pl.pallas_call(
         functools.partial(tile_kernel, *pieces),
         out_shape=parts,
-        in_specs=[SMEM, ANY] + [VMEM] * len(parts),
+        in_specs=[SMEM] + [VMEM] * (1 + len(parts)),
         out_specs=[VMEM] * len(parts),
         scratch_shapes=[
-            pltpu.VMEM(tiles.shape, jnp.float32),
             pltpu.VMEM((blocks + 8, 2 * vectors, side), jnp.bfloat16),
             pltpu.VMEM((blocks + 8, 2 * vectors, side), jnp.bfloat16),
             pltpu.VMEM((blocks + 8, vectors, side), jnp.float32),
             pltpu.VMEM((blocks + 8, vectors, side), jnp.float32),
-            pltpu.SemaphoreType.DMA((slots // CHUNK,)),
         ],
         compiler_params=pltpu.CompilerParams(vmem_limit_bytes=TLIM * 1024 * 1024),
         cost_estimate=pl.CostEstimate(flops=FLOPS, bytes_accessed=4 * slots * side * side, transcendentals=0),
     )(places, tiles, *row_inputs, *col_inputs)
     return results[:pieces[0]], results[pieces[0]:]
+
+
+def fetch_kernel(value, out):
+    out[...] = value[...]
+
+
+def fetch(value):
+    return pl.pallas_call(
+        fetch_kernel,
+        out_shape=jax.ShapeDtypeStruct(value.shape, value.dtype),
+        in_specs=[VMEM],
+        out_specs=VMEM,
+        compiler_params=pltpu.CompilerParams(vmem_limit_bytes=4 * 1024 * 1024),
+        cost_estimate=pl.CostEstimate(flops=FETCH_COST, bytes_accessed=1024, transcendentals=0),
+    )(value)
 
 
 def join_kernel(*refs):
@@ -129,7 +178,7 @@
         start += part.shape[0]
 
 
-def join(parts):
+def join(parts, cost=JOIN):
     size = sum(part.shape[0] for part in parts)
     return pl.pallas_call(
         join_kernel,
@@ -137,7 +186,7 @@
         in_specs=[VMEM] * len(parts),
         out_specs=VMEM,
         compiler_params=pltpu.CompilerParams(vmem_limit_bytes=4 * 1024 * 1024),
-        cost_estimate=pl.CostEstimate(flops=JOIN, bytes_accessed=1024, transcendentals=0),
+        cost_estimate=pl.CostEstimate(flops=cost, bytes_accessed=1024, transcendentals=0),
     )(*parts)
 
 
@@ -175,30 +224,38 @@
     def swap(value, axis, offset):
         return lax.ppermute(value, axis, [(j, j ^ offset) for j in range(lax.axis_size(axis))])
 
-    def swaps(values, axis, step):
-        sent = {index: swap(values[index], axis, index * step) for index in ORDER}
-        return [sent[index] for index in sorted(sent)]
+    def gray(offset):
+        return offset ^ (offset >> 1)
 
     rows, cols = tile_rows[0, 0], tile_cols[0, 0]
     row_offset = (rows // local_blocks) ^ lax.axis_index("col")
     col_offset = (cols // local_blocks) ^ lax.axis_index("row")
-    col_offset = (col_offset & 1) * (row_devices // 2) + (col_offset >> 1)
+    row_offset = (row_offset & 12) + gray(row_offset & 3)
+    near_z, near_x = col_offset >> 1 & 1, gray(col_offset >> 2)
+    col_offset = (col_offset & 1 ^ near_z ^ near_x & 1 ^ near_x >> 1) * 8 + near_x * 2 + near_z
     places = (row_offset * local_blocks + rows % local_blocks) * 128 + col_offset * local_blocks + cols % local_blocks
     slot = jnp.arange(slots, dtype=jnp.int32)
     places = jnp.where(slot < tile_counts[0, 0], places, col_devices * local_blocks * 128 + row_devices * local_blocks)
 
-    pair = join([own, swap(own, "row", 2)])
-    close = join([own] + swaps([own] * 4, "col", 1))
-    half = join([pair] + swaps([pair] * 4, "row", 4))
-    row_inputs = [close] + swaps([close] * 4, "col", 4)
+    local = fetch(own) if FETCH else own
+    couple = join([local, swap(own, "col", 1)])
+    pair = join([local, swap(own, "row", 3)], ROW_JOIN)
+    close = join([couple, swap(couple, "col", 3)])
+    quad = join([pair, swap(pair, "row", 5)], ROW_JOIN)
+    close, blocks = lax.optimization_barrier((close, tiles))
+    pairs = split_tiles(blocks[0, 0])
+    row_inputs = [close] + [swap(close, "col", offset) for offset in (4, 8, 12)]
+    half = join([quad, swap(quad, "row", 13)], ROW_JOIN)
     col_inputs = [half, swap(half, "row", 1)]
 
-    row_parts, col_parts = multiply(places, tiles[0, 0], row_inputs, col_inputs)
-
-    half = fold([col_parts[0], swap(col_parts[1], "row", 1)], 4)
-    close = fold([row_parts[0]] + swaps(row_parts, "col", 4), 4)
-    pair = fold([half[0]] + swaps(half, "row", 4), 2)
-    terms = [close[0]] + swaps(close, "col", 1) + [pair[0], swap(pair[1], "row", 2)]
+    row_parts, col_parts = multiply(places, pairs, row_inputs, col_inputs)
+
+    close = fold([row_parts[0]] + [swap(row_parts[index], "col", 4 * index) for index in (2, 1, 3)], 2)
+    half = fold([col_parts[0], swap(col_parts[1], "row", 1)], 2)
+    quad = fold([half[0], swap(half[1], "row", 13)], 2)
+    couple = fold([close[0], swap(close[1], "col", 3)], 2)
+    pair = fold([quad[0], swap(quad[1], "row", 5)], 2)
+    terms = [couple[0], swap(couple[1], "col", 1), pair[0], swap(pair[1], "row", 3)]
     total = functools.reduce(jnp.add, terms)
     return total.transpose(1, 0, 2).reshape(vector_count, width)
 

time: 53.2 us -> 48.5 us (0.912)
  the two profiles are of different devices: /device:TPU:6 before, /device:TPU:1 now
where the time goes in v4:
time: 48.5 us; the launch traced here: 48.3 us
  starting transfers between devices  33.9 us (70%)
  Pallas kernels  6.42 us (13%)
  waiting for transfers between devices  5.83 us (12%)
  between operations  0.78 us (2%)
  local copies, waits for them, and re-layouts  0.77 us (2%)
  other arithmetic  0.64 us (1%)
    ppermute x18, starting transfers between devices, swap(): lax.ppermute(value, axis, [(j, j ^ offset) for j in range(lax.axis_size(a...  33.9 us
    ppermute x18, waiting for transfers between devices, swap(): lax.ppermute(value, axis, [(j, j ^ offset) for j in range(lax.axis_size(a...  5.83 us
    pallas_call x1, Pallas kernels, multiply(): pl.pallas_call(functools.partial(tile_kernel, *pieces), out_shape=parts,...  4.77 us
    pallas_call x1, Pallas kernels, split_tiles(): pl.pallas_call(split_tiles_kernel, out_shape=jax.ShapeDtypeStruct((slots,...  1.56 us
  transfers between devices with their start and end apart: 18, of which 5 were waited for; matrix products, arithmetic and copies ran while one was open for 0% of the time, Pallas kernels for 3%

profile of v4, /device:TPU:1, one launch (start us, length us, event | category | flops | bytes accessed | tf_op | source)
XLA Modules:
  0.0 48.3 jit_solution(5866132084967100079)
XLA Ops:
  0.0 3.0 %collective-permute-start.5 = (f32[4,8,128]{2,1,0:T(8,128)}, f32[4,8,128]{2,1,0:T(8,128)S(1)}, u32[]{:S(2)}, u32[]{:S(2)}) collective-permute-start(f32[4,8,128]{2,1,0:T(8,128)} %bitcast.39), channel_id=1, source_target_pairs={{0,48},{16,32},{32,16},{48,0},{64,112},{80,96},{96,80},{112,64},{1... | collective-permute-start | bytes 49160 | tf_op jit(solution)/shard_map/ppermute | solution.py:225
  3.0 3.0 %collective-permute-start = (f32[4,8,128]{2,1,0:T(8,128)}, f32[4,8,128]{2,1,0:T(8,128)S(1)}, u32[]{:S(2)}, u32[]{:S(2)}) collective-permute-start(f32[4,8,128]{2,1,0:T(8,128)} %bitcast.40), channel_id=1, source_target_pairs={{0,1},{1,0},{2,3},{3,2},{4,5},{5,4},{6,7},{7,6},{8,9},{9,8},{10,11... | collective-permute-start | bytes 49160 | tf_op jit(solution)/shard_map/ppermute | solution.py:225
  6.0 0.0 copy-start
  6.0 0.7 %copy-done = f32[8,512]{1,0:T(8,128)S(1)} copy-done((f32[8,512]{1,0:T(8,128)S(1)}, f32[8,512]{1,0:T(8,128)}, u32[]{:S(2)}) %copy-start) | copy-done | bytes 16408
  6.8 0.0 copy-start.1
  7.5 0.0 copy-done.1
  7.5 0.0 copy-done.2
  7.5 0.0 collective-permute-done.5.refs_1_
  7.5 1.3 %collective-permute-start.6 = (f32[8,8,128]{2,1,0:T(8,128)S(1)}, f32[8,8,128]{2,1,0:T(8,128)S(1)}, u32[]{:S(2)}, u32[]{:S(2)}) collective-permute-start(f32[8,8,128]{2,1,0:T(8,128)S(1)} %shard_map.59.refs_0_), channel_id=1, source_target_pairs={{0,80},{16,64},{32,112},{48,96},{64,16},{80,0},{96,48},{112,32},{1... | collective-permute-start | bytes 98312 | tf_op jit(solution)/shard_map/ppermute | solution.py:225
  8.8 0.0 collective-permute-done.refs_1_
  8.8 3.3 %collective-permute-start.1 = (f32[8,8,128]{2,1,0:T(8,128)S(1)}, f32[8,8,128]{2,1,0:T(8,128)S(1)}, u32[]{:S(2)}, u32[]{:S(2)}) collective-permute-start(f32[8,8,128]{2,1,0:T(8,128)S(1)} %shard_map.56.refs_0_), channel_id=1, source_target_pairs={{0,3},{1,2},{2,1},{3,0},{4,7},{5,6},{6,5},{7,4},{8,11},{9,10},{10,... | collective-permute-start | bytes 98312 | tf_op jit(solution)/shard_map/ppermute | solution.py:225
  12.2 0.0 collective-permute-done.6.refs_1_
  12.2 3.4 %collective-permute-start.7 = (f32[16,8,128]{2,1,0:T(8,128)S(1)}, f32[16,8,128]{2,1,0:T(8,128)S(1)}, u32[]{:S(2)}, u32[]{:S(2)}) collective-permute-start(f32[16,8,128]{2,1,0:T(8,128)S(1)} %shard_map.60.refs_0_), channel_id=1, source_target_pairs={{0,208},{16,192},{32,240},{48,224},{64,144},{80,128},{96,176},{112... | collective-permute-start | bytes 196616 | tf_op jit(solution)/shard_map/ppermute | solution.py:225
  15.6 0.0 collective-permute-done.1.refs_1_
  15.6 0.0 slice-start
  15.6 0.0 slice-start.1
  15.6 2.8 %collective-permute-start.4 = (f32[16,8,128]{2,1,0:T(8,128)S(1)}, f32[16,8,128]{2,1,0:T(8,128)S(1)}, u32[]{:S(2)}, u32[]{:S(2)}) collective-permute-start(f32[16,8,128]{2,1,0:T(8,128)S(1)} %shard_map.57.refs_2_), channel_id=1, source_target_pairs={{0,12},{1,13},{2,14},{3,15},{4,8},{5,9},{6,10},{7,11},{8,4},{9,5},... | collective-permute-start | bytes 196616 | tf_op jit(solution)/shard_map/ppermute | solution.py:225
  18.4 0.3 collective-permute-start.3
  18.8 0.4 collective-permute-start.2
  19.1 0.0 collective-permute-done.7.refs_1_
  19.1 0.4 collective-permute-start.8
  19.6 0.0 slice-done
  19.6 0.0 slice-done.1
  19.6 1.6 %shard_map.58.refs_1_ = bf16[128,256,128]{2,1,0:T(8,128)(2,1)S(1)} custom-call(f32[128,128,128]{2,1,0:T(8,128)S(1)} %bitcast.38), custom_call_target="tpu_custom_call" | custom-call | flops 30000001024 | bytes 16777216 | tf_op jit(solution)/shard_map/pallas_call | solution.py:63
  21.2 0.3 collective-permute-done.4.refs_5_
  21.4 2.2 %collective-permute-done.3.refs_4_ = f32[16,8,128]{2,1,0:T(8,128)S(1)} collective-permute-done((f32[16,8,128]{2,1,0:T(8,128)S(1)}, f32[16,8,128]{2,1,0:T(8,128)S(1)}, u32[]{:S(2)}, u32[]{:S(2)}) %collective-permute-start.3) | collective-permute-done | bytes 65568 | tf_op jit(solution)/shard_map/ppermute | solution.py:225
  23.7 0.0 collective-permute-done.2.refs_3_
  23.7 0.0 collective-permute-done.8.refs_7_
  23.7 4.8 %shard_map.62 = (f32[16,8,128]{2,1,0:T(8,128)S(1)}, f32[16,8,128]{2,1,0:T(8,128)S(1)}, f32[16,8,128]{2,1,0:T(8,128)S(1)}, f32[16,8,128]{2,1,0:T(8,128)S(1)}, f32...) custom-call(s32[128]{0:T(128)S(1)} %compare_select_fusion.refs_0_, bf16[128,256,128]{2,1,0:T(8,128)(2,1)S(1)} %shard_map.58.refs_1_, ...), custom_call_target="tpu_custom_call" | custom-call | flops 268435456 | bytes 8388608 | tf_op jit(solution)/shard_map/pallas_call | solution.py:141
  28.5 1.2 %collective-permute-start.14 = (f32[32,8,128]{2,1,0:T(8,128)S(1)}, f32[32,8,128]{2,1,0:T(8,128)S(1)}, u32[]{:S(2)}, u32[]{:S(2)}) collective-permute-start(f32[32,8,128]{2,1,0:T(8,128)S(1)} %get-tuple-element.34), channel_id=1, source_target_pairs={{0,16},{16,0},{32,48},{48,32},{64,80},{80,64},{96,112},{112,96},{1... | collective-permute-start | bytes 393224 | tf_op jit(solution)/shard_map/ppermute | solution.py:225
  29.7 1.5 %collective-permute-start.9 = (f32[16,8,128]{2,1,0:T(8,128)S(1)}, f32[16,8,128]{2,1,0:T(8,128)S(1)}, u32[]{:S(2)}, u32[]{:S(2)}) collective-permute-start(f32[16,8,128]{2,1,0:T(8,128)S(1)} %get-tuple-element.26), channel_id=1, source_target_pairs={{0,8},{1,9},{2,10},{3,11},{4,12},{5,13},{6,14},{7,15},{8,0},{9,1},... | collective-permute-start | bytes 196616 | tf_op jit(solution)/shard_map/ppermute | solution.py:225
  31.2 0.4 collective-permute-start.10
  31.6 1.3 %collective-permute-start.11 = (f32[16,8,128]{2,1,0:T(8,128)S(1)}, f32[16,8,128]{2,1,0:T(8,128)S(1)}, u32[]{:S(2)}, u32[]{:S(2)}) collective-permute-start(f32[16,8,128]{2,1,0:T(8,128)S(1)} %get-tuple-element.28), channel_id=1, source_target_pairs={{0,12},{1,13},{2,14},{3,15},{4,8},{5,9},{6,10},{7,11},{8,4},{9,5},... | collective-permute-start | bytes 196616 | tf_op jit(solution)/shard_map/ppermute | solution.py:225
  32.9 0.0 collective-permute-done.14.refs_1_
  33.0 2.4 %collective-permute-start.15 = (f32[16,8,128]{2,1,0:T(8,128)S(1)}, f32[16,8,128]{2,1,0:T(8,128)S(1)}, u32[]{:S(2)}, u32[]{:S(2)}) collective-permute-start(f32[16,8,128]{2,1,0:T(8,128)S(1)} %get-tuple-element.36), channel_id=1, source_target_pairs={{0,208},{16,192},{32,240},{48,224},{64,144},{80,128},{96,176},{112... | collective-permute-start | bytes 196616 | tf_op jit(solution)/shard_map/ppermute | solution.py:225
  35.4 0.0 collective-permute-done.9.refs_1_
  35.4 0.0 collective-permute-done.10.refs_2_
  35.4 0.7 %collective-permute-done.11.refs_3_ = f32[16,8,128]{2,1,0:T(8,128)S(1)} collective-permute-done((f32[16,8,128]{2,1,0:T(8,128)S(1)}, f32[16,8,128]{2,1,0:T(8,128)S(1)}, u32[]{:S(2)}, u32[]{:S(2)}) %collective-permute-start.11) | collective-permute-done | bytes 65568 | tf_op jit(solution)/shard_map/ppermute | solution.py:225
  36.1 3.3 %collective-permute-start.12 = (f32[8,8,128]{2,1,0:T(8,128)S(1)}, f32[8,8,128]{2,1,0:T(8,128)S(1)}, u32[]{:S(2)}, u32[]{:S(2)}) collective-permute-start(f32[8,8,128]{2,1,0:T(8,128)S(1)} %get-tuple-element.30), channel_id=1, source_target_pairs={{0,3},{1,2},{2,1},{3,0},{4,7},{5,6},{6,5},{7,4},{8,11},{9,10},{10,... | collective-permute-start | bytes 98312 | tf_op jit(solution)/shard_map/ppermute | solution.py:225
  39.3 0.0 collective-permute-done.15.refs_1_
  39.4 2.6 %collective-permute-start.16 = (f32[8,8,128]{2,1,0:T(8,128)S(1)}, f32[8,8,128]{2,1,0:T(8,128)S(1)}, u32[]{:S(2)}, u32[]{:S(2)}) collective-permute-start(f32[8,8,128]{2,1,0:T(8,128)S(1)} %get-tuple-element.38), channel_id=1, source_target_pairs={{0,80},{16,64},{32,112},{48,96},{64,16},{80,0},{96,48},{112,32},{1... | collective-permute-start | bytes 98312 | tf_op jit(solution)/shard_map/ppermute | solution.py:225
  41.9 0.0 collective-permute-done.12.refs_1_
  41.9 1.3 %collective-permute-start.13 = (f32[4,8,128]{2,1,0:T(8,128)S(1)}, f32[4,8,128]{2,1,0:T(8,128)S(1)}, u32[]{:S(2)}, u32[]{:S(2)}) collective-permute-start(f32[4,8,128]{2,1,0:T(8,128)S(1)} %get-tuple-element.32), channel_id=1, source_target_pairs={{0,1},{1,0},{2,3},{3,2},{4,5},{5,4},{6,7},{7,6},{8,9},{9,8},{10,11... | collective-permute-start | bytes 49160 | tf_op jit(solution)/shard_map/ppermute | solution.py:225
  43.2 0.9 %collective-permute-done.16.refs_1_ = f32[8,8,128]{2,1,0:T(8,128)S(1)} collective-permute-done((f32[8,8,128]{2,1,0:T(8,128)S(1)}, f32[8,8,128]{2,1,0:T(8,128)S(1)}, u32[]{:S(2)}, u32[]{:S(2)}) %collective-permute-start.16) | collective-permute-done | bytes 32800 | tf_op jit(solution)/shard_map/ppermute | solution.py:225
  44.1 1.9 %collective-permute-start.17 = (f32[4,8,128]{2,1,0:T(8,128)S(1)}, f32[4,8,128]{2,1,0:T(8,128)S(1)}, u32[]{:S(2)}, u32[]{:S(2)}) collective-permute-start(f32[4,8,128]{2,1,0:T(8,128)S(1)} %get-tuple-element.40), channel_id=1, source_target_pairs={{0,48},{16,32},{32,16},{48,0},{64,112},{80,96},{96,80},{112,64},{1... | collective-permute-start | bytes 49160 | tf_op jit(solution)/shard_map/ppermute | solution.py:225
  46.0 0.0 collective-permute-done.13
  46.0 1.7 %collective-permute-done.17 = f32[4,8,128]{2,1,0:T(8,128)S(1)} collective-permute-done((f32[4,8,128]{2,1,0:T(8,128)S(1)}, f32[4,8,128]{2,1,0:T(8,128)S(1)}, u32[]{:S(2)}, u32[]{:S(2)}) %collective-permute-start.17) | collective-permute-done | bytes 16416 | tf_op jit(solution)/shard_map/ppermute | solution.py:225
  47.7 0.6 %add_bitcast_fusion = f32[8,512]{1,0:T(8,128)} fusion(f32[4,8,128]{2,1,0:T(8,128)S(1)} %collective-permute-done.17, f32[4,8,128]{2,1,0:T(8,128)S(1)} %get-tuple-element.39, f32[4,8,128]{2,1,0:T(8,128)S(1)} %get-tuple-element.31, f32[4,8,128]{2,1,0:T(8,128)S(1)} %collective-permute-done.13), kind=kLoop, calls=%fused_computation | loop fusion | flops 12288 | bytes 81920 | tf_op jit(solution)/shard_map/reshape | solution.py:260
  (14 shorter events, 0.1 us)
Async XLA Ops:
  0.0 7.5 %collective-permute-start.5 = (f32[4,8,128]{2,1,0:T(8,128)}, f32[4,8,128]{2,1,0:T(8,128)S(1)}, u32[]{:S(2)}, u32[]{:S(2)}) collective-permute-start(f32[4,8,128]{2,1,0:T(8,128)} %bitcast.39), channel_id=1, source_target_pairs={{0,48},{16,32},{32,16},{48,0},{64,112},{80,96},{96,80},{112,64},{1... | collective-permute-start | bytes 49160 | tf_op jit(solution)/shard_map/ppermute | solution.py:225
  3.0 5.8 %collective-permute-start = (f32[4,8,128]{2,1,0:T(8,128)}, f32[4,8,128]{2,1,0:T(8,128)S(1)}, u32[]{:S(2)}, u32[]{:S(2)}) collective-permute-start(f32[4,8,128]{2,1,0:T(8,128)} %bitcast.40), channel_id=1, source_target_pairs={{0,1},{1,0},{2,3},{3,2},{4,5},{5,4},{6,7},{7,6},{8,9},{9,8},{10,11... | collective-permute-start | bytes 49160 | tf_op jit(solution)/shard_map/ppermute | solution.py:225
  6.0 0.8 %copy-start = (f32[8,512]{1,0:T(8,128)S(1)}, f32[8,512]{1,0:T(8,128)}, u32[]{:S(2)}) copy-start(f32[8,512]{1,0:T(8,128)} %param.9) | copy-start | bytes 49156
  6.8 0.7 %copy-start.1 = (s32[1,1,128]{2,1,0:T(1,128)S(1)}, s32[1,1,128]{2,1,0:T(1,128)}, u32[]{:S(2)}) copy-start(s32[1,1,128]{2,1,0:T(1,128)} %param.7) | copy-start | bytes 1540
  6.8 0.7 %copy-start.2 = (s32[1,1,128]{2,1,0:T(1,128)S(1)}, s32[1,1,128]{2,1,0:T(1,128)}, u32[]{:S(2)}) copy-start(s32[1,1,128]{2,1,0:T(1,128)} %param.6) | copy-start | bytes 1540
  7.5 4.7 %collective-permute-start.6 = (f32[8,8,128]{2,1,0:T(8,128)S(1)}, f32[8,8,128]{2,1,0:T(8,128)S(1)}, u32[]{:S(2)}, u32[]{:S(2)}) collective-permute-start(f32[8,8,128]{2,1,0:T(8,128)S(1)} %shard_map.59.refs_0_), channel_id=1, source_target_pairs={{0,80},{16,64},{32,112},{48,96},{64,16},{80,0},{96,48},{112,32},{1... | collective-permute-start | bytes 98312 | tf_op jit(solution)/shard_map/ppermute | solution.py:225
  8.8 6.7 %collective-permute-start.1 = (f32[8,8,128]{2,1,0:T(8,128)S(1)}, f32[8,8,128]{2,1,0:T(8,128)S(1)}, u32[]{:S(2)}, u32[]{:S(2)}) collective-permute-start(f32[8,8,128]{2,1,0:T(8,128)S(1)} %shard_map.56.refs_0_), channel_id=1, source_target_pairs={{0,3},{1,2},{2,1},{3,0},{4,7},{5,6},{6,5},{7,4},{8,11},{9,10},{10,... | collective-permute-start | bytes 98312 | tf_op jit(solution)/shard_map/ppermute | solution.py:225
  12.2 6.9 %collective-permute-start.7 = (f32[16,8,128]{2,1,0:T(8,128)S(1)}, f32[16,8,128]{2,1,0:T(8,128)S(1)}, u32[]{:S(2)}, u32[]{:S(2)}) collective-permute-start(f32[16,8,128]{2,1,0:T(8,128)S(1)} %shard_map.60.refs_0_), channel_id=1, source_target_pairs={{0,208},{16,192},{32,240},{48,224},{64,144},{80,128},{96,176},{112... | collective-permute-start | bytes 196616 | tf_op jit(solution)/shard_map/ppermute | solution.py:225
  15.6 4.0 %slice-start = ((s8[8388608]{0:T(1024)(128)(4,1)}), s8[4194304]{0:T(1024)(128)(4,1)S(1)}, s32[]{:S(2)}) async-start(s8[8388608]{0:T(1024)(128)(4,1)} %bitcast.36), calls=%async_computation | async-start | bytes 8388608
  15.6 4.0 %slice-start.1 = ((s8[8388608]{0:T(1024)(128)(4,1)}), s8[4194304]{0:T(1024)(128)(4,1)S(1)}, s32[]{:S(2)}) async-start(s8[8388608]{0:T(1024)(128)(4,1)} %bitcast.36), calls=%async_computation.1 | async-start | bytes 8388608
  15.6 5.8 %collective-permute-start.4 = (f32[16,8,128]{2,1,0:T(8,128)S(1)}, f32[16,8,128]{2,1,0:T(8,128)S(1)}, u32[]{:S(2)}, u32[]{:S(2)}) collective-permute-start(f32[16,8,128]{2,1,0:T(8,128)S(1)} %shard_map.57.refs_2_), channel_id=1, source_target_pairs={{0,12},{1,13},{2,14},{3,15},{4,8},{5,9},{6,10},{7,11},{8,4},{9,5},... | collective-permute-start | bytes 196616 | tf_op jit(solution)/shard_map/ppermute | solution.py:225
  18.4 5.3 %collective-permute-start.3 = (f32[16,8,128]{2,1,0:T(8,128)S(1)}, f32[16,8,128]{2,1,0:T(8,128)S(1)}, u32[]{:S(2)}, u32[]{:S(2)}) collective-permute-start(f32[16,8,128]{2,1,0:T(8,128)S(1)} %shard_map.57.refs_2_), channel_id=1, source_target_pairs={{0,8},{1,9},{2,10},{3,11},{4,12},{5,13},{6,14},{7,15},{8,0},{9,1},... | collective-permute-start | bytes 196616 | tf_op jit(solution)/shard_map/ppermute | solution.py:225
  18.8 4.9 %collective-permute-start.2 = (f32[16,8,128]{2,1,0:T(8,128)S(1)}, f32[16,8,128]{2,1,0:T(8,128)S(1)}, u32[]{:S(2)}, u32[]{:S(2)}) collective-permute-start(f32[16,8,128]{2,1,0:T(8,128)S(1)} %shard_map.57.refs_2_), channel_id=1, source_target_pairs={{0,4},{1,5},{2,6},{3,7},{4,0},{5,1},{6,2},{7,3},{8,12},{9,13},{10,... | collective-permute-start | bytes 196616 | tf_op jit(solution)/shard_map/ppermute | solution.py:225
  19.1 4.5 %collective-permute-start.8 = (f32[32,8,128]{2,1,0:T(8,128)S(1)}, f32[32,8,128]{2,1,0:T(8,128)S(1)}, u32[]{:S(2)}, u32[]{:S(2)}) collective-permute-start(f32[32,8,128]{2,1,0:T(8,128)S(1)} %shard_map.61.refs_6_), channel_id=1, source_target_pairs={{0,16},{16,0},{32,48},{48,32},{64,80},{80,64},{96,112},{112,96},{1... | collective-permute-start | bytes 393224 | tf_op jit(solution)/shard_map/ppermute | solution.py:225
  28.5 4.5 %collective-permute-start.14 = (f32[32,8,128]{2,1,0:T(8,128)S(1)}, f32[32,8,128]{2,1,0:T(8,128)S(1)}, u32[]{:S(2)}, u32[]{:S(2)}) collective-permute-start(f32[32,8,128]{2,1,0:T(8,128)S(1)} %get-tuple-element.34), channel_id=1, source_target_pairs={{0,16},{16,0},{32,48},{48,32},{64,80},{80,64},{96,112},{112,96},{1... | collective-permute-start | bytes 393224 | tf_op jit(solution)/shard_map/ppermute | solution.py:225
  29.7 5.7 %collective-permute-start.9 = (f32[16,8,128]{2,1,0:T(8,128)S(1)}, f32[16,8,128]{2,1,0:T(8,128)S(1)}, u32[]{:S(2)}, u32[]{:S(2)}) collective-permute-start(f32[16,8,128]{2,1,0:T(8,128)S(1)} %get-tuple-element.26), channel_id=1, source_target_pairs={{0,8},{1,9},{2,10},{3,11},{4,12},{5,13},{6,14},{7,15},{8,0},{9,1},... | collective-permute-start | bytes 196616 | tf_op jit(solution)/shard_map/ppermute | solution.py:225
  31.2 4.2 %collective-permute-start.10 = (f32[16,8,128]{2,1,0:T(8,128)S(1)}, f32[16,8,128]{2,1,0:T(8,128)S(1)}, u32[]{:S(2)}, u32[]{:S(2)}) collective-permute-start(f32[16,8,128]{2,1,0:T(8,128)S(1)} %get-tuple-element.27), channel_id=1, source_target_pairs={{0,4},{1,5},{2,6},{3,7},{4,0},{5,1},{6,2},{7,3},{8,12},{9,13},{10,... | collective-permute-start | bytes 196616 | tf_op jit(solution)/shard_map/ppermute | solution.py:225
  31.6 4.5 %collective-permute-start.11 = (f32[16,8,128]{2,1,0:T(8,128)S(1)}, f32[16,8,128]{2,1,0:T(8,128)S(1)}, u32[]{:S(2)}, u32[]{:S(2)}) collective-permute-start(f32[16,8,128]{2,1,0:T(8,128)S(1)} %get-tuple-element.28), channel_id=1, source_target_pairs={{0,12},{1,13},{2,14},{3,15},{4,8},{5,9},{6,10},{7,11},{8,4},{9,5},... | collective-permute-start | bytes 196616 | tf_op jit(solution)/shard_map/ppermute | solution.py:225
  33.0 6.4 %collective-permute-start.15 = (f32[16,8,128]{2,1,0:T(8,128)S(1)}, f32[16,8,128]{2,1,0:T(8,128)S(1)}, u32[]{:S(2)}, u32[]{:S(2)}) collective-permute-start(f32[16,8,128]{2,1,0:T(8,128)S(1)} %get-tuple-element.36), channel_id=1, source_target_pairs={{0,208},{16,192},{32,240},{48,224},{64,144},{80,128},{96,176},{112... | collective-permute-start | bytes 196616 | tf_op jit(solution)/shard_map/ppermute | solution.py:225
  36.1 5.9 %collective-permute-start.12 = (f32[8,8,128]{2,1,0:T(8,128)S(1)}, f32[8,8,128]{2,1,0:T(8,128)S(1)}, u32[]{:S(2)}, u32[]{:S(2)}) collective-permute-start(f32[8,8,128]{2,1,0:T(8,128)S(1)} %get-tuple-element.30), channel_id=1, source_target_pairs={{0,3},{1,2},{2,1},{3,0},{4,7},{5,6},{6,5},{7,4},{8,11},{9,10},{10,... | collective-permute-start | bytes 98312 | tf_op jit(solution)/shard_map/ppermute | solution.py:225
  39.4 4.8 %collective-permute-start.16 = (f32[8,8,128]{2,1,0:T(8,128)S(1)}, f32[8,8,128]{2,1,0:T(8,128)S(1)}, u32[]{:S(2)}, u32[]{:S(2)}) collective-permute-start(f32[8,8,128]{2,1,0:T(8,128)S(1)} %get-tuple-element.38), channel_id=1, source_target_pairs={{0,80},{16,64},{32,112},{48,96},{64,16},{80,0},{96,48},{112,32},{1... | collective-permute-start | bytes 98312 | tf_op jit(solution)/shard_map/ppermute | solution.py:225
  41.9 4.1 %collective-permute-start.13 = (f32[4,8,128]{2,1,0:T(8,128)S(1)}, f32[4,8,128]{2,1,0:T(8,128)S(1)}, u32[]{:S(2)}, u32[]{:S(2)}) collective-permute-start(f32[4,8,128]{2,1,0:T(8,128)S(1)} %get-tuple-element.32), channel_id=1, source_target_pairs={{0,1},{1,0},{2,3},{3,2},{4,5},{5,4},{6,7},{7,6},{8,9},{9,8},{10,11... | collective-permute-start | bytes 49160 | tf_op jit(solution)/shard_map/ppermute | solution.py:225
  44.1 3.6 %collective-permute-start.17 = (f32[4,8,128]{2,1,0:T(8,128)S(1)}, f32[4,8,128]{2,1,0:T(8,128)S(1)}, u32[]{:S(2)}, u32[]{:S(2)}) collective-permute-start(f32[4,8,128]{2,1,0:T(8,128)S(1)} %get-tuple-element.40), channel_id=1, source_target_pairs={{0,48},{16,32},{32,16},{48,0},{64,112},{80,96},{96,80},{112,64},{1... | collective-permute-start | bytes 49160 | tf_op jit(solution)/shard_map/ppermute | solution.py:225

commit v5 on v4

--- a/solution.py
+++ b/solution.py
@@ -7,19 +7,21 @@
 from jax.experimental.pallas import tpu as pltpu
 from jax.sharding import PartitionSpec as P
 
-CHUNK = 32
+CHUNK = 128
 AHEAD = 2
 SLIM = 62
 TLIM = 24
 JOIN = 5 * 10 ** 10
 FETCH = True
-RING = 8
+RING = 4
 PIECE = 16
+PREP_RING = 8
 PLIM = 24
 PREP = 3 * 10 ** 10
 FETCH_COST = 10 ** 10
 ROW_JOIN = JOIN
-FLOPS = 4 * 16 * 256 * 128 * 128
+ROW_FOLD = JOIN
+FLOPS = 2 * 10 ** 10
 SMEM = pl.BlockSpec(memory_space=pltpu.SMEM)
 VMEM = pl.BlockSpec(memory_space=pltpu.VMEM)
 ANY = pl.BlockSpec(memory_space=pl.ANY)
@@ -66,8 +68,8 @@
         in_specs=[ANY],
         out_specs=VMEM,
         scratch_shapes=[
-            pltpu.VMEM((RING, PIECE, side, side), jnp.float32),
-            pltpu.SemaphoreType.DMA((RING,)),
+            pltpu.VMEM((PREP_RING, PIECE, side, side), jnp.float32),
+            pltpu.SemaphoreType.DMA((PREP_RING,)),
         ],
         compiler_params=pltpu.CompilerParams(vmem_limit_bytes=PLIM * 1024 * 1024),
         cost_estimate=pl.CostEstimate(flops=PREP, bytes_accessed=8 * slots * side * side, transcendentals=0),
@@ -80,24 +82,20 @@
     return taken
 
 
-def tile_kernel(row_pieces, col_pieces, *refs):
+def product_kernel(flipped, pieces, outputs, *refs):
     refs = list(refs)
-    places, tiles = take(refs, 2)
-    row_sources, col_sources = take(refs, row_pieces), take(refs, col_pieces)
-    row_parts, col_parts = take(refs, row_pieces), take(refs, col_pieces)
-    row_split, col_split, row_sum, col_sum = refs
-    slots, _, side = tiles.shape
-    vectors = row_sum.shape[1]
-
-    for sources, parts in ((row_sources, row_split), (col_sources, col_split)):
-        start = 0
-        for source in sources:
-            high, low = split(source[...])
-            parts[start:start + source.shape[0]] = jnp.concatenate([high, low], axis=1)
-            start += source.shape[0]
-        parts[start] = jnp.zeros_like(parts[start])
-    row_sum[...] = jnp.zeros_like(row_sum)
-    col_sum[...] = jnp.zeros_like(col_sum)
+    places, pairs = take(refs, 2)
+    sources, parts = take(refs, pieces), take(refs, outputs)
+    inputs, sums = refs
+    slots, _, side = pairs.shape
+    vectors = sums.shape[1]
+    start = 0
+    for source in sources:
+        high, low = split(source[...])
+        inputs[start:start + source.shape[0]] = jnp.concatenate([high, low], axis=1)
+        start += source.shape[0]
+    inputs[start] = jnp.zeros_like(inputs[start])
+    sums[...] = jnp.zeros_like(sums)
 
     def step(chunk, carry):
         results = []
@@ -105,54 +103,44 @@
             slot = chunk * CHUNK + offset
             place = places[slot]
             row, col = place // 128, place % 128
-            pair = tiles[slot]
-            from_cols = col_split[col]
-            from_rows = row_split[row]
-            first = lax.dot_general(
-                jnp.concatenate([from_cols, from_cols], axis=1),
-                jnp.concatenate([pair[:side], pair[side:]], axis=1),
-                (((1,), (1,)), ((), ())), preferred_element_type=jnp.float32,
+            pair = pairs[slot]
+            if flipped:
+                value, target, contract = inputs[row], col, 0
+            else:
+                value, target, contract = inputs[col], row, 1
+                pair = jnp.concatenate([pair[:side], pair[side:]], axis=1)
+            result = lax.dot_general(
+                jnp.concatenate([value, value], axis=1), pair,
+                (((1,), (contract,)), ((), ())), preferred_element_type=jnp.float32,
             )
-            second = lax.dot_general(
-                jnp.concatenate([from_rows, from_rows], axis=1),
-                pair,
-                (((1,), (0,)), ((), ())), preferred_element_type=jnp.float32,
-            )
-            results.append((row, col, first[:vectors] + first[vectors:], second[:vectors] + second[vectors:]))
-        for row, col, first, second in results:
-            row_sum[row] += first
-            col_sum[col] += second
+            results.append((target, result[:vectors] + result[vectors:]))
+        for target, result in results:
+            sums[target] += result
         return carry
 
     lax.fori_loop(0, slots // CHUNK, step, 0)
-    for parts, total in ((row_parts, row_sum), (col_parts, col_sum)):
-        start = 0
-        for part in parts:
-            part[...] = total[start:start + part.shape[0]]
-            start += part.shape[0]
-
-
-def multiply(places, tiles, row_inputs, col_inputs):
-    slots, _, side = tiles.shape
-    pieces = len(row_inputs), len(col_inputs)
-    blocks = sum(part.shape[0] for part in row_inputs)
-    vectors = row_inputs[0].shape[1]
-    parts = [jax.ShapeDtypeStruct(part.shape, jnp.float32) for part in [*row_inputs, *col_inputs]]
-    results = pl.pallas_call(
-        functools.partial(tile_kernel, *pieces),
-        out_shape=parts,
-        in_specs=[SMEM] + [VMEM] * (1 + len(parts)),
-        out_specs=[VMEM] * len(parts),
+    start = 0
+    for part in parts:
+        part[...] = sums[start:start + part.shape[0]]
+        start += part.shape[0]
+
+
+def product(flipped, places, pairs, sources, sizes):
+    slots, _, side = pairs.shape
+    blocks = sum(source.shape[0] for source in sources)
+    vectors = sources[0].shape[1]
+    return pl.pallas_call(
+        functools.partial(product_kernel, flipped, len(sources), len(sizes)),
+        out_shape=[jax.ShapeDtypeStruct((size, vectors, side), jnp.float32) for size in sizes],
+        in_specs=[SMEM] + [VMEM] * (1 + len(sources)),
+        out_specs=[VMEM] * len(sizes),
         scratch_shapes=[
             pltpu.VMEM((blocks + 8, 2 * vectors, side), jnp.bfloat16),
-            pltpu.VMEM((blocks + 8, 2 * vectors, side), jnp.bfloat16),
-            pltpu.VMEM((blocks + 8, vectors, side), jnp.float32),
-            pltpu.VMEM((blocks + 8, vectors, side), jnp.float32),
+            pltpu.VMEM((sum(sizes) + 8, vectors, side), jnp.float32),
         ],
         compiler_params=pltpu.CompilerParams(vmem_limit_bytes=TLIM * 1024 * 1024),
         cost_estimate=pl.CostEstimate(flops=FLOPS, bytes_accessed=4 * slots * side * side, transcendentals=0),
-    )(places, tiles, *row_inputs, *col_inputs)
-    return results[:pieces[0]], results[pieces[0]:]
+    )(places, pairs, *sources)
 
 
 def fetch_kernel(value, out):
@@ -200,7 +188,7 @@
         start += out.shape[0]
 
 
-def fold(parts, pieces):
+def fold(parts, pieces, cost=JOIN):
     size, *rest = parts[0].shape
     out = jax.ShapeDtypeStruct((size // pieces, *rest), parts[0].dtype)
     return pl.pallas_call(
@@ -209,7 +197,7 @@
         in_specs=[VMEM] * len(parts),
         out_specs=[VMEM] * pieces,
         compiler_params=pltpu.CompilerParams(vmem_limit_bytes=4 * 1024 * 1024),
-        cost_estimate=pl.CostEstimate(flops=JOIN, bytes_accessed=1024, transcendentals=0),
+        cost_estimate=pl.CostEstimate(flops=cost, bytes_accessed=1024, transcendentals=0),
     )(*parts)
 
 
@@ -248,13 +236,17 @@
     half = join([quad, swap(quad, "row", 13)], ROW_JOIN)
     col_inputs = [half, swap(half, "row", 1)]
 
-    row_parts, col_parts = multiply(places, pairs, row_inputs, col_inputs)
-
-    close = fold([row_parts[0]] + [swap(row_parts[index], "col", 4 * index) for index in (2, 1, 3)], 2)
-    half = fold([col_parts[0], swap(col_parts[1], "row", 1)], 2)
-    quad = fold([half[0], swap(half[1], "row", 13)], 2)
+    quarter, half_size = close.shape[0], half.shape[0]
+    row_parts = product(False, places, pairs, col_inputs, [quarter] * RING)
+    later_places, _ = lax.optimization_barrier((places, row_parts[0]))
+    col_parts = product(True, later_places, pairs, row_inputs, [half_size] * 2)
+
+    across = fold([row_parts[0], swap(row_parts[2], "col", 8)], 1)
+    close = fold([across[0], swap(row_parts[1], "col", 4), swap(row_parts[3], "col", 12)], 2)
+    half = fold([col_parts[0], swap(col_parts[1], "row", 1)], 2, ROW_FOLD)
+    quad = fold([half[0], swap(half[1], "row", 13)], 2, ROW_FOLD)
     couple = fold([close[0], swap(close[1], "col", 3)], 2)
-    pair = fold([quad[0], swap(quad[1], "row", 5)], 2)
+    pair = fold([quad[0], swap(quad[1], "row", 5)], 2, ROW_FOLD)
     terms = [couple[0], swap(couple[1], "col", 1), pair[0], swap(pair[1], "row", 3)]
     total = functools.reduce(jnp.add, terms)
     return total.transpose(1, 0, 2).reshape(vector_count, width)

time: 48.5 us -> 46.8 us (0.965)
  waiting for transfers between devices: 5.83 us -> 4.33 us
  starting transfers between devices: 33.9 us -> 33.2 us
    ppermute x18, waiting for transfers between devices: 5.83 us -> 4.33 us  [swap(): lax.ppermute(value, axis, [(j, j ^ offset) for j in range(lax.axis_size(a...]
    ppermute x18, starting transfers between devices: 33.9 us -> 33.2 us  [swap(): lax.ppermute(value, axis, [(j, j ^ offset) for j in range(lax.axis_size(a...]
    pallas_call x1 -> x2, Pallas kernels: 4.77 us -> 5.08 us  [product(): pl.pallas_call(functools.partial(product_kernel, flipped, len(sources), l...]
  transfers between devices with their start and end apart: 18 -> 18, of which waited for: 5 -> 4; matrix products, arithmetic and copies ran while one was open for 0% -> 0% of each run, Pallas kernels for 3% -> 15%
where the time goes in v5:
time: 46.8 us; the launch traced here: 46.4 us
  starting transfers between devices  33.2 us (71%)
  Pallas kernels  6.73 us (14%)
  waiting for transfers between devices  4.33 us (9%)
  between operations  0.79 us (2%)
  local copies, waits for them, and re-layouts  0.77 us (2%)
  other arithmetic  0.64 us (1%)
    ppermute x18, starting transfers between devices, swap(): lax.ppermute(value, axis, [(j, j ^ offset) for j in range(lax.axis_size(a...  33.2 us
    pallas_call x2, Pallas kernels, product(): pl.pallas_call(functools.partial(product_kernel, flipped, len(sources), l...  5.08 us
    ppermute x18, waiting for transfers between devices, swap(): lax.ppermute(value, axis, [(j, j ^ offset) for j in range(lax.axis_size(a...  4.33 us
    pallas_call x1, Pallas kernels, split_tiles(): pl.pallas_call(split_tiles_kernel, out_shape=jax.ShapeDtypeStruct((slots,...  1.56 us
  transfers between devices with their start and end apart: 18, of which 4 were waited for; matrix products, arithmetic and copies ran while one was open for 0% of the time, Pallas kernels for 15%

profile of v5, /device:TPU:1, one launch (start us, length us, event | category | flops | bytes accessed | tf_op | source)
XLA Modules:
  0.0 46.4 jit_solution(13968783483358417815)
XLA Ops:
  0.0 0.0 copy-start.1
  0.0 0.0 copy-start.2
  0.0 3.0 %collective-permute-start.2 = (f32[4,8,128]{2,1,0:T(8,128)}, f32[4,8,128]{2,1,0:T(8,128)S(1)}, u32[]{:S(2)}, u32[]{:S(2)}) collective-permute-start(f32[4,8,128]{2,1,0:T(8,128)} %bitcast.39), channel_id=1, source_target_pairs={{0,48},{16,32},{32,16},{48,0},{64,112},{80,96},{96,80},{112,64},{1... | collective-permute-start | bytes 49160 | tf_op jit(solution)/shard_map/ppermute | solution.py:213
  3.0 3.0 %collective-permute-start = (f32[4,8,128]{2,1,0:T(8,128)}, f32[4,8,128]{2,1,0:T(8,128)S(1)}, u32[]{:S(2)}, u32[]{:S(2)}) collective-permute-start(f32[4,8,128]{2,1,0:T(8,128)} %bitcast.40), channel_id=1, source_target_pairs={{0,1},{1,0},{2,3},{3,2},{4,5},{5,4},{6,7},{7,6},{8,9},{9,8},{10,11... | collective-permute-start | bytes 49160 | tf_op jit(solution)/shard_map/ppermute | solution.py:213
  6.0 0.7 %copy-done = f32[8,512]{1,0:T(8,128)S(1)} copy-done((f32[8,512]{1,0:T(8,128)S(1)}, f32[8,512]{1,0:T(8,128)}, u32[]{:S(2)}) %copy-start) | copy-done | bytes 16408
  7.4 0.0 copy-done.1
  7.4 0.0 copy-done.2
  7.5 0.0 collective-permute-done.2.refs_1_
  7.5 1.3 %collective-permute-start.3 = (f32[8,8,128]{2,1,0:T(8,128)S(1)}, f32[8,8,128]{2,1,0:T(8,128)S(1)}, u32[]{:S(2)}, u32[]{:S(2)}) collective-permute-start(f32[8,8,128]{2,1,0:T(8,128)S(1)} %shard_map.59.refs_0_), channel_id=1, source_target_pairs={{0,80},{16,64},{32,112},{48,96},{64,16},{80,0},{96,48},{112,32},{1... | collective-permute-start | bytes 98312 | tf_op jit(solution)/shard_map/ppermute | solution.py:213
  8.8 0.0 collective-permute-done.refs_1_
  8.8 3.4 %collective-permute-start.1 = (f32[8,8,128]{2,1,0:T(8,128)S(1)}, f32[8,8,128]{2,1,0:T(8,128)S(1)}, u32[]{:S(2)}, u32[]{:S(2)}) collective-permute-start(f32[8,8,128]{2,1,0:T(8,128)S(1)} %shard_map.56.refs_0_), channel_id=1, source_target_pairs={{0,3},{1,2},{2,1},{3,0},{4,7},{5,6},{6,5},{7,4},{8,11},{9,10},{10,... | collective-permute-start | bytes 98312 | tf_op jit(solution)/shard_map/ppermute | solution.py:213
  12.2 0.0 collective-permute-done.3.refs_1_
  12.2 3.4 %collective-permute-start.4 = (f32[16,8,128]{2,1,0:T(8,128)S(1)}, f32[16,8,128]{2,1,0:T(8,128)S(1)}, u32[]{:S(2)}, u32[]{:S(2)}) collective-permute-start(f32[16,8,128]{2,1,0:T(8,128)S(1)} %shard_map.60.refs_0_), channel_id=1, source_target_pairs={{0,208},{16,192},{32,240},{48,224},{64,144},{80,128},{96,176},{112... | collective-permute-start | bytes 196616 | tf_op jit(solution)/shard_map/ppermute | solution.py:213
  15.6 0.0 collective-permute-done.1.refs_1_
  15.6 0.0 slice-start.1
  15.6 1.4 %collective-permute-start.11 = (f32[16,8,128]{2,1,0:T(8,128)S(1)}, f32[16,8,128]{2,1,0:T(8,128)S(1)}, u32[]{:S(2)}, u32[]{:S(2)}) collective-permute-start(f32[16,8,128]{2,1,0:T(8,128)S(1)} %shard_map.57.refs_2_), channel_id=1, source_target_pairs={{0,4},{1,5},{2,6},{3,7},{4,0},{5,1},{6,2},{7,3},{8,12},{9,13},{10,... | collective-permute-start | bytes 196616 | tf_op jit(solution)/shard_map/ppermute | solution.py:213
  17.0 2.6 %collective-permute-start.12 = (f32[16,8,128]{2,1,0:T(8,128)S(1)}, f32[16,8,128]{2,1,0:T(8,128)S(1)}, u32[]{:S(2)}, u32[]{:S(2)}) collective-permute-start(f32[16,8,128]{2,1,0:T(8,128)S(1)} %shard_map.57.refs_2_), channel_id=1, source_target_pairs={{0,8},{1,9},{2,10},{3,11},{4,12},{5,13},{6,14},{7,15},{8,0},{9,1},... | collective-permute-start | bytes 196616 | tf_op jit(solution)/shard_map/ppermute | solution.py:213
  19.6 0.0 collective-permute-start.13
  19.6 0.0 collective-permute-done.4.refs_1_
  19.6 0.5 %collective-permute-start.5 = (f32[32,8,128]{2,1,0:T(8,128)S(1)}, f32[32,8,128]{2,1,0:T(8,128)S(1)}, u32[]{:S(2)}, u32[]{:S(2)}) collective-permute-start(f32[32,8,128]{2,1,0:T(8,128)S(1)} %shard_map.61.refs_2_), channel_id=1, source_target_pairs={{0,16},{16,0},{32,48},{48,32},{64,80},{80,64},{96,112},{112,96},{1... | collective-permute-start | bytes 393224 | tf_op jit(solution)/shard_map/ppermute | solution.py:213
  20.2 0.0 slice-done
  20.2 0.0 slice-done.1
  20.2 1.6 %shard_map.58.refs_1_ = bf16[128,256,128]{2,1,0:T(8,128)(2,1)S(1)} custom-call(f32[128,128,128]{2,1,0:T(8,128)S(1)} %bitcast.38), custom_call_target="tpu_custom_call" | custom-call | flops 30000001024 | bytes 16777216 | tf_op jit(solution)/shard_map/pallas_call | solution.py:65
  21.8 0.0 collective-permute-done.5.refs_3_
  21.8 3.0 %shard_map.62 = (f32[16,8,128]{2,1,0:T(8,128)S(1)}, f32[16,8,128]{2,1,0:T(8,128)S(1)}, f32[16,8,128]{2,1,0:T(8,128)S(1)}, f32[16,8,128]{2,1,0:T(8,128)S(1)}) custom-call(s32[128]{0:T(128)S(1)} %compare_select_fusion.refs_0_, bf16[128,256,128]{2,1,0:T(8,128)(2,1)S(1)} %shard_map.58.refs_1_, f32[32,8,128]{2,1,0:T(8,128)S(1)} %shard_map.61.refs_2_, ...), custom_call_target="tpu_custom_call" | custom-call | flops 20000000000 | bytes 8388608 | tf_op jit(solution)/shard_map/pallas_call | solution.py:132
  24.8 1.9 %collective-permute-start.6 = (f32[16,8,128]{2,1,0:T(8,128)S(1)}, f32[16,8,128]{2,1,0:T(8,128)S(1)}, u32[]{:S(2)}, u32[]{:S(2)}) collective-permute-start(f32[16,8,128]{2,1,0:T(8,128)S(1)} %get-tuple-element.26), channel_id=1, source_target_pairs={{0,8},{1,9},{2,10},{3,11},{4,12},{5,13},{6,14},{7,15},{8,0},{9,1},... | collective-permute-start | bytes 196616 | tf_op jit(solution)/shard_map/ppermute | solution.py:213
  26.7 1.5 %collective-permute-start.7 = (f32[16,8,128]{2,1,0:T(8,128)S(1)}, f32[16,8,128]{2,1,0:T(8,128)S(1)}, u32[]{:S(2)}, u32[]{:S(2)}) collective-permute-start(f32[16,8,128]{2,1,0:T(8,128)S(1)} %get-tuple-element.27), channel_id=1, source_target_pairs={{0,4},{1,5},{2,6},{3,7},{4,0},{5,1},{6,2},{7,3},{8,12},{9,13},{10,... | collective-permute-start | bytes 196616 | tf_op jit(solution)/shard_map/ppermute | solution.py:213
  28.2 0.0 collective-permute-done.11.refs_3_
  28.2 0.0 collective-permute-start.8
  28.2 0.0 collective-permute-done.12.refs_4_
  28.2 0.0 collective-permute-done.13.refs_5_
  28.2 2.1 %shard_map.66 = (f32[32,8,128]{2,1,0:T(8,128)S(1)}, f32[32,8,128]{2,1,0:T(8,128)S(1)}) custom-call(s32[128]{0:T(128)S(1)} %compare_select_fusion.refs_0_, bf16[128,256,128]{2,1,0:T(8,128)(2,1)S(1)} %shard_map.58.refs_1_, f32[16,8,128]{2,1,0:T(8,128)S(1)} %shard_map.57.refs_2_, f32[16,8,128]{2,1,0:T(8,128)S(1)} %collective-permute-done.11.refs_3_, ...), custom_call_target="tpu_custom_call" | custom-call | flops 20000000000 | bytes 8388608 | tf_op jit(solution)/shard_map/pallas_call | solution.py:132
  30.3 0.9 %collective-permute-start.14 = (f32[32,8,128]{2,1,0:T(8,128)S(1)}, f32[32,8,128]{2,1,0:T(8,128)S(1)}, u32[]{:S(2)}, u32[]{:S(2)}) collective-permute-start(f32[32,8,128]{2,1,0:T(8,128)S(1)} %get-tuple-element.36), channel_id=1, source_target_pairs={{0,16},{16,0},{32,48},{48,32},{64,80},{80,64},{96,112},{112,96},{1... | collective-permute-start | bytes 393224 | tf_op jit(solution)/shard_map/ppermute | solution.py:213
  31.2 0.0 collective-permute-done.6.refs_1_
  31.2 1.0 %collective-permute-done.14.refs_1_ = f32[32,8,128]{2,1,0:T(8,128)S(1)} collective-permute-done((f32[32,8,128]{2,1,0:T(8,128)S(1)}, f32[32,8,128]{2,1,0:T(8,128)S(1)}, u32[]{:S(2)}, u32[]{:S(2)}) %collective-permute-start.14) | collective-permute-done | bytes 131104 | tf_op jit(solution)/shard_map/ppermute | solution.py:213
  32.2 2.3 %collective-permute-start.15 = (f32[16,8,128]{2,1,0:T(8,128)S(1)}, f32[16,8,128]{2,1,0:T(8,128)S(1)}, u32[]{:S(2)}, u32[]{:S(2)}) collective-permute-start(f32[16,8,128]{2,1,0:T(8,128)S(1)} %get-tuple-element.38), channel_id=1, source_target_pairs={{0,208},{16,192},{32,240},{48,224},{64,144},{80,128},{96,176},{112... | collective-permute-start | bytes 196616 | tf_op jit(solution)/shard_map/ppermute | solution.py:213
  34.5 0.0 collective-permute-done.7.refs_1_
  34.5 0.0 collective-permute-done.8.refs_2_
  34.6 4.0 %collective-permute-start.9 = (f32[8,8,128]{2,1,0:T(8,128)S(1)}, f32[8,8,128]{2,1,0:T(8,128)S(1)}, u32[]{:S(2)}, u32[]{:S(2)}) collective-permute-start(f32[8,8,128]{2,1,0:T(8,128)S(1)} %get-tuple-element.30), channel_id=1, source_target_pairs={{0,3},{1,2},{2,1},{3,0},{4,7},{5,6},{6,5},{7,4},{8,11},{9,10},{10,... | collective-permute-start | bytes 98312 | tf_op jit(solution)/shard_map/ppermute | solution.py:213
  38.6 0.0 collective-permute-done.15.refs_1_
  38.6 0.9 %collective-permute-start.16 = (f32[8,8,128]{2,1,0:T(8,128)S(1)}, f32[8,8,128]{2,1,0:T(8,128)S(1)}, u32[]{:S(2)}, u32[]{:S(2)}) collective-permute-start(f32[8,8,128]{2,1,0:T(8,128)S(1)} %get-tuple-element.40), channel_id=1, source_target_pairs={{0,80},{16,64},{32,112},{48,96},{64,16},{80,0},{96,48},{112,32},{1... | collective-permute-start | bytes 98312 | tf_op jit(solution)/shard_map/ppermute | solution.py:213
  39.4 0.7 %collective-permute-done.9.refs_1_ = f32[8,8,128]{2,1,0:T(8,128)S(1)} collective-permute-done((f32[8,8,128]{2,1,0:T(8,128)S(1)}, f32[8,8,128]{2,1,0:T(8,128)S(1)}, u32[]{:S(2)}, u32[]{:S(2)}) %collective-permute-start.9) | collective-permute-done | bytes 32800 | tf_op jit(solution)/shard_map/ppermute | solution.py:213
  40.2 2.4 %collective-permute-start.10 = (f32[4,8,128]{2,1,0:T(8,128)S(1)}, f32[4,8,128]{2,1,0:T(8,128)S(1)}, u32[]{:S(2)}, u32[]{:S(2)}) collective-permute-start(f32[4,8,128]{2,1,0:T(8,128)S(1)} %get-tuple-element.32), channel_id=1, source_target_pairs={{0,1},{1,0},{2,3},{3,2},{4,5},{5,4},{6,7},{7,6},{8,9},{9,8},{10,11... | collective-permute-start | bytes 49160 | tf_op jit(solution)/shard_map/ppermute | solution.py:213
  42.5 0.0 collective-permute-done.16.refs_1_
  42.6 0.7 %collective-permute-start.17 = (f32[4,8,128]{2,1,0:T(8,128)S(1)}, f32[4,8,128]{2,1,0:T(8,128)S(1)}, u32[]{:S(2)}, u32[]{:S(2)}) collective-permute-start(f32[4,8,128]{2,1,0:T(8,128)S(1)} %get-tuple-element.42), channel_id=1, source_target_pairs={{0,48},{16,32},{32,16},{48,0},{64,112},{80,96},{96,80},{112,64},{1... | collective-permute-start | bytes 49160 | tf_op jit(solution)/shard_map/ppermute | solution.py:213
  43.2 0.6 %collective-permute-done.10 = f32[4,8,128]{2,1,0:T(8,128)S(1)} collective-permute-done((f32[4,8,128]{2,1,0:T(8,128)S(1)}, f32[4,8,128]{2,1,0:T(8,128)S(1)}, u32[]{:S(2)}, u32[]{:S(2)}) %collective-permute-start.10) | collective-permute-done | bytes 16416 | tf_op jit(solution)/shard_map/ppermute | solution.py:213
  43.8 2.0 %collective-permute-done.17 = f32[4,8,128]{2,1,0:T(8,128)S(1)} collective-permute-done((f32[4,8,128]{2,1,0:T(8,128)S(1)}, f32[4,8,128]{2,1,0:T(8,128)S(1)}, u32[]{:S(2)}, u32[]{:S(2)}) %collective-permute-start.17) | collective-permute-done | bytes 16416 | tf_op jit(solution)/shard_map/ppermute | solution.py:213
  45.8 0.6 %add_bitcast_fusion = f32[8,512]{1,0:T(8,128)} fusion(f32[4,8,128]{2,1,0:T(8,128)S(1)} %collective-permute-done.17, f32[4,8,128]{2,1,0:T(8,128)S(1)} %get-tuple-element.41, f32[4,8,128]{2,1,0:T(8,128)S(1)} %get-tuple-element.31, f32[4,8,128]{2,1,0:T(8,128)S(1)} %collective-permute-done.10), kind=kLoop, calls=%fused_computation | loop fusion | flops 12288 | bytes 81920 | tf_op jit(solution)/shard_map/reshape | solution.py:252
  (16 shorter events, 0.1 us)
Async XLA Ops:
  0.0 7.4 %copy-start.1 = (s32[1,1,128]{2,1,0:T(1,128)S(1)}, s32[1,1,128]{2,1,0:T(1,128)}, u32[]{:S(2)}) copy-start(s32[1,1,128]{2,1,0:T(1,128)} %param.7) | copy-start | bytes 1540
  0.0 7.4 %copy-start.2 = (s32[1,1,128]{2,1,0:T(1,128)S(1)}, s32[1,1,128]{2,1,0:T(1,128)}, u32[]{:S(2)}) copy-start(s32[1,1,128]{2,1,0:T(1,128)} %param.6) | copy-start | bytes 1540
  0.0 7.5 %collective-permute-start.2 = (f32[4,8,128]{2,1,0:T(8,128)}, f32[4,8,128]{2,1,0:T(8,128)S(1)}, u32[]{:S(2)}, u32[]{:S(2)}) collective-permute-start(f32[4,8,128]{2,1,0:T(8,128)} %bitcast.39), channel_id=1, source_target_pairs={{0,48},{16,32},{32,16},{48,0},{64,112},{80,96},{96,80},{112,64},{1... | collective-permute-start | bytes 49160 | tf_op jit(solution)/shard_map/ppermute | solution.py:213
  3.0 5.8 %collective-permute-start = (f32[4,8,128]{2,1,0:T(8,128)}, f32[4,8,128]{2,1,0:T(8,128)S(1)}, u32[]{:S(2)}, u32[]{:S(2)}) collective-permute-start(f32[4,8,128]{2,1,0:T(8,128)} %bitcast.40), channel_id=1, source_target_pairs={{0,1},{1,0},{2,3},{3,2},{4,5},{5,4},{6,7},{7,6},{8,9},{9,8},{10,11... | collective-permute-start | bytes 49160 | tf_op jit(solution)/shard_map/ppermute | solution.py:213
  6.0 0.8 %copy-start = (f32[8,512]{1,0:T(8,128)S(1)}, f32[8,512]{1,0:T(8,128)}, u32[]{:S(2)}) copy-start(f32[8,512]{1,0:T(8,128)} %param.9) | copy-start | bytes 49156
  7.5 4.7 %collective-permute-start.3 = (f32[8,8,128]{2,1,0:T(8,128)S(1)}, f32[8,8,128]{2,1,0:T(8,128)S(1)}, u32[]{:S(2)}, u32[]{:S(2)}) collective-permute-start(f32[8,8,128]{2,1,0:T(8,128)S(1)} %shard_map.59.refs_0_), channel_id=1, source_target_pairs={{0,80},{16,64},{32,112},{48,96},{64,16},{80,0},{96,48},{112,32},{1... | collective-permute-start | bytes 98312 | tf_op jit(solution)/shard_map/ppermute | solution.py:213
  8.8 6.8 %collective-permute-start.1 = (f32[8,8,128]{2,1,0:T(8,128)S(1)}, f32[8,8,128]{2,1,0:T(8,128)S(1)}, u32[]{:S(2)}, u32[]{:S(2)}) collective-permute-start(f32[8,8,128]{2,1,0:T(8,128)S(1)} %shard_map.56.refs_0_), channel_id=1, source_target_pairs={{0,3},{1,2},{2,1},{3,0},{4,7},{5,6},{6,5},{7,4},{8,11},{9,10},{10,... | collective-permute-start | bytes 98312 | tf_op jit(solution)/shard_map/ppermute | solution.py:213
  12.2 7.4 %collective-permute-start.4 = (f32[16,8,128]{2,1,0:T(8,128)S(1)}, f32[16,8,128]{2,1,0:T(8,128)S(1)}, u32[]{:S(2)}, u32[]{:S(2)}) collective-permute-start(f32[16,8,128]{2,1,0:T(8,128)S(1)} %shard_map.60.refs_0_), channel_id=1, source_target_pairs={{0,208},{16,192},{32,240},{48,224},{64,144},{80,128},{96,176},{112... | collective-permute-start | bytes 196616 | tf_op jit(solution)/shard_map/ppermute | solution.py:213
  15.6 4.6 %slice-start = ((s8[8388608]{0:T(1024)(128)(4,1)}), s8[4194304]{0:T(1024)(128)(4,1)S(1)}, s32[]{:S(2)}) async-start(s8[8388608]{0:T(1024)(128)(4,1)} %bitcast.36), calls=%async_computation | async-start | bytes 8388608
  15.6 4.6 %slice-start.1 = ((s8[8388608]{0:T(1024)(128)(4,1)}), s8[4194304]{0:T(1024)(128)(4,1)S(1)}, s32[]{:S(2)}) async-start(s8[8388608]{0:T(1024)(128)(4,1)} %bitcast.36), calls=%async_computation.1 | async-start | bytes 8388608
  15.6 12.6 %collective-permute-start.11 = (f32[16,8,128]{2,1,0:T(8,128)S(1)}, f32[16,8,128]{2,1,0:T(8,128)S(1)}, u32[]{:S(2)}, u32[]{:S(2)}) collective-permute-start(f32[16,8,128]{2,1,0:T(8,128)S(1)} %shard_map.57.refs_2_), channel_id=1, source_target_pairs={{0,4},{1,5},{2,6},{3,7},{4,0},{5,1},{6,2},{7,3},{8,12},{9,13},{10,... | collective-permute-start | bytes 196616 | tf_op jit(solution)/shard_map/ppermute | solution.py:213
  17.0 11.2 %collective-permute-start.12 = (f32[16,8,128]{2,1,0:T(8,128)S(1)}, f32[16,8,128]{2,1,0:T(8,128)S(1)}, u32[]{:S(2)}, u32[]{:S(2)}) collective-permute-start(f32[16,8,128]{2,1,0:T(8,128)S(1)} %shard_map.57.refs_2_), channel_id=1, source_target_pairs={{0,8},{1,9},{2,10},{3,11},{4,12},{5,13},{6,14},{7,15},{8,0},{9,1},... | collective-permute-start | bytes 196616 | tf_op jit(solution)/shard_map/ppermute | solution.py:213
  19.6 8.6 %collective-permute-start.13 = (f32[16,8,128]{2,1,0:T(8,128)S(1)}, f32[16,8,128]{2,1,0:T(8,128)S(1)}, u32[]{:S(2)}, u32[]{:S(2)}) collective-permute-start(f32[16,8,128]{2,1,0:T(8,128)S(1)} %shard_map.57.refs_2_), channel_id=1, source_target_pairs={{0,12},{1,13},{2,14},{3,15},{4,8},{5,9},{6,10},{7,11},{8,4},{9,5},... | collective-permute-start | bytes 196616 | tf_op jit(solution)/shard_map/ppermute | solution.py:213
  19.6 2.1 %collective-permute-start.5 = (f32[32,8,128]{2,1,0:T(8,128)S(1)}, f32[32,8,128]{2,1,0:T(8,128)S(1)}, u32[]{:S(2)}, u32[]{:S(2)}) collective-permute-start(f32[32,8,128]{2,1,0:T(8,128)S(1)} %shard_map.61.refs_2_), channel_id=1, source_target_pairs={{0,16},{16,0},{32,48},{48,32},{64,80},{80,64},{96,112},{112,96},{1... | collective-permute-start | bytes 393224 | tf_op jit(solution)/shard_map/ppermute | solution.py:213
  24.8 6.4 %collective-permute-start.6 = (f32[16,8,128]{2,1,0:T(8,128)S(1)}, f32[16,8,128]{2,1,0:T(8,128)S(1)}, u32[]{:S(2)}, u32[]{:S(2)}) collective-permute-start(f32[16,8,128]{2,1,0:T(8,128)S(1)} %get-tuple-element.26), channel_id=1, source_target_pairs={{0,8},{1,9},{2,10},{3,11},{4,12},{5,13},{6,14},{7,15},{8,0},{9,1},... | collective-permute-start | bytes 196616 | tf_op jit(solution)/shard_map/ppermute | solution.py:213
  26.7 7.9 %collective-permute-start.7 = (f32[16,8,128]{2,1,0:T(8,128)S(1)}, f32[16,8,128]{2,1,0:T(8,128)S(1)}, u32[]{:S(2)}, u32[]{:S(2)}) collective-permute-start(f32[16,8,128]{2,1,0:T(8,128)S(1)} %get-tuple-element.27), channel_id=1, source_target_pairs={{0,4},{1,5},{2,6},{3,7},{4,0},{5,1},{6,2},{7,3},{8,12},{9,13},{10,... | collective-permute-start | bytes 196616 | tf_op jit(solution)/shard_map/ppermute | solution.py:213
  28.2 6.4 %collective-permute-start.8 = (f32[16,8,128]{2,1,0:T(8,128)S(1)}, f32[16,8,128]{2,1,0:T(8,128)S(1)}, u32[]{:S(2)}, u32[]{:S(2)}) collective-permute-start(f32[16,8,128]{2,1,0:T(8,128)S(1)} %get-tuple-element.28), channel_id=1, source_target_pairs={{0,12},{1,13},{2,14},{3,15},{4,8},{5,9},{6,10},{7,11},{8,4},{9,5},... | collective-permute-start | bytes 196616 | tf_op jit(solution)/shard_map/ppermute | solution.py:213
  30.3 1.9 %collective-permute-start.14 = (f32[32,8,128]{2,1,0:T(8,128)S(1)}, f32[32,8,128]{2,1,0:T(8,128)S(1)}, u32[]{:S(2)}, u32[]{:S(2)}) collective-permute-start(f32[32,8,128]{2,1,0:T(8,128)S(1)} %get-tuple-element.36), channel_id=1, source_target_pairs={{0,16},{16,0},{32,48},{48,32},{64,80},{80,64},{96,112},{112,96},{1... | collective-permute-start | bytes 393224 | tf_op jit(solution)/shard_map/ppermute | solution.py:213
  32.2 6.4 %collective-permute-start.15 = (f32[16,8,128]{2,1,0:T(8,128)S(1)}, f32[16,8,128]{2,1,0:T(8,128)S(1)}, u32[]{:S(2)}, u32[]{:S(2)}) collective-permute-start(f32[16,8,128]{2,1,0:T(8,128)S(1)} %get-tuple-element.38), channel_id=1, source_target_pairs={{0,208},{16,192},{32,240},{48,224},{64,144},{80,128},{96,176},{112... | collective-permute-start | bytes 196616 | tf_op jit(solution)/shard_map/ppermute | solution.py:213
  34.6 5.6 %collective-permute-start.9 = (f32[8,8,128]{2,1,0:T(8,128)S(1)}, f32[8,8,128]{2,1,0:T(8,128)S(1)}, u32[]{:S(2)}, u32[]{:S(2)}) collective-permute-start(f32[8,8,128]{2,1,0:T(8,128)S(1)} %get-tuple-element.30), channel_id=1, source_target_pairs={{0,3},{1,2},{2,1},{3,0},{4,7},{5,6},{6,5},{7,4},{8,11},{9,10},{10,... | collective-permute-start | bytes 98312 | tf_op jit(solution)/shard_map/ppermute | solution.py:213
  38.6 4.0 %collective-permute-start.16 = (f32[8,8,128]{2,1,0:T(8,128)S(1)}, f32[8,8,128]{2,1,0:T(8,128)S(1)}, u32[]{:S(2)}, u32[]{:S(2)}) collective-permute-start(f32[8,8,128]{2,1,0:T(8,128)S(1)} %get-tuple-element.40), channel_id=1, source_target_pairs={{0,80},{16,64},{32,112},{48,96},{64,16},{80,0},{96,48},{112,32},{1... | collective-permute-start | bytes 98312 | tf_op jit(solution)/shard_map/ppermute | solution.py:213
  40.2 3.7 %collective-permute-start.10 = (f32[4,8,128]{2,1,0:T(8,128)S(1)}, f32[4,8,128]{2,1,0:T(8,128)S(1)}, u32[]{:S(2)}, u32[]{:S(2)}) collective-permute-start(f32[4,8,128]{2,1,0:T(8,128)S(1)} %get-tuple-element.32), channel_id=1, source_target_pairs={{0,1},{1,0},{2,3},{3,2},{4,5},{5,4},{6,7},{7,6},{8,9},{9,8},{10,11... | collective-permute-start | bytes 49160 | tf_op jit(solution)/shard_map/ppermute | solution.py:213
  42.6 3.3 %collective-permute-start.17 = (f32[4,8,128]{2,1,0:T(8,128)S(1)}, f32[4,8,128]{2,1,0:T(8,128)S(1)}, u32[]{:S(2)}, u32[]{:S(2)}) collective-permute-start(f32[4,8,128]{2,1,0:T(8,128)S(1)} %get-tuple-element.42), channel_id=1, source_target_pairs={{0,48},{16,32},{32,16},{48,0},{64,112},{80,96},{96,80},{112,64},{1... | collective-permute-start | bytes 49160 | tf_op jit(solution)/shard_map/ppermute | solution.py:213

commit v6 on v5

--- a/solution.py
+++ b/solution.py
@@ -14,8 +14,9 @@
 JOIN = 5 * 10 ** 10
 FETCH = True
 RING = 4
-PIECE = 16
-PREP_RING = 8
+PIECE = 8
+PREP_RING = 2
+HEAD = 16
 PLIM = 24
 PREP = 3 * 10 ** 10
 FETCH_COST = 10 ** 10
@@ -61,10 +62,10 @@
 
 
 def split_tiles(tiles):
-    slots, side, _ = tiles.shape
+    side = tiles.shape[1]
     return pl.pallas_call(
         split_tiles_kernel,
-        out_shape=jax.ShapeDtypeStruct((slots, 2 * side, side), jnp.bfloat16),
+        out_shape=jax.ShapeDtypeStruct((HEAD, 2 * side, side), jnp.bfloat16),
         in_specs=[ANY],
         out_specs=VMEM,
         scratch_shapes=[
@@ -72,7 +73,7 @@
             pltpu.SemaphoreType.DMA((PREP_RING,)),
         ],
         compiler_params=pltpu.CompilerParams(vmem_limit_bytes=PLIM * 1024 * 1024),
-        cost_estimate=pl.CostEstimate(flops=PREP, bytes_accessed=8 * slots * side * side, transcendentals=0),
+        cost_estimate=pl.CostEstimate(flops=PREP, bytes_accessed=1 << 24, transcendentals=0),
     )(tiles)
 
 
@@ -84,10 +85,10 @@
 
 def product_kernel(flipped, pieces, outputs, *refs):
     refs = list(refs)
-    places, pairs = take(refs, 2)
+    places, tiles, pairs = take(refs, 3)
     sources, parts = take(refs, pieces), take(refs, outputs)
     inputs, sums = refs
-    slots, _, side = pairs.shape
+    slots, side, _ = tiles.shape
     vectors = sums.shape[1]
     start = 0
     for source in sources:
@@ -103,12 +104,15 @@
             slot = chunk * CHUNK + offset
             place = places[slot]
             row, col = place // 128, place % 128
-            pair = pairs[slot]
+            if offset < HEAD:
+                high, low = pairs[slot, :side, :], pairs[slot, side:, :]
+            else:
+                high, low = split(tiles[slot])
             if flipped:
                 value, target, contract = inputs[row], col, 0
             else:
                 value, target, contract = inputs[col], row, 1
-                pair = jnp.concatenate([pair[:side], pair[side:]], axis=1)
+            pair = jnp.concatenate([high, low], axis=contract)
             result = lax.dot_general(
                 jnp.concatenate([value, value], axis=1), pair,
                 (((1,), (contract,)), ((), ())), preferred_element_type=jnp.float32,
@@ -125,14 +129,14 @@
         start += part.shape[0]
 
 
-def product(flipped, places, pairs, sources, sizes):
-    slots, _, side = pairs.shape
+def product(flipped, places, tiles, pairs, sources, sizes):
+    slots, side, _ = tiles.shape
     blocks = sum(source.shape[0] for source in sources)
     vectors = sources[0].shape[1]
     return pl.pallas_call(
         functools.partial(product_kernel, flipped, len(sources), len(sizes)),
         out_shape=[jax.ShapeDtypeStruct((size, vectors, side), jnp.float32) for size in sizes],
-        in_specs=[SMEM] + [VMEM] * (1 + len(sources)),
+        in_specs=[SMEM] + [VMEM] * (2 + len(sources)),
         out_specs=[VMEM] * len(sizes),
         scratch_shapes=[
             pltpu.VMEM((blocks + 8, 2 * vectors, side), jnp.bfloat16),
@@ -140,7 +144,7 @@
         ],
         compiler_params=pltpu.CompilerParams(vmem_limit_bytes=TLIM * 1024 * 1024),
         cost_estimate=pl.CostEstimate(flops=FLOPS, bytes_accessed=4 * slots * side * side, transcendentals=0),
-    )(places, pairs, *sources)
+    )(places, tiles, pairs, *sources)
 
 
 def fetch_kernel(value, out):
@@ -237,9 +241,9 @@
     col_inputs = [half, swap(half, "row", 1)]
 
     quarter, half_size = close.shape[0], half.shape[0]
-    row_parts = product(False, places, pairs, col_inputs, [quarter] * RING)
+    row_parts = product(False, places, blocks[0, 0], pairs, col_inputs, [quarter] * RING)
     later_places, _ = lax.optimization_barrier((places, row_parts[0]))
-    col_parts = product(True, later_places, pairs, row_inputs, [half_size] * 2)
+    col_parts = product(True, later_places, blocks[0, 0], pairs, row_inputs, [half_size] * 2)
 
     across = fold([row_parts[0], swap(row_parts[2], "col", 8)], 1)
     close = fold([across[0], swap(row_parts[1], "col", 4), swap(row_parts[3], "col", 12)], 2)

time: 46.8 us -> 46.7 us (level)
  Pallas kernels: 6.73 us -> 5.27 us
  waiting for transfers between devices: 4.33 us -> 5.44 us
    pallas_call x1, Pallas kernels: 1.56 us -> 0.22 us  [split_tiles(): pl.pallas_call(split_tiles_kernel, out_shape=jax.ShapeDtypeStruct((HEAD,...]
    ppermute x18, waiting for transfers between devices: 4.33 us -> 5.44 us  [swap(): lax.ppermute(value, axis, [(j, j ^ offset) for j in range(lax.axis_size(a...]
  transfers between devices with their start and end apart: 18 -> 18, of which waited for: 4 -> 5; matrix products, arithmetic and copies ran while one was open for 0% -> 0% of each run, Pallas kernels for 15% -> 11%
where the time goes in v6:
time: 46.7 us; the launch traced here: 46.5 us
  starting transfers between devices  33.6 us (72%)
  waiting for transfers between devices  5.44 us (12%)
  Pallas kernels  5.27 us (11%)
  between operations  0.78 us (2%)
  local copies, waits for them, and re-layouts  0.77 us (2%)
  other arithmetic  0.64 us (1%)
    ppermute x18, starting transfers between devices, swap(): lax.ppermute(value, axis, [(j, j ^ offset) for j in range(lax.axis_size(a...  33.6 us
    ppermute x18, waiting for transfers between devices, swap(): lax.ppermute(value, axis, [(j, j ^ offset) for j in range(lax.axis_size(a...  5.44 us
    pallas_call x2, Pallas kernels, product(): pl.pallas_call(functools.partial(product_kernel, flipped, len(sources), l...  4.97 us
  transfers between devices with their start and end apart: 18, of which 5 were waited for; matrix products, arithmetic and copies ran while one was open for 0% of the time, Pallas kernels for 11%

profile of v6, /device:TPU:1, one launch (start us, length us, event | category | flops | bytes accessed | tf_op | source)
XLA Modules:
  0.0 46.5 jit_solution(5892799209282616028)
XLA Ops:
  0.0 0.0 copy-start.1
  0.0 0.0 copy-start.2
  0.0 3.0 %collective-permute-start.2 = (f32[4,8,128]{2,1,0:T(8,128)}, f32[4,8,128]{2,1,0:T(8,128)S(1)}, u32[]{:S(2)}, u32[]{:S(2)}) collective-permute-start(f32[4,8,128]{2,1,0:T(8,128)} %bitcast.41), channel_id=1, source_target_pairs={{0,48},{16,32},{32,16},{48,0},{64,112},{80,96},{96,80},{112,64},{1... | collective-permute-start | bytes 49160 | tf_op jit(solution)/shard_map/ppermute | solution.py:217
  3.0 3.0 %collective-permute-start = (f32[4,8,128]{2,1,0:T(8,128)}, f32[4,8,128]{2,1,0:T(8,128)S(1)}, u32[]{:S(2)}, u32[]{:S(2)}) collective-permute-start(f32[4,8,128]{2,1,0:T(8,128)} %bitcast.42), channel_id=1, source_target_pairs={{0,1},{1,0},{2,3},{3,2},{4,5},{5,4},{6,7},{7,6},{8,9},{9,8},{10,11... | collective-permute-start | bytes 49160 | tf_op jit(solution)/shard_map/ppermute | solution.py:217
  6.0 0.7 %copy-done = f32[8,512]{1,0:T(8,128)S(1)} copy-done((f32[8,512]{1,0:T(8,128)S(1)}, f32[8,512]{1,0:T(8,128)}, u32[]{:S(2)}) %copy-start) | copy-done | bytes 16408
  7.4 0.0 copy-done.1
  7.4 0.0 copy-done.2
  7.5 0.0 collective-permute-done.2.refs_1_
  7.5 1.3 %collective-permute-start.3 = (f32[8,8,128]{2,1,0:T(8,128)S(1)}, f32[8,8,128]{2,1,0:T(8,128)S(1)}, u32[]{:S(2)}, u32[]{:S(2)}) collective-permute-start(f32[8,8,128]{2,1,0:T(8,128)S(1)} %shard_map.59.refs_0_), channel_id=1, source_target_pairs={{0,80},{16,64},{32,112},{48,96},{64,16},{80,0},{96,48},{112,32},{1... | collective-permute-start | bytes 98312 | tf_op jit(solution)/shard_map/ppermute | solution.py:217
  8.8 0.0 collective-permute-done.refs_1_
  8.8 3.4 %collective-permute-start.1 = (f32[8,8,128]{2,1,0:T(8,128)S(1)}, f32[8,8,128]{2,1,0:T(8,128)S(1)}, u32[]{:S(2)}, u32[]{:S(2)}) collective-permute-start(f32[8,8,128]{2,1,0:T(8,128)S(1)} %shard_map.56.refs_0_), channel_id=1, source_target_pairs={{0,3},{1,2},{2,1},{3,0},{4,7},{5,6},{6,5},{7,4},{8,11},{9,10},{10,... | collective-permute-start | bytes 98312 | tf_op jit(solution)/shard_map/ppermute | solution.py:217
  12.2 0.0 collective-permute-done.3.refs_1_
  12.2 3.4 %collective-permute-start.4 = (f32[16,8,128]{2,1,0:T(8,128)S(1)}, f32[16,8,128]{2,1,0:T(8,128)S(1)}, u32[]{:S(2)}, u32[]{:S(2)}) collective-permute-start(f32[16,8,128]{2,1,0:T(8,128)S(1)} %shard_map.60.refs_0_), channel_id=1, source_target_pairs={{0,208},{16,192},{32,240},{48,224},{64,144},{80,128},{96,176},{112... | collective-permute-start | bytes 196616 | tf_op jit(solution)/shard_map/ppermute | solution.py:217
  15.6 0.0 collective-permute-done.1.refs_1_
  15.6 0.0 slice-start.1
  15.6 1.4 %collective-permute-start.11 = (f32[16,8,128]{2,1,0:T(8,128)S(1)}, f32[16,8,128]{2,1,0:T(8,128)S(1)}, u32[]{:S(2)}, u32[]{:S(2)}) collective-permute-start(f32[16,8,128]{2,1,0:T(8,128)S(1)} %shard_map.57.refs_3_), channel_id=1, source_target_pairs={{0,4},{1,5},{2,6},{3,7},{4,0},{5,1},{6,2},{7,3},{8,12},{9,13},{10,... | collective-permute-start | bytes 196616 | tf_op jit(solution)/shard_map/ppermute | solution.py:217
  17.0 2.6 %collective-permute-start.12 = (f32[16,8,128]{2,1,0:T(8,128)S(1)}, f32[16,8,128]{2,1,0:T(8,128)S(1)}, u32[]{:S(2)}, u32[]{:S(2)}) collective-permute-start(f32[16,8,128]{2,1,0:T(8,128)S(1)} %shard_map.57.refs_3_), channel_id=1, source_target_pairs={{0,8},{1,9},{2,10},{3,11},{4,12},{5,13},{6,14},{7,15},{8,0},{9,1},... | collective-permute-start | bytes 196616 | tf_op jit(solution)/shard_map/ppermute | solution.py:217
  19.6 0.0 collective-permute-start.13
  19.6 0.0 collective-permute-done.4.refs_1_
  19.6 0.5 %collective-permute-start.5 = (f32[32,8,128]{2,1,0:T(8,128)S(1)}, f32[32,8,128]{2,1,0:T(8,128)S(1)}, u32[]{:S(2)}, u32[]{:S(2)}) collective-permute-start(f32[32,8,128]{2,1,0:T(8,128)S(1)} %shard_map.61.refs_3_), channel_id=1, source_target_pairs={{0,16},{16,0},{32,48},{48,32},{64,80},{80,64},{96,112},{112,96},{1... | collective-permute-start | bytes 393224 | tf_op jit(solution)/shard_map/ppermute | solution.py:217
  20.2 0.0 slice-done
  20.2 0.0 slice-done.1
  20.2 0.2 shard_map.58.refs_2_
  20.4 0.8 %collective-permute-done.5.refs_4_ = f32[32,8,128]{2,1,0:T(8,128)S(1)} collective-permute-done((f32[32,8,128]{2,1,0:T(8,128)S(1)}, f32[32,8,128]{2,1,0:T(8,128)S(1)}, u32[]{:S(2)}, u32[]{:S(2)}) %collective-permute-start.5) | collective-permute-done | bytes 131104 | tf_op jit(solution)/shard_map/ppermute | solution.py:217
  21.2 3.0 %shard_map.62 = (f32[16,8,128]{2,1,0:T(8,128)S(1)}, f32[16,8,128]{2,1,0:T(8,128)S(1)}, f32[16,8,128]{2,1,0:T(8,128)S(1)}, f32[16,8,128]{2,1,0:T(8,128)S(1)}) custom-call(s32[128]{0:T(128)S(1)} %compare_select_fusion.refs_0_, f32[128,128,128]{2,1,0:T(8,128)S(1)} %bitcast.39, bf16[16,256,128]{2,1,0:T(8,128)(2,1)S(1)} %shard_map.58.refs_2_, ...), custom_call_target="tpu_custom_call" | custom-call | flops 20000000000 | bytes 8388608 | tf_op jit(solution)/shard_map/pallas_call | solution.py:136
  24.2 1.8 %collective-permute-start.6 = (f32[16,8,128]{2,1,0:T(8,128)S(1)}, f32[16,8,128]{2,1,0:T(8,128)S(1)}, u32[]{:S(2)}, u32[]{:S(2)}) collective-permute-start(f32[16,8,128]{2,1,0:T(8,128)S(1)} %get-tuple-element.26), channel_id=1, source_target_pairs={{0,8},{1,9},{2,10},{3,11},{4,12},{5,13},{6,14},{7,15},{8,0},{9,1},... | collective-permute-start | bytes 196616 | tf_op jit(solution)/shard_map/ppermute | solution.py:217
  26.0 1.6 %collective-permute-start.7 = (f32[16,8,128]{2,1,0:T(8,128)S(1)}, f32[16,8,128]{2,1,0:T(8,128)S(1)}, u32[]{:S(2)}, u32[]{:S(2)}) collective-permute-start(f32[16,8,128]{2,1,0:T(8,128)S(1)} %get-tuple-element.27), channel_id=1, source_target_pairs={{0,4},{1,5},{2,6},{3,7},{4,0},{5,1},{6,2},{7,3},{8,12},{9,13},{10,... | collective-permute-start | bytes 196616 | tf_op jit(solution)/shard_map/ppermute | solution.py:217
  27.6 0.0 collective-permute-done.11.refs_4_
  27.6 0.0 collective-permute-start.8
  27.6 0.0 collective-permute-done.12.refs_5_
  27.6 0.0 collective-permute-done.13.refs_6_
  27.6 1.9 %shard_map.66 = (f32[32,8,128]{2,1,0:T(8,128)S(1)}, f32[32,8,128]{2,1,0:T(8,128)S(1)}) custom-call(s32[128]{0:T(128)S(1)} %compare_select_fusion.refs_0_, f32[128,128,128]{2,1,0:T(8,128)S(1)} %bitcast.40, bf16[16,256,128]{2,1,0:T(8,128)(2,1)S(1)} %shard_map.58.refs_2_, f32[16,8,128]{2,1,0:T(8,128)S(1)} %shard_map.57.refs_3_, ...), custom_call_target="tpu_custom_call" | custom-call | flops 20000000000 | bytes 8388608 | tf_op jit(solution)/shard_map/pallas_call | solution.py:136
  29.6 1.2 %collective-permute-start.14 = (f32[32,8,128]{2,1,0:T(8,128)S(1)}, f32[32,8,128]{2,1,0:T(8,128)S(1)}, u32[]{:S(2)}, u32[]{:S(2)}) collective-permute-start(f32[32,8,128]{2,1,0:T(8,128)S(1)} %get-tuple-element.36), channel_id=1, source_target_pairs={{0,16},{16,0},{32,48},{48,32},{64,80},{80,64},{96,112},{112,96},{1... | collective-permute-start | bytes 393224 | tf_op jit(solution)/shard_map/ppermute | solution.py:217
  30.8 0.0 collective-permute-done.6.refs_1_
  30.8 1.0 %collective-permute-done.14.refs_1_ = f32[32,8,128]{2,1,0:T(8,128)S(1)} collective-permute-done((f32[32,8,128]{2,1,0:T(8,128)S(1)}, f32[32,8,128]{2,1,0:T(8,128)S(1)}, u32[]{:S(2)}, u32[]{:S(2)}) %collective-permute-start.14) | collective-permute-done | bytes 131104 | tf_op jit(solution)/shard_map/ppermute | solution.py:217
  31.8 2.4 %collective-permute-start.15 = (f32[16,8,128]{2,1,0:T(8,128)S(1)}, f32[16,8,128]{2,1,0:T(8,128)S(1)}, u32[]{:S(2)}, u32[]{:S(2)}) collective-permute-start(f32[16,8,128]{2,1,0:T(8,128)S(1)} %get-tuple-element.38), channel_id=1, source_target_pairs={{0,208},{16,192},{32,240},{48,224},{64,144},{80,128},{96,176},{112... | collective-permute-start | bytes 196616 | tf_op jit(solution)/shard_map/ppermute | solution.py:217
  34.2 0.0 collective-permute-done.7.refs_1_
  34.2 0.0 collective-permute-done.8.refs_2_
  34.2 3.9 %collective-permute-start.9 = (f32[8,8,128]{2,1,0:T(8,128)S(1)}, f32[8,8,128]{2,1,0:T(8,128)S(1)}, u32[]{:S(2)}, u32[]{:S(2)}) collective-permute-start(f32[8,8,128]{2,1,0:T(8,128)S(1)} %get-tuple-element.30), channel_id=1, source_target_pairs={{0,3},{1,2},{2,1},{3,0},{4,7},{5,6},{6,5},{7,4},{8,11},{9,10},{10,... | collective-permute-start | bytes 98312 | tf_op jit(solution)/shard_map/ppermute | solution.py:217
  38.2 0.0 collective-permute-done.15.refs_1_
  38.2 1.0 %collective-permute-start.16 = (f32[8,8,128]{2,1,0:T(8,128)S(1)}, f32[8,8,128]{2,1,0:T(8,128)S(1)}, u32[]{:S(2)}, u32[]{:S(2)}) collective-permute-start(f32[8,8,128]{2,1,0:T(8,128)S(1)} %get-tuple-element.40), channel_id=1, source_target_pairs={{0,80},{16,64},{32,112},{48,96},{64,16},{80,0},{96,48},{112,32},{1... | collective-permute-start | bytes 98312 | tf_op jit(solution)/shard_map/ppermute | solution.py:217
  39.2 0.6 %collective-permute-done.9.refs_1_ = f32[8,8,128]{2,1,0:T(8,128)S(1)} collective-permute-done((f32[8,8,128]{2,1,0:T(8,128)S(1)}, f32[8,8,128]{2,1,0:T(8,128)S(1)}, u32[]{:S(2)}, u32[]{:S(2)}) %collective-permute-start.9) | collective-permute-done | bytes 32800 | tf_op jit(solution)/shard_map/ppermute | solution.py:217
  39.8 2.5 %collective-permute-start.10 = (f32[4,8,128]{2,1,0:T(8,128)S(1)}, f32[4,8,128]{2,1,0:T(8,128)S(1)}, u32[]{:S(2)}, u32[]{:S(2)}) collective-permute-start(f32[4,8,128]{2,1,0:T(8,128)S(1)} %get-tuple-element.32), channel_id=1, source_target_pairs={{0,1},{1,0},{2,3},{3,2},{4,5},{5,4},{6,7},{7,6},{8,9},{9,8},{10,11... | collective-permute-start | bytes 49160 | tf_op jit(solution)/shard_map/ppermute | solution.py:217
  42.3 0.0 collective-permute-done.16.refs_1_
  42.3 0.5 %collective-permute-start.17 = (f32[4,8,128]{2,1,0:T(8,128)S(1)}, f32[4,8,128]{2,1,0:T(8,128)S(1)}, u32[]{:S(2)}, u32[]{:S(2)}) collective-permute-start(f32[4,8,128]{2,1,0:T(8,128)S(1)} %get-tuple-element.42), channel_id=1, source_target_pairs={{0,48},{16,32},{32,16},{48,0},{64,112},{80,96},{96,80},{112,64},{1... | collective-permute-start | bytes 49160 | tf_op jit(solution)/shard_map/ppermute | solution.py:217
  42.9 0.6 %collective-permute-done.10 = f32[4,8,128]{2,1,0:T(8,128)S(1)} collective-permute-done((f32[4,8,128]{2,1,0:T(8,128)S(1)}, f32[4,8,128]{2,1,0:T(8,128)S(1)}, u32[]{:S(2)}, u32[]{:S(2)}) %collective-permute-start.10) | collective-permute-done | bytes 16416 | tf_op jit(solution)/shard_map/ppermute | solution.py:217
  43.4 2.5 %collective-permute-done.17 = f32[4,8,128]{2,1,0:T(8,128)S(1)} collective-permute-done((f32[4,8,128]{2,1,0:T(8,128)S(1)}, f32[4,8,128]{2,1,0:T(8,128)S(1)}, u32[]{:S(2)}, u32[]{:S(2)}) %collective-permute-start.17) | collective-permute-done | bytes 16416 | tf_op jit(solution)/shard_map/ppermute | solution.py:217
  45.9 0.6 %add_bitcast_fusion = f32[8,512]{1,0:T(8,128)} fusion(f32[4,8,128]{2,1,0:T(8,128)S(1)} %collective-permute-done.17, f32[4,8,128]{2,1,0:T(8,128)S(1)} %get-tuple-element.41, f32[4,8,128]{2,1,0:T(8,128)S(1)} %get-tuple-element.31, f32[4,8,128]{2,1,0:T(8,128)S(1)} %collective-permute-done.10), kind=kLoop, calls=%fused_computation | loop fusion | flops 12288 | bytes 81920 | tf_op jit(solution)/shard_map/reshape | solution.py:256
  (16 shorter events, 0.1 us)
Async XLA Ops:
  0.0 7.4 %copy-start.1 = (s32[1,1,128]{2,1,0:T(1,128)S(1)}, s32[1,1,128]{2,1,0:T(1,128)}, u32[]{:S(2)}) copy-start(s32[1,1,128]{2,1,0:T(1,128)} %param.7) | copy-start | bytes 1540
  0.0 7.4 %copy-start.2 = (s32[1,1,128]{2,1,0:T(1,128)S(1)}, s32[1,1,128]{2,1,0:T(1,128)}, u32[]{:S(2)}) copy-start(s32[1,1,128]{2,1,0:T(1,128)} %param.6) | copy-start | bytes 1540
  0.0 7.5 %collective-permute-start.2 = (f32[4,8,128]{2,1,0:T(8,128)}, f32[4,8,128]{2,1,0:T(8,128)S(1)}, u32[]{:S(2)}, u32[]{:S(2)}) collective-permute-start(f32[4,8,128]{2,1,0:T(8,128)} %bitcast.41), channel_id=1, source_target_pairs={{0,48},{16,32},{32,16},{48,0},{64,112},{80,96},{96,80},{112,64},{1... | collective-permute-start | bytes 49160 | tf_op jit(solution)/shard_map/ppermute | solution.py:217
  3.0 5.8 %collective-permute-start = (f32[4,8,128]{2,1,0:T(8,128)}, f32[4,8,128]{2,1,0:T(8,128)S(1)}, u32[]{:S(2)}, u32[]{:S(2)}) collective-permute-start(f32[4,8,128]{2,1,0:T(8,128)} %bitcast.42), channel_id=1, source_target_pairs={{0,1},{1,0},{2,3},{3,2},{4,5},{5,4},{6,7},{7,6},{8,9},{9,8},{10,11... | collective-permute-start | bytes 49160 | tf_op jit(solution)/shard_map/ppermute | solution.py:217
  6.0 0.8 %copy-start = (f32[8,512]{1,0:T(8,128)S(1)}, f32[8,512]{1,0:T(8,128)}, u32[]{:S(2)}) copy-start(f32[8,512]{1,0:T(8,128)} %param.9) | copy-start | bytes 49156
  7.5 4.7 %collective-permute-start.3 = (f32[8,8,128]{2,1,0:T(8,128)S(1)}, f32[8,8,128]{2,1,0:T(8,128)S(1)}, u32[]{:S(2)}, u32[]{:S(2)}) collective-permute-start(f32[8,8,128]{2,1,0:T(8,128)S(1)} %shard_map.59.refs_0_), channel_id=1, source_target_pairs={{0,80},{16,64},{32,112},{48,96},{64,16},{80,0},{96,48},{112,32},{1... | collective-permute-start | bytes 98312 | tf_op jit(solution)/shard_map/ppermute | solution.py:217
  8.8 6.8 %collective-permute-start.1 = (f32[8,8,128]{2,1,0:T(8,128)S(1)}, f32[8,8,128]{2,1,0:T(8,128)S(1)}, u32[]{:S(2)}, u32[]{:S(2)}) collective-permute-start(f32[8,8,128]{2,1,0:T(8,128)S(1)} %shard_map.56.refs_0_), channel_id=1, source_target_pairs={{0,3},{1,2},{2,1},{3,0},{4,7},{5,6},{6,5},{7,4},{8,11},{9,10},{10,... | collective-permute-start | bytes 98312 | tf_op jit(solution)/shard_map/ppermute | solution.py:217
  12.2 7.4 %collective-permute-start.4 = (f32[16,8,128]{2,1,0:T(8,128)S(1)}, f32[16,8,128]{2,1,0:T(8,128)S(1)}, u32[]{:S(2)}, u32[]{:S(2)}) collective-permute-start(f32[16,8,128]{2,1,0:T(8,128)S(1)} %shard_map.60.refs_0_), channel_id=1, source_target_pairs={{0,208},{16,192},{32,240},{48,224},{64,144},{80,128},{96,176},{112... | collective-permute-start | bytes 196616 | tf_op jit(solution)/shard_map/ppermute | solution.py:217
  15.6 4.6 %slice-start = ((s8[8388608]{0:T(1024)(128)(4,1)}), s8[4194304]{0:T(1024)(128)(4,1)S(1)}, s32[]{:S(2)}) async-start(s8[8388608]{0:T(1024)(128)(4,1)} %bitcast.36), calls=%async_computation | async-start | bytes 8388608
  15.6 4.6 %slice-start.1 = ((s8[8388608]{0:T(1024)(128)(4,1)}), s8[4194304]{0:T(1024)(128)(4,1)S(1)}, s32[]{:S(2)}) async-start(s8[8388608]{0:T(1024)(128)(4,1)} %bitcast.36), calls=%async_computation.1 | async-start | bytes 8388608
  15.6 12.0 %collective-permute-start.11 = (f32[16,8,128]{2,1,0:T(8,128)S(1)}, f32[16,8,128]{2,1,0:T(8,128)S(1)}, u32[]{:S(2)}, u32[]{:S(2)}) collective-permute-start(f32[16,8,128]{2,1,0:T(8,128)S(1)} %shard_map.57.refs_3_), channel_id=1, source_target_pairs={{0,4},{1,5},{2,6},{3,7},{4,0},{5,1},{6,2},{7,3},{8,12},{9,13},{10,... | collective-permute-start | bytes 196616 | tf_op jit(solution)/shard_map/ppermute | solution.py:217
  17.0 10.6 %collective-permute-start.12 = (f32[16,8,128]{2,1,0:T(8,128)S(1)}, f32[16,8,128]{2,1,0:T(8,128)S(1)}, u32[]{:S(2)}, u32[]{:S(2)}) collective-permute-start(f32[16,8,128]{2,1,0:T(8,128)S(1)} %shard_map.57.refs_3_), channel_id=1, source_target_pairs={{0,8},{1,9},{2,10},{3,11},{4,12},{5,13},{6,14},{7,15},{8,0},{9,1},... | collective-permute-start | bytes 196616 | tf_op jit(solution)/shard_map/ppermute | solution.py:217
  19.6 8.0 %collective-permute-start.13 = (f32[16,8,128]{2,1,0:T(8,128)S(1)}, f32[16,8,128]{2,1,0:T(8,128)S(1)}, u32[]{:S(2)}, u32[]{:S(2)}) collective-permute-start(f32[16,8,128]{2,1,0:T(8,128)S(1)} %shard_map.57.refs_3_), channel_id=1, source_target_pairs={{0,12},{1,13},{2,14},{3,15},{4,8},{5,9},{6,10},{7,11},{8,4},{9,5},... | collective-permute-start | bytes 196616 | tf_op jit(solution)/shard_map/ppermute | solution.py:217
  19.6 1.5 %collective-permute-start.5 = (f32[32,8,128]{2,1,0:T(8,128)S(1)}, f32[32,8,128]{2,1,0:T(8,128)S(1)}, u32[]{:S(2)}, u32[]{:S(2)}) collective-permute-start(f32[32,8,128]{2,1,0:T(8,128)S(1)} %shard_map.61.refs_3_), channel_id=1, source_target_pairs={{0,16},{16,0},{32,48},{48,32},{64,80},{80,64},{96,112},{112,96},{1... | collective-permute-start | bytes 393224 | tf_op jit(solution)/shard_map/ppermute | solution.py:217
  24.2 6.6 %collective-permute-start.6 = (f32[16,8,128]{2,1,0:T(8,128)S(1)}, f32[16,8,128]{2,1,0:T(8,128)S(1)}, u32[]{:S(2)}, u32[]{:S(2)}) collective-permute-start(f32[16,8,128]{2,1,0:T(8,128)S(1)} %get-tuple-element.26), channel_id=1, source_target_pairs={{0,8},{1,9},{2,10},{3,11},{4,12},{5,13},{6,14},{7,15},{8,0},{9,1},... | collective-permute-start | bytes 196616 | tf_op jit(solution)/shard_map/ppermute | solution.py:217
  26.0 8.2 %collective-permute-start.7 = (f32[16,8,128]{2,1,0:T(8,128)S(1)}, f32[16,8,128]{2,1,0:T(8,128)S(1)}, u32[]{:S(2)}, u32[]{:S(2)}) collective-permute-start(f32[16,8,128]{2,1,0:T(8,128)S(1)} %get-tuple-element.27), channel_id=1, source_target_pairs={{0,4},{1,5},{2,6},{3,7},{4,0},{5,1},{6,2},{7,3},{8,12},{9,13},{10,... | collective-permute-start | bytes 196616 | tf_op jit(solution)/shard_map/ppermute | solution.py:217
  27.6 6.6 %collective-permute-start.8 = (f32[16,8,128]{2,1,0:T(8,128)S(1)}, f32[16,8,128]{2,1,0:T(8,128)S(1)}, u32[]{:S(2)}, u32[]{:S(2)}) collective-permute-start(f32[16,8,128]{2,1,0:T(8,128)S(1)} %get-tuple-element.28), channel_id=1, source_target_pairs={{0,12},{1,13},{2,14},{3,15},{4,8},{5,9},{6,10},{7,11},{8,4},{9,5},... | collective-permute-start | bytes 196616 | tf_op jit(solution)/shard_map/ppermute | solution.py:217
  29.6 2.2 %collective-permute-start.14 = (f32[32,8,128]{2,1,0:T(8,128)S(1)}, f32[32,8,128]{2,1,0:T(8,128)S(1)}, u32[]{:S(2)}, u32[]{:S(2)}) collective-permute-start(f32[32,8,128]{2,1,0:T(8,128)S(1)} %get-tuple-element.36), channel_id=1, source_target_pairs={{0,16},{16,0},{32,48},{48,32},{64,80},{80,64},{96,112},{112,96},{1... | collective-permute-start | bytes 393224 | tf_op jit(solution)/shard_map/ppermute | solution.py:217
  31.8 6.4 %collective-permute-start.15 = (f32[16,8,128]{2,1,0:T(8,128)S(1)}, f32[16,8,128]{2,1,0:T(8,128)S(1)}, u32[]{:S(2)}, u32[]{:S(2)}) collective-permute-start(f32[16,8,128]{2,1,0:T(8,128)S(1)} %get-tuple-element.38), channel_id=1, source_target_pairs={{0,208},{16,192},{32,240},{48,224},{64,144},{80,128},{96,176},{112... | collective-permute-start | bytes 196616 | tf_op jit(solution)/shard_map/ppermute | solution.py:217
  34.2 5.6 %collective-permute-start.9 = (f32[8,8,128]{2,1,0:T(8,128)S(1)}, f32[8,8,128]{2,1,0:T(8,128)S(1)}, u32[]{:S(2)}, u32[]{:S(2)}) collective-permute-start(f32[8,8,128]{2,1,0:T(8,128)S(1)} %get-tuple-element.30), channel_id=1, source_target_pairs={{0,3},{1,2},{2,1},{3,0},{4,7},{5,6},{6,5},{7,4},{8,11},{9,10},{10,... | collective-permute-start | bytes 98312 | tf_op jit(solution)/shard_map/ppermute | solution.py:217
  38.2 4.1 %collective-permute-start.16 = (f32[8,8,128]{2,1,0:T(8,128)S(1)}, f32[8,8,128]{2,1,0:T(8,128)S(1)}, u32[]{:S(2)}, u32[]{:S(2)}) collective-permute-start(f32[8,8,128]{2,1,0:T(8,128)S(1)} %get-tuple-element.40), channel_id=1, source_target_pairs={{0,80},{16,64},{32,112},{48,96},{64,16},{80,0},{96,48},{112,32},{1... | collective-permute-start | bytes 98312 | tf_op jit(solution)/shard_map/ppermute | solution.py:217
  39.8 3.6 %collective-permute-start.10 = (f32[4,8,128]{2,1,0:T(8,128)S(1)}, f32[4,8,128]{2,1,0:T(8,128)S(1)}, u32[]{:S(2)}, u32[]{:S(2)}) collective-permute-start(f32[4,8,128]{2,1,0:T(8,128)S(1)} %get-tuple-element.32), channel_id=1, source_target_pairs={{0,1},{1,0},{2,3},{3,2},{4,5},{5,4},{6,7},{7,6},{8,9},{9,8},{10,11... | collective-permute-start | bytes 49160 | tf_op jit(solution)/shard_map/ppermute | solution.py:217
  42.3 3.6 %collective-permute-start.17 = (f32[4,8,128]{2,1,0:T(8,128)S(1)}, f32[4,8,128]{2,1,0:T(8,128)S(1)}, u32[]{:S(2)}, u32[]{:S(2)}) collective-permute-start(f32[4,8,128]{2,1,0:T(8,128)S(1)} %get-tuple-element.42), channel_id=1, source_target_pairs={{0,48},{16,32},{32,16},{48,0},{64,112},{80,96},{96,80},{112,64},{1... | collective-permute-start | bytes 49160 | tf_op jit(solution)/shard_map/ppermute | solution.py:217

commit v7 on v5

--- a/solution.py
+++ b/solution.py
@@ -33,61 +33,20 @@
     return high, low
 
 
-def split_tiles_kernel(tiles, out, held, arrived):
-    slots = out.shape[0]
-    ring, size, side, _ = held.shape
-    chunks = slots // size
-
-    def fetch(chunk):
-        return pltpu.make_async_copy(tiles.at[pl.ds(chunk * size, size)], held.at[chunk % ring], arrived.at[chunk % ring])
-
-    for chunk in range(ring):
-        fetch(chunk).start()
-
-    def step(chunk, carry):
-        fetch(chunk).wait()
-        for offset in range(size):
-            high, low = split(held[chunk % ring, offset])
-            out[chunk * size + offset, :side, :] = high
-            out[chunk * size + offset, side:, :] = low
-
-        @pl.when(chunk + ring < chunks)
-        def _():
-            fetch(chunk + ring).start()
-
-        return carry
-
-    lax.fori_loop(0, chunks, step, 0)
-
-
-def split_tiles(tiles):
-    slots, side, _ = tiles.shape
-    return pl.pallas_call(
-        split_tiles_kernel,
-        out_shape=jax.ShapeDtypeStruct((slots, 2 * side, side), jnp.bfloat16),
-        in_specs=[ANY],
-        out_specs=VMEM,
-        scratch_shapes=[
-            pltpu.VMEM((PREP_RING, PIECE, side, side), jnp.float32),
-            pltpu.SemaphoreType.DMA((PREP_RING,)),
-        ],
-        compiler_params=pltpu.CompilerParams(vmem_limit_bytes=PLIM * 1024 * 1024),
-        cost_estimate=pl.CostEstimate(flops=PREP, bytes_accessed=8 * slots * side * side, transcendentals=0),
-    )(tiles)
-
-
 def take(refs, count):
     taken = refs[:count]
     del refs[:count]
     return taken
 
 
-def product_kernel(flipped, pieces, outputs, *refs):
+def product_kernel(flipped, pieces, markers, outputs, *refs):
     refs = list(refs)
-    places, pairs = take(refs, 2)
-    sources, parts = take(refs, pieces), take(refs, outputs)
+    places, tiles = take(refs, 2)
+    sources = take(refs, pieces)
+    take(refs, markers)
+    parts = take(refs, outputs)
     inputs, sums = refs
-    slots, _, side = pairs.shape
+    slots, _, side = tiles.shape
     vectors = sums.shape[1]
     start = 0
     for source in sources:
@@ -103,12 +62,12 @@
             slot = chunk * CHUNK + offset
             place = places[slot]
             row, col = place // 128, place % 128
-            pair = pairs[slot]
+            high, low = split(tiles[slot])
             if flipped:
                 value, target, contract = inputs[row], col, 0
             else:
                 value, target, contract = inputs[col], row, 1
-                pair = jnp.concatenate([pair[:side], pair[side:]], axis=1)
+            pair = jnp.concatenate([high, low], axis=contract)
             result = lax.dot_general(
                 jnp.concatenate([value, value], axis=1), pair,
                 (((1,), (contract,)), ((), ())), preferred_element_type=jnp.float32,
@@ -125,22 +84,23 @@
         start += part.shape[0]
 
 
-def product(flipped, places, pairs, sources, sizes):
-    slots, _, side = pairs.shape
+def product(flipped, places, tiles, sources, sizes, *markers):
+    slots, _, side = tiles.shape
     blocks = sum(source.shape[0] for source in sources)
     vectors = sources[0].shape[1]
-    return pl.pallas_call(
-        functools.partial(product_kernel, flipped, len(sources), len(sizes)),
-        out_shape=[jax.ShapeDtypeStruct((size, vectors, side), jnp.float32) for size in sizes],
-        in_specs=[SMEM] + [VMEM] * (1 + len(sources)),
-        out_specs=[VMEM] * len(sizes),
+    out_shape = [jax.ShapeDtypeStruct((size, vectors, side), jnp.float32) for size in sizes]
+    return pl.pallas_call(
+        functools.partial(product_kernel, flipped, len(sources), len(markers), len(sizes)),
+        out_shape=out_shape,
+        in_specs=[SMEM] + [VMEM] * (1 + len(sources) + len(markers)),
+        out_specs=[VMEM] * len(out_shape),
         scratch_shapes=[
             pltpu.VMEM((blocks + 8, 2 * vectors, side), jnp.bfloat16),
             pltpu.VMEM((sum(sizes) + 8, vectors, side), jnp.float32),
         ],
         compiler_params=pltpu.CompilerParams(vmem_limit_bytes=TLIM * 1024 * 1024),
-        cost_estimate=pl.CostEstimate(flops=FLOPS, bytes_accessed=4 * slots * side * side, transcendentals=0),
-    )(places, pairs, *sources)
+        cost_estimate=pl.CostEstimate(flops=FLOPS, bytes_accessed=4 * slots * 128 * 128, transcendentals=0),
+    )(places, tiles, *sources, *markers)
 
 
 def fetch_kernel(value, out):
@@ -155,6 +115,21 @@
         out_specs=VMEM,
         compiler_params=pltpu.CompilerParams(vmem_limit_bytes=4 * 1024 * 1024),
         cost_estimate=pl.CostEstimate(flops=FETCH_COST, bytes_accessed=1024, transcendentals=0),
+    )(value)
+
+
+def mark_kernel(value, out):
+    out[...] = value[0]
+
+
+def mark(value):
+    return pl.pallas_call(
+        mark_kernel,
+        out_shape=jax.ShapeDtypeStruct(value.shape[1:], value.dtype),
+        in_specs=[VMEM],
+        out_specs=VMEM,
+        compiler_params=pltpu.CompilerParams(vmem_limit_bytes=4 * 1024 * 1024),
+        cost_estimate=pl.CostEstimate(flops=PREP, bytes_accessed=1 << 24, transcendentals=0),
     )(value)
 
 
@@ -220,26 +195,30 @@
     col_offset = (cols // local_blocks) ^ lax.axis_index("row")
     row_offset = (row_offset & 12) + gray(row_offset & 3)
     near_z, near_x = col_offset >> 1 & 1, gray(col_offset >> 2)
-    col_offset = (col_offset & 1 ^ near_z ^ near_x & 1 ^ near_x >> 1) * 8 + near_x * 2 + near_z
-    places = (row_offset * local_blocks + rows % local_blocks) * 128 + col_offset * local_blocks + cols % local_blocks
+    other_core = col_offset & 1 ^ near_z ^ near_x & 1 ^ near_x >> 1
     slot = jnp.arange(slots, dtype=jnp.int32)
-    places = jnp.where(slot < tile_counts[0, 0], places, col_devices * local_blocks * 128 + row_devices * local_blocks)
+
+    def place(col_offset):
+        places = (row_offset * local_blocks + rows % local_blocks) * 128 + col_offset * local_blocks + cols % local_blocks
+        return jnp.where(slot < tile_counts[0, 0], places, col_devices * local_blocks * 128 + row_devices * local_blocks)
+
+    places = place((near_x >> 1) * 8 + other_core * 4 + (near_x & 1) * 2 + near_z)
+    scatter_places = place(other_core * 8 + near_x * 2 + near_z)
 
     local = fetch(own) if FETCH else own
     couple = join([local, swap(own, "col", 1)])
     pair = join([local, swap(own, "row", 3)], ROW_JOIN)
     close = join([couple, swap(couple, "col", 3)])
     quad = join([pair, swap(pair, "row", 5)], ROW_JOIN)
-    close, blocks = lax.optimization_barrier((close, tiles))
-    pairs = split_tiles(blocks[0, 0])
+    marker = mark(close)
     row_inputs = [close] + [swap(close, "col", offset) for offset in (4, 8, 12)]
-    half = join([quad, swap(quad, "row", 13)], ROW_JOIN)
-    col_inputs = [half, swap(half, "row", 1)]
+    half = join([quad, swap(quad, "row", 1)], ROW_JOIN)
+    col_inputs = [half, swap(half, "row", 13)]
 
     quarter, half_size = close.shape[0], half.shape[0]
-    row_parts = product(False, places, pairs, col_inputs, [quarter] * RING)
-    later_places, _ = lax.optimization_barrier((places, row_parts[0]))
-    col_parts = product(True, later_places, pairs, row_inputs, [half_size] * 2)
+    row_parts = product(False, places, tiles[0, 0], col_inputs, [quarter] * RING, marker)
+    later_places, _ = lax.optimization_barrier((scatter_places, row_parts[0]))
+    col_parts = product(True, later_places, tiles[0, 0], row_inputs, [half_size] * 2)
 
     across = fold([row_parts[0], swap(row_parts[2], "col", 8)], 1)
     close = fold([across[0], swap(row_parts[1], "col", 4), swap(row_parts[3], "col", 12)], 2)

time: 46.8 us -> 46.4 us (level)
  waiting for transfers between devices: 4.33 us -> 6.57 us
  Pallas kernels: 6.73 us -> 5.06 us
  starting transfers between devices: 33.2 us -> 32.4 us
    ppermute x18, waiting for transfers between devices: 4.33 us -> 6.57 us  [swap(): lax.ppermute(value, axis, [(j, j ^ offset) for j in range(lax.axis_size(a...]
    pallas_call x1, Pallas kernels: 1.56 us -> 0.01 us  [mark(): pl.pallas_call(mark_kernel, out_shape=jax.ShapeDtypeStruct(value.shape[1:...]
    ppermute x18, starting transfers between devices: 33.2 us -> 32.4 us  [swap(): lax.ppermute(value, axis, [(j, j ^ offset) for j in range(lax.axis_size(a...]
  transfers between devices with their start and end apart: 18 -> 18, of which waited for: 4 -> 8; matrix products, arithmetic and copies ran while one was open for 0% -> 0% of each run, Pallas kernels for 15% -> 11%
where the time goes in v7:
time: 46.4 us; the launch traced here: 46.2 us
  starting transfers between devices  32.4 us (70%)
  waiting for transfers between devices  6.57 us (14%)
  Pallas kernels  5.06 us (11%)
  local copies, waits for them, and re-layouts  0.77 us (2%)
  between operations  0.77 us (2%)
  other arithmetic  0.66 us (1%)
    ppermute x18, starting transfers between devices, swap(): lax.ppermute(value, axis, [(j, j ^ offset) for j in range(lax.axis_size(a...  32.4 us
    ppermute x18, waiting for transfers between devices, swap(): lax.ppermute(value, axis, [(j, j ^ offset) for j in range(lax.axis_size(a...  6.57 us
    pallas_call x2, Pallas kernels, product(): pl.pallas_call(functools.partial(product_kernel, flipped, len(sources), l...  4.97 us
  transfers between devices with their start and end apart: 18, of which 8 were waited for; matrix products, arithmetic and copies ran while one was open for 0% of the time, Pallas kernels for 11%

profile of v7, /device:TPU:1, one launch (start us, length us, event | category | flops | bytes accessed | tf_op | source)
XLA Modules:
  0.0 46.2 jit_solution(15034115568537398893)
XLA Ops:
  0.0 0.0 copy-start.1
  0.0 0.0 copy-start.2
  0.0 3.0 %collective-permute-start = (f32[4,8,128]{2,1,0:T(8,128)}, f32[4,8,128]{2,1,0:T(8,128)S(1)}, u32[]{:S(2)}, u32[]{:S(2)}) collective-permute-start(f32[4,8,128]{2,1,0:T(8,128)} %bitcast.51), channel_id=1, source_target_pairs={{0,48},{16,32},{32,16},{48,0},{64,112},{80,96},{96,80},{112,64},{1... | collective-permute-start | bytes 49160 | tf_op jit(solution)/shard_map/ppermute | solution.py:188
  3.0 3.0 %collective-permute-start.4 = (f32[4,8,128]{2,1,0:T(8,128)}, f32[4,8,128]{2,1,0:T(8,128)S(1)}, u32[]{:S(2)}, u32[]{:S(2)}) collective-permute-start(f32[4,8,128]{2,1,0:T(8,128)} %bitcast.52), channel_id=1, source_target_pairs={{0,1},{1,0},{2,3},{3,2},{4,5},{5,4},{6,7},{7,6},{8,9},{9,8},{10,11... | collective-permute-start | bytes 49160 | tf_op jit(solution)/shard_map/ppermute | solution.py:188
  6.0 0.0 copy-start
  6.0 0.7 %copy-done = f32[8,512]{1,0:T(8,128)S(1)} copy-done((f32[8,512]{1,0:T(8,128)S(1)}, f32[8,512]{1,0:T(8,128)}, u32[]{:S(2)}) %copy-start) | copy-done | bytes 16408
  7.4 0.0 copy-done.1
  7.4 0.0 copy-done.2
  7.5 0.0 collective-permute-done.refs_1_
  7.5 1.3 %collective-permute-start.1 = (f32[8,8,128]{2,1,0:T(8,128)S(1)}, f32[8,8,128]{2,1,0:T(8,128)S(1)}, u32[]{:S(2)}, u32[]{:S(2)}) collective-permute-start(f32[8,8,128]{2,1,0:T(8,128)S(1)} %shard_map.56.refs_0_), channel_id=1, source_target_pairs={{0,80},{16,64},{32,112},{48,96},{64,16},{80,0},{96,48},{112,32},{1... | collective-permute-start | bytes 98312 | tf_op jit(solution)/shard_map/ppermute | solution.py:188
  8.8 0.0 collective-permute-done.4.refs_1_
  8.8 3.4 %collective-permute-start.5 = (f32[8,8,128]{2,1,0:T(8,128)S(1)}, f32[8,8,128]{2,1,0:T(8,128)S(1)}, u32[]{:S(2)}, u32[]{:S(2)}) collective-permute-start(f32[8,8,128]{2,1,0:T(8,128)S(1)} %shard_map.59.refs_0_), channel_id=1, source_target_pairs={{0,3},{1,2},{2,1},{3,0},{4,7},{5,6},{6,5},{7,4},{8,11},{9,10},{10,... | collective-permute-start | bytes 98312 | tf_op jit(solution)/shard_map/ppermute | solution.py:188
  12.2 0.0 collective-permute-done.1.refs_1_
  12.2 1.0 %collective-permute-start.2 = (f32[16,8,128]{2,1,0:T(8,128)S(1)}, f32[16,8,128]{2,1,0:T(8,128)S(1)}, u32[]{:S(2)}, u32[]{:S(2)}) collective-permute-start(f32[16,8,128]{2,1,0:T(8,128)S(1)} %shard_map.57.refs_0_), channel_id=1, source_target_pairs={{0,16},{16,0},{32,48},{48,32},{64,80},{80,64},{96,112},{112,96},{1... | collective-permute-start | bytes 196616 | tf_op jit(solution)/shard_map/ppermute | solution.py:188
  13.2 0.5 %collective-permute-done.5.refs_1_ = f32[8,8,128]{2,1,0:T(8,128)S(1)} collective-permute-done((f32[8,8,128]{2,1,0:T(8,128)S(1)}, f32[8,8,128]{2,1,0:T(8,128)S(1)}, u32[]{:S(2)}, u32[]{:S(2)}) %collective-permute-start.5) | collective-permute-done | bytes 32800 | tf_op jit(solution)/shard_map/ppermute | solution.py:188
  13.7 0.0 slice-start.1
  13.7 0.4 collective-permute-done.2.refs_1_
  14.1 3.4 %collective-permute-start.3 = (f32[32,8,128]{2,1,0:T(8,128)S(1)}, f32[32,8,128]{2,1,0:T(8,128)S(1)}, u32[]{:S(2)}, u32[]{:S(2)}) collective-permute-start(f32[32,8,128]{2,1,0:T(8,128)S(1)} %shard_map.58.refs_2_), channel_id=1, source_target_pairs={{0,208},{16,192},{32,240},{48,224},{64,144},{80,128},{96,176},{112... | collective-permute-start | bytes 393224 | tf_op jit(solution)/shard_map/ppermute | solution.py:188
  17.5 1.3 %collective-permute-start.11 = (f32[16,8,128]{2,1,0:T(8,128)S(1)}, f32[16,8,128]{2,1,0:T(8,128)S(1)}, u32[]{:S(2)}, u32[]{:S(2)}) collective-permute-start(f32[16,8,128]{2,1,0:T(8,128)S(1)} %shard_map.60.value.refs_2_), channel_id=1, source_target_pairs={{0,4},{1,5},{2,6},{3,7},{4,0},{5,1},{6,2},{7,3},{8,12},{9,13},{10,... | collective-permute-start | bytes 196616 | tf_op jit(solution)/shard_map/ppermute | solution.py:188
  18.8 2.6 %collective-permute-start.12 = (f32[16,8,128]{2,1,0:T(8,128)S(1)}, f32[16,8,128]{2,1,0:T(8,128)S(1)}, u32[]{:S(2)}, u32[]{:S(2)}) collective-permute-start(f32[16,8,128]{2,1,0:T(8,128)S(1)} %shard_map.60.value.refs_2_), channel_id=1, source_target_pairs={{0,8},{1,9},{2,10},{3,11},{4,12},{5,13},{6,14},{7,15},{8,0},{9,1},... | collective-permute-start | bytes 196616 | tf_op jit(solution)/shard_map/ppermute | solution.py:188
  21.4 0.0 collective-permute-start.13
  21.4 0.3 collective-permute-done.3.refs_3_
  21.7 0.0 slice-done
  21.7 0.0 slice-done.1
  21.7 3.0 %shard_map.62 = (f32[16,8,128]{2,1,0:T(8,128)S(1)}, f32[16,8,128]{2,1,0:T(8,128)S(1)}, f32[16,8,128]{2,1,0:T(8,128)S(1)}, f32[16,8,128]{2,1,0:T(8,128)S(1)}) custom-call(s32[128]{0:T(128)S(1)} %get-tuple-element.39.refs_0_, f32[128,128,128]{2,1,0:T(8,128)S(1)} %bitcast.49, f32[32,8,128]{2,1,0:T(8,128)S(1)} %shard_map.58.refs_2_, ...), custom_call_target="tpu_custom_call" | custom-call | flops 20000000000 | bytes 8388608 | tf_op jit(solution)/shard_map/pallas_call | solution.py:92
  24.7 3.0 %collective-permute-start.6 = (f32[16,8,128]{2,1,0:T(8,128)S(1)}, f32[16,8,128]{2,1,0:T(8,128)S(1)}, u32[]{:S(2)}, u32[]{:S(2)}) collective-permute-start(f32[16,8,128]{2,1,0:T(8,128)S(1)} %get-tuple-element.23), channel_id=1, source_target_pairs={{0,8},{1,9},{2,10},{3,11},{4,12},{5,13},{6,14},{7,15},{8,0},{9,1},... | collective-permute-start | bytes 196616 | tf_op jit(solution)/shard_map/ppermute | solution.py:188
  27.7 0.4 collective-permute-start.7
  28.1 0.0 collective-permute-done.11.refs_3_
  28.1 0.4 collective-permute-start.8
  28.5 0.0 collective-permute-done.12.refs_4_
  28.5 0.0 collective-permute-done.13.refs_5_
  28.5 2.0 %shard_map.66 = (f32[32,8,128]{2,1,0:T(8,128)S(1)}, f32[32,8,128]{2,1,0:T(8,128)S(1)}) custom-call(s32[128]{0:T(128)S(1)} %compare_select_fusion.6.refs_0_, f32[128,128,128]{2,1,0:T(8,128)S(1)} %bitcast.50, f32[16,8,128]{2,1,0:T(8,128)S(1)} %shard_map.60.value.refs_2_, f32[16,8,128]{2,1,0:T(8,128)S(1)} %collective-permute-done.11.refs_3_, ...), custom_call_target="tpu_custom_call" | custom-call | flops 20000000000 | bytes 8388608 | tf_op jit(solution)/shard_map/pallas_call | solution.py:92
  30.5 1.2 %collective-permute-start.14 = (f32[32,8,128]{2,1,0:T(8,128)S(1)}, f32[32,8,128]{2,1,0:T(8,128)S(1)}, u32[]{:S(2)}, u32[]{:S(2)}) collective-permute-start(f32[32,8,128]{2,1,0:T(8,128)S(1)} %get-tuple-element.32), channel_id=1, source_target_pairs={{0,16},{16,0},{32,48},{48,32},{64,80},{80,64},{96,112},{112,96},{1... | collective-permute-start | bytes 393224 | tf_op jit(solution)/shard_map/ppermute | solution.py:188
  31.7 0.0 collective-permute-done.6.refs_1_
  31.7 1.0 %collective-permute-done.14.refs_1_ = f32[32,8,128]{2,1,0:T(8,128)S(1)} collective-permute-done((f32[32,8,128]{2,1,0:T(8,128)S(1)}, f32[32,8,128]{2,1,0:T(8,128)S(1)}, u32[]{:S(2)}, u32[]{:S(2)}) %collective-permute-start.14) | collective-permute-done | bytes 131104 | tf_op jit(solution)/shard_map/ppermute | solution.py:188
  32.7 2.4 %collective-permute-start.15 = (f32[16,8,128]{2,1,0:T(8,128)S(1)}, f32[16,8,128]{2,1,0:T(8,128)S(1)}, u32[]{:S(2)}, u32[]{:S(2)}) collective-permute-start(f32[16,8,128]{2,1,0:T(8,128)S(1)} %get-tuple-element.34), channel_id=1, source_target_pairs={{0,208},{16,192},{32,240},{48,224},{64,144},{80,128},{96,176},{112... | collective-permute-start | bytes 196616 | tf_op jit(solution)/shard_map/ppermute | solution.py:188
  35.0 0.0 collective-permute-done.7.refs_1_
  35.1 0.0 collective-permute-done.8.refs_2_
  35.1 2.7 %collective-permute-start.9 = (f32[8,8,128]{2,1,0:T(8,128)S(1)}, f32[8,8,128]{2,1,0:T(8,128)S(1)}, u32[]{:S(2)}, u32[]{:S(2)}) collective-permute-start(f32[8,8,128]{2,1,0:T(8,128)S(1)} %get-tuple-element.27), channel_id=1, source_target_pairs={{0,3},{1,2},{2,1},{3,0},{4,7},{5,6},{6,5},{7,4},{8,11},{9,10},{10,... | collective-permute-start | bytes 98312 | tf_op jit(solution)/shard_map/ppermute | solution.py:188
  37.8 0.2 collective-permute-done.15.refs_1_
  38.1 0.7 %collective-permute-start.16 = (f32[8,8,128]{2,1,0:T(8,128)S(1)}, f32[8,8,128]{2,1,0:T(8,128)S(1)}, u32[]{:S(2)}, u32[]{:S(2)}) collective-permute-start(f32[8,8,128]{2,1,0:T(8,128)S(1)} %get-tuple-element.36), channel_id=1, source_target_pairs={{0,80},{16,64},{32,112},{48,96},{64,16},{80,0},{96,48},{112,32},{1... | collective-permute-start | bytes 98312 | tf_op jit(solution)/shard_map/ppermute | solution.py:188
  38.8 1.3 %collective-permute-done.9.refs_1_ = f32[8,8,128]{2,1,0:T(8,128)S(1)} collective-permute-done((f32[8,8,128]{2,1,0:T(8,128)S(1)}, f32[8,8,128]{2,1,0:T(8,128)S(1)}, u32[]{:S(2)}, u32[]{:S(2)}) %collective-permute-start.9) | collective-permute-done | bytes 32800 | tf_op jit(solution)/shard_map/ppermute | solution.py:188
  40.1 1.2 %collective-permute-start.10 = (f32[4,8,128]{2,1,0:T(8,128)S(1)}, f32[4,8,128]{2,1,0:T(8,128)S(1)}, u32[]{:S(2)}, u32[]{:S(2)}) collective-permute-start(f32[4,8,128]{2,1,0:T(8,128)S(1)} %get-tuple-element.29), channel_id=1, source_target_pairs={{0,1},{1,0},{2,3},{3,2},{4,5},{5,4},{6,7},{7,6},{8,9},{9,8},{10,11... | collective-permute-start | bytes 49160 | tf_op jit(solution)/shard_map/ppermute | solution.py:188
  41.2 0.9 %collective-permute-done.16.refs_1_ = f32[8,8,128]{2,1,0:T(8,128)S(1)} collective-permute-done((f32[8,8,128]{2,1,0:T(8,128)S(1)}, f32[8,8,128]{2,1,0:T(8,128)S(1)}, u32[]{:S(2)}, u32[]{:S(2)}) %collective-permute-start.16) | collective-permute-done | bytes 32800 | tf_op jit(solution)/shard_map/ppermute | solution.py:188
  42.1 1.4 %collective-permute-start.17 = (f32[4,8,128]{2,1,0:T(8,128)S(1)}, f32[4,8,128]{2,1,0:T(8,128)S(1)}, u32[]{:S(2)}, u32[]{:S(2)}) collective-permute-start(f32[4,8,128]{2,1,0:T(8,128)S(1)} %get-tuple-element.38), channel_id=1, source_target_pairs={{0,48},{16,32},{32,16},{48,0},{64,112},{80,96},{96,80},{112,64},{1... | collective-permute-start | bytes 49160 | tf_op jit(solution)/shard_map/ppermute | solution.py:188
  43.6 0.0 collective-permute-done.10
  43.6 2.0 %collective-permute-done.17 = f32[4,8,128]{2,1,0:T(8,128)S(1)} collective-permute-done((f32[4,8,128]{2,1,0:T(8,128)S(1)}, f32[4,8,128]{2,1,0:T(8,128)S(1)}, u32[]{:S(2)}, u32[]{:S(2)}) %collective-permute-start.17) | collective-permute-done | bytes 16416 | tf_op jit(solution)/shard_map/ppermute | solution.py:188
  45.6 0.6 %add_bitcast_fusion = f32[8,512]{1,0:T(8,128)} fusion(f32[4,8,128]{2,1,0:T(8,128)S(1)} %collective-permute-done.17, f32[4,8,128]{2,1,0:T(8,128)S(1)} %get-tuple-element.37, f32[4,8,128]{2,1,0:T(8,128)S(1)} %get-tuple-element.28, f32[4,8,128]{2,1,0:T(8,128)S(1)} %collective-permute-done.10), kind=kLoop, calls=%fused_computation | loop fusion | flops 12288 | bytes 81920 | tf_op jit(solution)/shard_map/reshape | solution.py:231
  (17 shorter events, 0.1 us)
Async XLA Ops:
  0.0 7.4 %copy-start.1 = (s32[1,1,128]{2,1,0:T(1,128)S(1)}, s32[1,1,128]{2,1,0:T(1,128)}, u32[]{:S(2)}) copy-start(s32[1,1,128]{2,1,0:T(1,128)} %param.7) | copy-start | bytes 1540
  0.0 7.4 %copy-start.2 = (s32[1,1,128]{2,1,0:T(1,128)S(1)}, s32[1,1,128]{2,1,0:T(1,128)}, u32[]{:S(2)}) copy-start(s32[1,1,128]{2,1,0:T(1,128)} %param.6) | copy-start | bytes 1540
  0.0 7.5 %collective-permute-start = (f32[4,8,128]{2,1,0:T(8,128)}, f32[4,8,128]{2,1,0:T(8,128)S(1)}, u32[]{:S(2)}, u32[]{:S(2)}) collective-permute-start(f32[4,8,128]{2,1,0:T(8,128)} %bitcast.51), channel_id=1, source_target_pairs={{0,48},{16,32},{32,16},{48,0},{64,112},{80,96},{96,80},{112,64},{1... | collective-permute-start | bytes 49160 | tf_op jit(solution)/shard_map/ppermute | solution.py:188
  3.0 5.8 %collective-permute-start.4 = (f32[4,8,128]{2,1,0:T(8,128)}, f32[4,8,128]{2,1,0:T(8,128)S(1)}, u32[]{:S(2)}, u32[]{:S(2)}) collective-permute-start(f32[4,8,128]{2,1,0:T(8,128)} %bitcast.52), channel_id=1, source_target_pairs={{0,1},{1,0},{2,3},{3,2},{4,5},{5,4},{6,7},{7,6},{8,9},{9,8},{10,11... | collective-permute-start | bytes 49160 | tf_op jit(solution)/shard_map/ppermute | solution.py:188
  6.0 0.8 %copy-start = (f32[8,512]{1,0:T(8,128)S(1)}, f32[8,512]{1,0:T(8,128)}, u32[]{:S(2)}) copy-start(f32[8,512]{1,0:T(8,128)} %param.9) | copy-start | bytes 49156
  7.5 4.7 %collective-permute-start.1 = (f32[8,8,128]{2,1,0:T(8,128)S(1)}, f32[8,8,128]{2,1,0:T(8,128)S(1)}, u32[]{:S(2)}, u32[]{:S(2)}) collective-permute-start(f32[8,8,128]{2,1,0:T(8,128)S(1)} %shard_map.56.refs_0_), channel_id=1, source_target_pairs={{0,80},{16,64},{32,112},{48,96},{64,16},{80,0},{96,48},{112,32},{1... | collective-permute-start | bytes 98312 | tf_op jit(solution)/shard_map/ppermute | solution.py:188
  8.8 4.9 %collective-permute-start.5 = (f32[8,8,128]{2,1,0:T(8,128)S(1)}, f32[8,8,128]{2,1,0:T(8,128)S(1)}, u32[]{:S(2)}, u32[]{:S(2)}) collective-permute-start(f32[8,8,128]{2,1,0:T(8,128)S(1)} %shard_map.59.refs_0_), channel_id=1, source_target_pairs={{0,3},{1,2},{2,1},{3,0},{4,7},{5,6},{6,5},{7,4},{8,11},{9,10},{10,... | collective-permute-start | bytes 98312 | tf_op jit(solution)/shard_map/ppermute | solution.py:188
  12.2 1.9 %collective-permute-start.2 = (f32[16,8,128]{2,1,0:T(8,128)S(1)}, f32[16,8,128]{2,1,0:T(8,128)S(1)}, u32[]{:S(2)}, u32[]{:S(2)}) collective-permute-start(f32[16,8,128]{2,1,0:T(8,128)S(1)} %shard_map.57.refs_0_), channel_id=1, source_target_pairs={{0,16},{16,0},{32,48},{48,32},{64,80},{80,64},{96,112},{112,96},{1... | collective-permute-start | bytes 196616 | tf_op jit(solution)/shard_map/ppermute | solution.py:188
  13.7 8.0 %slice-start = ((s8[8388608]{0:T(1024)(128)(4,1)}), s8[4194304]{0:T(1024)(128)(4,1)S(1)}, s32[]{:S(2)}) async-start(s8[8388608]{0:T(1024)(128)(4,1)} %bitcast.47), calls=%async_computation | async-start | bytes 8388608
  13.7 8.0 %slice-start.1 = ((s8[8388608]{0:T(1024)(128)(4,1)}), s8[4194304]{0:T(1024)(128)(4,1)S(1)}, s32[]{:S(2)}) async-start(s8[8388608]{0:T(1024)(128)(4,1)} %bitcast.47), calls=%async_computation.1 | async-start | bytes 8388608
  14.1 7.6 %collective-permute-start.3 = (f32[32,8,128]{2,1,0:T(8,128)S(1)}, f32[32,8,128]{2,1,0:T(8,128)S(1)}, u32[]{:S(2)}, u32[]{:S(2)}) collective-permute-start(f32[32,8,128]{2,1,0:T(8,128)S(1)} %shard_map.58.refs_2_), channel_id=1, source_target_pairs={{0,208},{16,192},{32,240},{48,224},{64,144},{80,128},{96,176},{112... | collective-permute-start | bytes 393224 | tf_op jit(solution)/shard_map/ppermute | solution.py:188
  17.5 10.6 %collective-permute-start.11 = (f32[16,8,128]{2,1,0:T(8,128)S(1)}, f32[16,8,128]{2,1,0:T(8,128)S(1)}, u32[]{:S(2)}, u32[]{:S(2)}) collective-permute-start(f32[16,8,128]{2,1,0:T(8,128)S(1)} %shard_map.60.value.refs_2_), channel_id=1, source_target_pairs={{0,4},{1,5},{2,6},{3,7},{4,0},{5,1},{6,2},{7,3},{8,12},{9,13},{10,... | collective-permute-start | bytes 196616 | tf_op jit(solution)/shard_map/ppermute | solution.py:188
  18.8 9.7 %collective-permute-start.12 = (f32[16,8,128]{2,1,0:T(8,128)S(1)}, f32[16,8,128]{2,1,0:T(8,128)S(1)}, u32[]{:S(2)}, u32[]{:S(2)}) collective-permute-start(f32[16,8,128]{2,1,0:T(8,128)S(1)} %shard_map.60.value.refs_2_), channel_id=1, source_target_pairs={{0,8},{1,9},{2,10},{3,11},{4,12},{5,13},{6,14},{7,15},{8,0},{9,1},... | collective-permute-start | bytes 196616 | tf_op jit(solution)/shard_map/ppermute | solution.py:188
  21.4 7.1 %collective-permute-start.13 = (f32[16,8,128]{2,1,0:T(8,128)S(1)}, f32[16,8,128]{2,1,0:T(8,128)S(1)}, u32[]{:S(2)}, u32[]{:S(2)}) collective-permute-start(f32[16,8,128]{2,1,0:T(8,128)S(1)} %shard_map.60.value.refs_2_), channel_id=1, source_target_pairs={{0,12},{1,13},{2,14},{3,15},{4,8},{5,9},{6,10},{7,11},{8,4},{9,5},... | collective-permute-start | bytes 196616 | tf_op jit(solution)/shard_map/ppermute | solution.py:188
  24.7 7.0 %collective-permute-start.6 = (f32[16,8,128]{2,1,0:T(8,128)S(1)}, f32[16,8,128]{2,1,0:T(8,128)S(1)}, u32[]{:S(2)}, u32[]{:S(2)}) collective-permute-start(f32[16,8,128]{2,1,0:T(8,128)S(1)} %get-tuple-element.23), channel_id=1, source_target_pairs={{0,8},{1,9},{2,10},{3,11},{4,12},{5,13},{6,14},{7,15},{8,0},{9,1},... | collective-permute-start | bytes 196616 | tf_op jit(solution)/shard_map/ppermute | solution.py:188
  27.7 7.3 %collective-permute-start.7 = (f32[16,8,128]{2,1,0:T(8,128)S(1)}, f32[16,8,128]{2,1,0:T(8,128)S(1)}, u32[]{:S(2)}, u32[]{:S(2)}) collective-permute-start(f32[16,8,128]{2,1,0:T(8,128)S(1)} %get-tuple-element.24), channel_id=1, source_target_pairs={{0,4},{1,5},{2,6},{3,7},{4,0},{5,1},{6,2},{7,3},{8,12},{9,13},{10,... | collective-permute-start | bytes 196616 | tf_op jit(solution)/shard_map/ppermute | solution.py:188
  28.1 6.9 %collective-permute-start.8 = (f32[16,8,128]{2,1,0:T(8,128)S(1)}, f32[16,8,128]{2,1,0:T(8,128)S(1)}, u32[]{:S(2)}, u32[]{:S(2)}) collective-permute-start(f32[16,8,128]{2,1,0:T(8,128)S(1)} %get-tuple-element.25), channel_id=1, source_target_pairs={{0,12},{1,13},{2,14},{3,15},{4,8},{5,9},{6,10},{7,11},{8,4},{9,5},... | collective-permute-start | bytes 196616 | tf_op jit(solution)/shard_map/ppermute | solution.py:188
  30.5 2.2 %collective-permute-start.14 = (f32[32,8,128]{2,1,0:T(8,128)S(1)}, f32[32,8,128]{2,1,0:T(8,128)S(1)}, u32[]{:S(2)}, u32[]{:S(2)}) collective-permute-start(f32[32,8,128]{2,1,0:T(8,128)S(1)} %get-tuple-element.32), channel_id=1, source_target_pairs={{0,16},{16,0},{32,48},{48,32},{64,80},{80,64},{96,112},{112,96},{1... | collective-permute-start | bytes 393224 | tf_op jit(solution)/shard_map/ppermute | solution.py:188
  32.7 5.4 %collective-permute-start.15 = (f32[16,8,128]{2,1,0:T(8,128)S(1)}, f32[16,8,128]{2,1,0:T(8,128)S(1)}, u32[]{:S(2)}, u32[]{:S(2)}) collective-permute-start(f32[16,8,128]{2,1,0:T(8,128)S(1)} %get-tuple-element.34), channel_id=1, source_target_pairs={{0,208},{16,192},{32,240},{48,224},{64,144},{80,128},{96,176},{112... | collective-permute-start | bytes 196616 | tf_op jit(solution)/shard_map/ppermute | solution.py:188
  35.1 5.0 %collective-permute-start.9 = (f32[8,8,128]{2,1,0:T(8,128)S(1)}, f32[8,8,128]{2,1,0:T(8,128)S(1)}, u32[]{:S(2)}, u32[]{:S(2)}) collective-permute-start(f32[8,8,128]{2,1,0:T(8,128)S(1)} %get-tuple-element.27), channel_id=1, source_target_pairs={{0,3},{1,2},{2,1},{3,0},{4,7},{5,6},{6,5},{7,4},{8,11},{9,10},{10,... | collective-permute-start | bytes 98312 | tf_op jit(solution)/shard_map/ppermute | solution.py:188
  38.1 4.1 %collective-permute-start.16 = (f32[8,8,128]{2,1,0:T(8,128)S(1)}, f32[8,8,128]{2,1,0:T(8,128)S(1)}, u32[]{:S(2)}, u32[]{:S(2)}) collective-permute-start(f32[8,8,128]{2,1,0:T(8,128)S(1)} %get-tuple-element.36), channel_id=1, source_target_pairs={{0,80},{16,64},{32,112},{48,96},{64,16},{80,0},{96,48},{112,32},{1... | collective-permute-start | bytes 98312 | tf_op jit(solution)/shard_map/ppermute | solution.py:188
  40.1 3.5 %collective-permute-start.10 = (f32[4,8,128]{2,1,0:T(8,128)S(1)}, f32[4,8,128]{2,1,0:T(8,128)S(1)}, u32[]{:S(2)}, u32[]{:S(2)}) collective-permute-start(f32[4,8,128]{2,1,0:T(8,128)S(1)} %get-tuple-element.29), channel_id=1, source_target_pairs={{0,1},{1,0},{2,3},{3,2},{4,5},{5,4},{6,7},{7,6},{8,9},{9,8},{10,11... | collective-permute-start | bytes 49160 | tf_op jit(solution)/shard_map/ppermute | solution.py:188
  42.1 3.5 %collective-permute-start.17 = (f32[4,8,128]{2,1,0:T(8,128)S(1)}, f32[4,8,128]{2,1,0:T(8,128)S(1)}, u32[]{:S(2)}, u32[]{:S(2)}) collective-permute-start(f32[4,8,128]{2,1,0:T(8,128)S(1)} %get-tuple-element.38), channel_id=1, source_target_pairs={{0,48},{16,32},{32,16},{48,0},{64,112},{80,96},{96,80},{112,64},{1... | collective-permute-start | bytes 49160 | tf_op jit(solution)/shard_map/ppermute | solution.py:188

commit v8 on v7

--- a/solution.py
+++ b/solution.py
@@ -176,6 +176,26 @@
     )(*parts)
 
 
+def finish_kernel(*refs):
+    out = refs[-1]
+    total = refs[0][...]
+    for part in refs[1:-1]:
+        total = total + part[...]
+    blocks, _, side = total.shape
+    for block in range(blocks):
+        out[:, block * side:(block + 1) * side] = total[block]
+
+
+def finish(terms, like):
+    return pl.pallas_call(
+        finish_kernel,
+        out_shape=jax.ShapeDtypeStruct(like.shape, like.dtype),
+        in_specs=[VMEM] * len(terms),
+        out_specs=VMEM,
+        compiler_params=pltpu.CompilerParams(vmem_limit_bytes=4 * 1024 * 1024),
+    )(*terms)
+
+
 def body(tiles, tile_rows, tile_cols, tile_counts, vectors):
     vector_count, width = vectors.shape
     slots, side = tiles.shape[2:4]
@@ -227,8 +247,7 @@
     couple = fold([close[0], swap(close[1], "col", 3)], 2)
     pair = fold([quad[0], swap(quad[1], "row", 5)], 2, ROW_FOLD)
     terms = [couple[0], swap(couple[1], "col", 1), pair[0], swap(pair[1], "row", 3)]
-    total = functools.reduce(jnp.add, terms)
-    return total.transpose(1, 0, 2).reshape(vector_count, width)
+    return finish(terms, vectors)
 
 
 def solution(mesh):

time: 46.4 us -> 46.4 us (level)
  other arithmetic: 0.66 us -> 0.04 us
  Pallas kernels: 5.06 us -> 5.67 us
    reshape x1 -> x0, other arithmetic: 0.61 us -> none  [body(): return total.transpose(1, 0, 2).reshape(vector_count, width)]
    pallas_call x0 -> x1, Pallas kernels: none -> 0.61 us  [finish(): pl.pallas_call(finish_kernel, out_shape=jax.ShapeDtypeStruct(like.shape,...]
where the time goes in v8:
time: 46.4 us; the launch traced here: 46.2 us
  starting transfers between devices  32.4 us (70%)
  waiting for transfers between devices  6.55 us (14%)
  Pallas kernels  5.67 us (12%)
  between operations  0.79 us (2%)
  local copies, waits for them, and re-layouts  0.77 us (2%)
    ppermute x18, starting transfers between devices, swap(): lax.ppermute(value, axis, [(j, j ^ offset) for j in range(lax.axis_size(a...  32.4 us
    ppermute x18, waiting for transfers between devices, swap(): lax.ppermute(value, axis, [(j, j ^ offset) for j in range(lax.axis_size(a...  6.55 us
    pallas_call x2, Pallas kernels, product(): pl.pallas_call(functools.partial(product_kernel, flipped, len(sources), l...  4.97 us
  transfers between devices with their start and end apart: 18, of which 8 were waited for; matrix products, arithmetic and copies ran while one was open for 0% of the time, Pallas kernels for 11%

profile of v8, /device:TPU:1, one launch (start us, length us, event | category | flops | bytes accessed | tf_op | source)
XLA Modules:
  0.0 46.2 jit_solution(6385301850791175350)
XLA Ops:
  0.0 3.0 %collective-permute-start = (f32[4,8,128]{2,1,0:T(8,128)}, f32[4,8,128]{2,1,0:T(8,128)S(1)}, u32[]{:S(2)}, u32[]{:S(2)}) collective-permute-start(f32[4,8,128]{2,1,0:T(8,128)} %bitcast.47), channel_id=1, source_target_pairs={{0,48},{16,32},{32,16},{48,0},{64,112},{80,96},{96,80},{112,64},{1... | collective-permute-start | bytes 49160 | tf_op jit(solution)/shard_map/ppermute | solution.py:208
  3.0 3.0 %collective-permute-start.4 = (f32[4,8,128]{2,1,0:T(8,128)}, f32[4,8,128]{2,1,0:T(8,128)S(1)}, u32[]{:S(2)}, u32[]{:S(2)}) collective-permute-start(f32[4,8,128]{2,1,0:T(8,128)} %bitcast.48), channel_id=1, source_target_pairs={{0,1},{1,0},{2,3},{3,2},{4,5},{5,4},{6,7},{7,6},{8,9},{9,8},{10,11... | collective-permute-start | bytes 49160 | tf_op jit(solution)/shard_map/ppermute | solution.py:208
  6.0 0.0 copy-start
  6.0 0.7 %copy-done = f32[8,512]{1,0:T(8,128)S(1)} copy-done((f32[8,512]{1,0:T(8,128)S(1)}, f32[8,512]{1,0:T(8,128)}, u32[]{:S(2)}) %copy-start) | copy-done | bytes 16408
  6.8 0.0 copy-start.1
  6.8 0.0 copy-start.2
  7.5 0.0 copy-done.1
  7.5 0.0 copy-done.2
  7.5 0.0 collective-permute-done.refs_1_
  7.6 1.3 %collective-permute-start.1 = (f32[8,8,128]{2,1,0:T(8,128)S(1)}, f32[8,8,128]{2,1,0:T(8,128)S(1)}, u32[]{:S(2)}, u32[]{:S(2)}) collective-permute-start(f32[8,8,128]{2,1,0:T(8,128)S(1)} %shard_map.56.refs_0_), channel_id=1, source_target_pairs={{0,80},{16,64},{32,112},{48,96},{64,16},{80,0},{96,48},{112,32},{1... | collective-permute-start | bytes 98312 | tf_op jit(solution)/shard_map/ppermute | solution.py:208
  8.9 0.0 collective-permute-done.4.refs_1_
  8.9 3.3 %collective-permute-start.5 = (f32[8,8,128]{2,1,0:T(8,128)S(1)}, f32[8,8,128]{2,1,0:T(8,128)S(1)}, u32[]{:S(2)}, u32[]{:S(2)}) collective-permute-start(f32[8,8,128]{2,1,0:T(8,128)S(1)} %shard_map.59.refs_0_), channel_id=1, source_target_pairs={{0,3},{1,2},{2,1},{3,0},{4,7},{5,6},{6,5},{7,4},{8,11},{9,10},{10,... | collective-permute-start | bytes 98312 | tf_op jit(solution)/shard_map/ppermute | solution.py:208
  12.2 0.0 collective-permute-done.1.refs_1_
  12.2 1.0 %collective-permute-start.2 = (f32[16,8,128]{2,1,0:T(8,128)S(1)}, f32[16,8,128]{2,1,0:T(8,128)S(1)}, u32[]{:S(2)}, u32[]{:S(2)}) collective-permute-start(f32[16,8,128]{2,1,0:T(8,128)S(1)} %shard_map.57.refs_0_), channel_id=1, source_target_pairs={{0,16},{16,0},{32,48},{48,32},{64,80},{80,64},{96,112},{112,96},{1... | collective-permute-start | bytes 196616 | tf_op jit(solution)/shard_map/ppermute | solution.py:208
  13.2 0.5 %collective-permute-done.5.refs_1_ = f32[8,8,128]{2,1,0:T(8,128)S(1)} collective-permute-done((f32[8,8,128]{2,1,0:T(8,128)S(1)}, f32[8,8,128]{2,1,0:T(8,128)S(1)}, u32[]{:S(2)}, u32[]{:S(2)}) %collective-permute-start.5) | collective-permute-done | bytes 32800 | tf_op jit(solution)/shard_map/ppermute | solution.py:208
  13.8 0.0 slice-start.1
  13.8 0.3 collective-permute-done.2.refs_1_
  14.1 3.4 %collective-permute-start.3 = (f32[32,8,128]{2,1,0:T(8,128)S(1)}, f32[32,8,128]{2,1,0:T(8,128)S(1)}, u32[]{:S(2)}, u32[]{:S(2)}) collective-permute-start(f32[32,8,128]{2,1,0:T(8,128)S(1)} %shard_map.58.refs_2_), channel_id=1, source_target_pairs={{0,208},{16,192},{32,240},{48,224},{64,144},{80,128},{96,176},{112... | collective-permute-start | bytes 393224 | tf_op jit(solution)/shard_map/ppermute | solution.py:208
  17.5 1.3 %collective-permute-start.11 = (f32[16,8,128]{2,1,0:T(8,128)S(1)}, f32[16,8,128]{2,1,0:T(8,128)S(1)}, u32[]{:S(2)}, u32[]{:S(2)}) collective-permute-start(f32[16,8,128]{2,1,0:T(8,128)S(1)} %shard_map.60.value.refs_2_), channel_id=1, source_target_pairs={{0,4},{1,5},{2,6},{3,7},{4,0},{5,1},{6,2},{7,3},{8,12},{9,13},{10,... | collective-permute-start | bytes 196616 | tf_op jit(solution)/shard_map/ppermute | solution.py:208
  18.8 2.6 %collective-permute-start.12 = (f32[16,8,128]{2,1,0:T(8,128)S(1)}, f32[16,8,128]{2,1,0:T(8,128)S(1)}, u32[]{:S(2)}, u32[]{:S(2)}) collective-permute-start(f32[16,8,128]{2,1,0:T(8,128)S(1)} %shard_map.60.value.refs_2_), channel_id=1, source_target_pairs={{0,8},{1,9},{2,10},{3,11},{4,12},{5,13},{6,14},{7,15},{8,0},{9,1},... | collective-permute-start | bytes 196616 | tf_op jit(solution)/shard_map/ppermute | solution.py:208
  21.4 0.0 collective-permute-start.13
  21.4 0.2 collective-permute-done.3.refs_3_
  21.7 0.0 slice-done
  21.7 0.0 slice-done.1
  21.7 3.0 %shard_map.62 = (f32[16,8,128]{2,1,0:T(8,128)S(1)}, f32[16,8,128]{2,1,0:T(8,128)S(1)}, f32[16,8,128]{2,1,0:T(8,128)S(1)}, f32[16,8,128]{2,1,0:T(8,128)S(1)}) custom-call(s32[128]{0:T(128)S(1)} %compare_select_fusion.7.refs_0_, f32[128,128,128]{2,1,0:T(8,128)S(1)} %bitcast.45, f32[32,8,128]{2,1,0:T(8,128)S(1)} %shard_map.58.refs_2_, ...), custom_call_target="tpu_custom_call" | custom-call | flops 20000000000 | bytes 8388608 | tf_op jit(solution)/shard_map/pallas_call | solution.py:92
  24.7 3.0 %collective-permute-start.6 = (f32[16,8,128]{2,1,0:T(8,128)S(1)}, f32[16,8,128]{2,1,0:T(8,128)S(1)}, u32[]{:S(2)}, u32[]{:S(2)}) collective-permute-start(f32[16,8,128]{2,1,0:T(8,128)S(1)} %get-tuple-element.23), channel_id=1, source_target_pairs={{0,8},{1,9},{2,10},{3,11},{4,12},{5,13},{6,14},{7,15},{8,0},{9,1},... | collective-permute-start | bytes 196616 | tf_op jit(solution)/shard_map/ppermute | solution.py:208
  27.7 0.4 collective-permute-start.7
  28.1 0.0 collective-permute-done.11.refs_3_
  28.1 0.4 collective-permute-start.8
  28.5 0.0 collective-permute-done.12.refs_4_
  28.5 0.0 collective-permute-done.13.refs_5_
  28.5 2.0 %shard_map.66 = (f32[32,8,128]{2,1,0:T(8,128)S(1)}, f32[32,8,128]{2,1,0:T(8,128)S(1)}) custom-call(s32[128]{0:T(128)S(1)} %get-tuple-element.30.refs_0_, f32[128,128,128]{2,1,0:T(8,128)S(1)} %bitcast.46, f32[16,8,128]{2,1,0:T(8,128)S(1)} %shard_map.60.value.refs_2_, f32[16,8,128]{2,1,0:T(8,128)S(1)} %collective-permute-done.11.refs_3_, ...), custom_call_target="tpu_custom_call" | custom-call | flops 20000000000 | bytes 8388608 | tf_op jit(solution)/shard_map/pallas_call | solution.py:92
  30.4 1.3 %collective-permute-start.14 = (f32[32,8,128]{2,1,0:T(8,128)S(1)}, f32[32,8,128]{2,1,0:T(8,128)S(1)}, u32[]{:S(2)}, u32[]{:S(2)}) collective-permute-start(f32[32,8,128]{2,1,0:T(8,128)S(1)} %get-tuple-element.32), channel_id=1, source_target_pairs={{0,16},{16,0},{32,48},{48,32},{64,80},{80,64},{96,112},{112,96},{1... | collective-permute-start | bytes 393224 | tf_op jit(solution)/shard_map/ppermute | solution.py:208
  31.7 0.0 collective-permute-done.6.refs_1_
  31.7 1.0 %collective-permute-done.14.refs_1_ = f32[32,8,128]{2,1,0:T(8,128)S(1)} collective-permute-done((f32[32,8,128]{2,1,0:T(8,128)S(1)}, f32[32,8,128]{2,1,0:T(8,128)S(1)}, u32[]{:S(2)}, u32[]{:S(2)}) %collective-permute-start.14) | collective-permute-done | bytes 131104 | tf_op jit(solution)/shard_map/ppermute | solution.py:208
  32.7 2.4 %collective-permute-start.15 = (f32[16,8,128]{2,1,0:T(8,128)S(1)}, f32[16,8,128]{2,1,0:T(8,128)S(1)}, u32[]{:S(2)}, u32[]{:S(2)}) collective-permute-start(f32[16,8,128]{2,1,0:T(8,128)S(1)} %get-tuple-element.34), channel_id=1, source_target_pairs={{0,208},{16,192},{32,240},{48,224},{64,144},{80,128},{96,176},{112... | collective-permute-start | bytes 196616 | tf_op jit(solution)/shard_map/ppermute | solution.py:208
  35.0 0.0 collective-permute-done.7.refs_1_
  35.0 0.0 collective-permute-done.8.refs_2_
  35.1 2.8 %collective-permute-start.9 = (f32[8,8,128]{2,1,0:T(8,128)S(1)}, f32[8,8,128]{2,1,0:T(8,128)S(1)}, u32[]{:S(2)}, u32[]{:S(2)}) collective-permute-start(f32[8,8,128]{2,1,0:T(8,128)S(1)} %get-tuple-element.27), channel_id=1, source_target_pairs={{0,3},{1,2},{2,1},{3,0},{4,7},{5,6},{6,5},{7,4},{8,11},{9,10},{10,... | collective-permute-start | bytes 98312 | tf_op jit(solution)/shard_map/ppermute | solution.py:208
  37.8 0.2 collective-permute-done.15.refs_1_
  38.1 0.7 %collective-permute-start.16 = (f32[8,8,128]{2,1,0:T(8,128)S(1)}, f32[8,8,128]{2,1,0:T(8,128)S(1)}, u32[]{:S(2)}, u32[]{:S(2)}) collective-permute-start(f32[8,8,128]{2,1,0:T(8,128)S(1)} %get-tuple-element.36), channel_id=1, source_target_pairs={{0,80},{16,64},{32,112},{48,96},{64,16},{80,0},{96,48},{112,32},{1... | collective-permute-start | bytes 98312 | tf_op jit(solution)/shard_map/ppermute | solution.py:208
  38.8 1.3 %collective-permute-done.9.refs_1_ = f32[8,8,128]{2,1,0:T(8,128)S(1)} collective-permute-done((f32[8,8,128]{2,1,0:T(8,128)S(1)}, f32[8,8,128]{2,1,0:T(8,128)S(1)}, u32[]{:S(2)}, u32[]{:S(2)}) %collective-permute-start.9) | collective-permute-done | bytes 32800 | tf_op jit(solution)/shard_map/ppermute | solution.py:208
  40.1 1.1 %collective-permute-start.10 = (f32[4,8,128]{2,1,0:T(8,128)S(1)}, f32[4,8,128]{2,1,0:T(8,128)S(1)}, u32[]{:S(2)}, u32[]{:S(2)}) collective-permute-start(f32[4,8,128]{2,1,0:T(8,128)S(1)} %get-tuple-element.29), channel_id=1, source_target_pairs={{0,1},{1,0},{2,3},{3,2},{4,5},{5,4},{6,7},{7,6},{8,9},{9,8},{10,11... | collective-permute-start | bytes 49160 | tf_op jit(solution)/shard_map/ppermute | solution.py:208
  41.2 0.9 %collective-permute-done.16.refs_1_ = f32[8,8,128]{2,1,0:T(8,128)S(1)} collective-permute-done((f32[8,8,128]{2,1,0:T(8,128)S(1)}, f32[8,8,128]{2,1,0:T(8,128)S(1)}, u32[]{:S(2)}, u32[]{:S(2)}) %collective-permute-start.16) | collective-permute-done | bytes 32800 | tf_op jit(solution)/shard_map/ppermute | solution.py:208
  42.1 1.4 %collective-permute-start.17 = (f32[4,8,128]{2,1,0:T(8,128)S(1)}, f32[4,8,128]{2,1,0:T(8,128)S(1)}, u32[]{:S(2)}, u32[]{:S(2)}) collective-permute-start(f32[4,8,128]{2,1,0:T(8,128)S(1)} %get-tuple-element.38), channel_id=1, source_target_pairs={{0,48},{16,32},{32,16},{48,0},{64,112},{80,96},{96,80},{112,64},{1... | collective-permute-start | bytes 49160 | tf_op jit(solution)/shard_map/ppermute | solution.py:208
  43.6 0.0 collective-permute-done.10.refs_1_
  43.6 2.0 %collective-permute-done.17.refs_3_ = f32[4,8,128]{2,1,0:T(8,128)S(1)} collective-permute-done((f32[4,8,128]{2,1,0:T(8,128)S(1)}, f32[4,8,128]{2,1,0:T(8,128)S(1)}, u32[]{:S(2)}, u32[]{:S(2)}) %collective-permute-start.17) | collective-permute-done | bytes 16416 | tf_op jit(solution)/shard_map/ppermute | solution.py:208
  45.6 0.6 %shard_map.70 = f32[8,512]{1,0:T(8,128)} custom-call(f32[4,8,128]{2,1,0:T(8,128)S(1)} %get-tuple-element.28.refs_0_, f32[4,8,128]{2,1,0:T(8,128)S(1)} %collective-permute-done.10.refs_1_, f32[4,8,128]{2,1,0:T(8,128)S(1)} %get-tuple-element.37.refs_2_, f32[4,8,128]{2,1,0:T(8,128)S(1)} %collective-permute-done.17.refs_3_), custom_call_target="tpu_custom_call" | custom-call | tf_op jit(solution)/shard_map/pallas_call | solution.py:190
  (17 shorter events, 0.1 us)
Async XLA Ops:
  0.0 7.5 %collective-permute-start = (f32[4,8,128]{2,1,0:T(8,128)}, f32[4,8,128]{2,1,0:T(8,128)S(1)}, u32[]{:S(2)}, u32[]{:S(2)}) collective-permute-start(f32[4,8,128]{2,1,0:T(8,128)} %bitcast.47), channel_id=1, source_target_pairs={{0,48},{16,32},{32,16},{48,0},{64,112},{80,96},{96,80},{112,64},{1... | collective-permute-start | bytes 49160 | tf_op jit(solution)/shard_map/ppermute | solution.py:208
  3.0 5.8 %collective-permute-start.4 = (f32[4,8,128]{2,1,0:T(8,128)}, f32[4,8,128]{2,1,0:T(8,128)S(1)}, u32[]{:S(2)}, u32[]{:S(2)}) collective-permute-start(f32[4,8,128]{2,1,0:T(8,128)} %bitcast.48), channel_id=1, source_target_pairs={{0,1},{1,0},{2,3},{3,2},{4,5},{5,4},{6,7},{7,6},{8,9},{9,8},{10,11... | collective-permute-start | bytes 49160 | tf_op jit(solution)/shard_map/ppermute | solution.py:208
  6.0 0.8 %copy-start = (f32[8,512]{1,0:T(8,128)S(1)}, f32[8,512]{1,0:T(8,128)}, u32[]{:S(2)}) copy-start(f32[8,512]{1,0:T(8,128)} %param.9) | copy-start | bytes 49156
  6.8 0.7 %copy-start.1 = (s32[1,1,128]{2,1,0:T(1,128)S(1)}, s32[1,1,128]{2,1,0:T(1,128)}, u32[]{:S(2)}) copy-start(s32[1,1,128]{2,1,0:T(1,128)} %param.7) | copy-start | bytes 1540
  6.8 0.7 %copy-start.2 = (s32[1,1,128]{2,1,0:T(1,128)S(1)}, s32[1,1,128]{2,1,0:T(1,128)}, u32[]{:S(2)}) copy-start(s32[1,1,128]{2,1,0:T(1,128)} %param.6) | copy-start | bytes 1540
  7.6 4.6 %collective-permute-start.1 = (f32[8,8,128]{2,1,0:T(8,128)S(1)}, f32[8,8,128]{2,1,0:T(8,128)S(1)}, u32[]{:S(2)}, u32[]{:S(2)}) collective-permute-start(f32[8,8,128]{2,1,0:T(8,128)S(1)} %shard_map.56.refs_0_), channel_id=1, source_target_pairs={{0,80},{16,64},{32,112},{48,96},{64,16},{80,0},{96,48},{112,32},{1... | collective-permute-start | bytes 98312 | tf_op jit(solution)/shard_map/ppermute | solution.py:208
  8.9 4.9 %collective-permute-start.5 = (f32[8,8,128]{2,1,0:T(8,128)S(1)}, f32[8,8,128]{2,1,0:T(8,128)S(1)}, u32[]{:S(2)}, u32[]{:S(2)}) collective-permute-start(f32[8,8,128]{2,1,0:T(8,128)S(1)} %shard_map.59.refs_0_), channel_id=1, source_target_pairs={{0,3},{1,2},{2,1},{3,0},{4,7},{5,6},{6,5},{7,4},{8,11},{9,10},{10,... | collective-permute-start | bytes 98312 | tf_op jit(solution)/shard_map/ppermute | solution.py:208
  12.2 1.9 %collective-permute-start.2 = (f32[16,8,128]{2,1,0:T(8,128)S(1)}, f32[16,8,128]{2,1,0:T(8,128)S(1)}, u32[]{:S(2)}, u32[]{:S(2)}) collective-permute-start(f32[16,8,128]{2,1,0:T(8,128)S(1)} %shard_map.57.refs_0_), channel_id=1, source_target_pairs={{0,16},{16,0},{32,48},{48,32},{64,80},{80,64},{96,112},{112,96},{1... | collective-permute-start | bytes 196616 | tf_op jit(solution)/shard_map/ppermute | solution.py:208
  13.8 7.9 %slice-start = ((s8[8388608]{0:T(1024)(128)(4,1)}), s8[4194304]{0:T(1024)(128)(4,1)S(1)}, s32[]{:S(2)}) async-start(s8[8388608]{0:T(1024)(128)(4,1)} %bitcast.43), calls=%async_computation | async-start | bytes 8388608
  13.8 7.9 %slice-start.1 = ((s8[8388608]{0:T(1024)(128)(4,1)}), s8[4194304]{0:T(1024)(128)(4,1)S(1)}, s32[]{:S(2)}) async-start(s8[8388608]{0:T(1024)(128)(4,1)} %bitcast.43), calls=%async_computation.1 | async-start | bytes 8388608
  14.1 7.5 %collective-permute-start.3 = (f32[32,8,128]{2,1,0:T(8,128)S(1)}, f32[32,8,128]{2,1,0:T(8,128)S(1)}, u32[]{:S(2)}, u32[]{:S(2)}) collective-permute-start(f32[32,8,128]{2,1,0:T(8,128)S(1)} %shard_map.58.refs_2_), channel_id=1, source_target_pairs={{0,208},{16,192},{32,240},{48,224},{64,144},{80,128},{96,176},{112... | collective-permute-start | bytes 393224 | tf_op jit(solution)/shard_map/ppermute | solution.py:208
  17.5 10.6 %collective-permute-start.11 = (f32[16,8,128]{2,1,0:T(8,128)S(1)}, f32[16,8,128]{2,1,0:T(8,128)S(1)}, u32[]{:S(2)}, u32[]{:S(2)}) collective-permute-start(f32[16,8,128]{2,1,0:T(8,128)S(1)} %shard_map.60.value.refs_2_), channel_id=1, source_target_pairs={{0,4},{1,5},{2,6},{3,7},{4,0},{5,1},{6,2},{7,3},{8,12},{9,13},{10,... | collective-permute-start | bytes 196616 | tf_op jit(solution)/shard_map/ppermute | solution.py:208
  18.8 9.7 %collective-permute-start.12 = (f32[16,8,128]{2,1,0:T(8,128)S(1)}, f32[16,8,128]{2,1,0:T(8,128)S(1)}, u32[]{:S(2)}, u32[]{:S(2)}) collective-permute-start(f32[16,8,128]{2,1,0:T(8,128)S(1)} %shard_map.60.value.refs_2_), channel_id=1, source_target_pairs={{0,8},{1,9},{2,10},{3,11},{4,12},{5,13},{6,14},{7,15},{8,0},{9,1},... | collective-permute-start | bytes 196616 | tf_op jit(solution)/shard_map/ppermute | solution.py:208
  21.4 7.0 %collective-permute-start.13 = (f32[16,8,128]{2,1,0:T(8,128)S(1)}, f32[16,8,128]{2,1,0:T(8,128)S(1)}, u32[]{:S(2)}, u32[]{:S(2)}) collective-permute-start(f32[16,8,128]{2,1,0:T(8,128)S(1)} %shard_map.60.value.refs_2_), channel_id=1, source_target_pairs={{0,12},{1,13},{2,14},{3,15},{4,8},{5,9},{6,10},{7,11},{8,4},{9,5},... | collective-permute-start | bytes 196616 | tf_op jit(solution)/shard_map/ppermute | solution.py:208
  24.7 7.0 %collective-permute-start.6 = (f32[16,8,128]{2,1,0:T(8,128)S(1)}, f32[16,8,128]{2,1,0:T(8,128)S(1)}, u32[]{:S(2)}, u32[]{:S(2)}) collective-permute-start(f32[16,8,128]{2,1,0:T(8,128)S(1)} %get-tuple-element.23), channel_id=1, source_target_pairs={{0,8},{1,9},{2,10},{3,11},{4,12},{5,13},{6,14},{7,15},{8,0},{9,1},... | collective-permute-start | bytes 196616 | tf_op jit(solution)/shard_map/ppermute | solution.py:208
  27.7 7.4 %collective-permute-start.7 = (f32[16,8,128]{2,1,0:T(8,128)S(1)}, f32[16,8,128]{2,1,0:T(8,128)S(1)}, u32[]{:S(2)}, u32[]{:S(2)}) collective-permute-start(f32[16,8,128]{2,1,0:T(8,128)S(1)} %get-tuple-element.24), channel_id=1, source_target_pairs={{0,4},{1,5},{2,6},{3,7},{4,0},{5,1},{6,2},{7,3},{8,12},{9,13},{10,... | collective-permute-start | bytes 196616 | tf_op jit(solution)/shard_map/ppermute | solution.py:208
  28.1 7.0 %collective-permute-start.8 = (f32[16,8,128]{2,1,0:T(8,128)S(1)}, f32[16,8,128]{2,1,0:T(8,128)S(1)}, u32[]{:S(2)}, u32[]{:S(2)}) collective-permute-start(f32[16,8,128]{2,1,0:T(8,128)S(1)} %get-tuple-element.25), channel_id=1, source_target_pairs={{0,12},{1,13},{2,14},{3,15},{4,8},{5,9},{6,10},{7,11},{8,4},{9,5},... | collective-permute-start | bytes 196616 | tf_op jit(solution)/shard_map/ppermute | solution.py:208
  30.4 2.2 %collective-permute-start.14 = (f32[32,8,128]{2,1,0:T(8,128)S(1)}, f32[32,8,128]{2,1,0:T(8,128)S(1)}, u32[]{:S(2)}, u32[]{:S(2)}) collective-permute-start(f32[32,8,128]{2,1,0:T(8,128)S(1)} %get-tuple-element.32), channel_id=1, source_target_pairs={{0,16},{16,0},{32,48},{48,32},{64,80},{80,64},{96,112},{112,96},{1... | collective-permute-start | bytes 393224 | tf_op jit(solution)/shard_map/ppermute | solution.py:208
  32.7 5.4 %collective-permute-start.15 = (f32[16,8,128]{2,1,0:T(8,128)S(1)}, f32[16,8,128]{2,1,0:T(8,128)S(1)}, u32[]{:S(2)}, u32[]{:S(2)}) collective-permute-start(f32[16,8,128]{2,1,0:T(8,128)S(1)} %get-tuple-element.34), channel_id=1, source_target_pairs={{0,208},{16,192},{32,240},{48,224},{64,144},{80,128},{96,176},{112... | collective-permute-start | bytes 196616 | tf_op jit(solution)/shard_map/ppermute | solution.py:208
  35.1 5.0 %collective-permute-start.9 = (f32[8,8,128]{2,1,0:T(8,128)S(1)}, f32[8,8,128]{2,1,0:T(8,128)S(1)}, u32[]{:S(2)}, u32[]{:S(2)}) collective-permute-start(f32[8,8,128]{2,1,0:T(8,128)S(1)} %get-tuple-element.27), channel_id=1, source_target_pairs={{0,3},{1,2},{2,1},{3,0},{4,7},{5,6},{6,5},{7,4},{8,11},{9,10},{10,... | collective-permute-start | bytes 98312 | tf_op jit(solution)/shard_map/ppermute | solution.py:208
  38.1 4.1 %collective-permute-start.16 = (f32[8,8,128]{2,1,0:T(8,128)S(1)}, f32[8,8,128]{2,1,0:T(8,128)S(1)}, u32[]{:S(2)}, u32[]{:S(2)}) collective-permute-start(f32[8,8,128]{2,1,0:T(8,128)S(1)} %get-tuple-element.36), channel_id=1, source_target_pairs={{0,80},{16,64},{32,112},{48,96},{64,16},{80,0},{96,48},{112,32},{1... | collective-permute-start | bytes 98312 | tf_op jit(solution)/shard_map/ppermute | solution.py:208
  40.1 3.5 %collective-permute-start.10 = (f32[4,8,128]{2,1,0:T(8,128)S(1)}, f32[4,8,128]{2,1,0:T(8,128)S(1)}, u32[]{:S(2)}, u32[]{:S(2)}) collective-permute-start(f32[4,8,128]{2,1,0:T(8,128)S(1)} %get-tuple-element.29), channel_id=1, source_target_pairs={{0,1},{1,0},{2,3},{3,2},{4,5},{5,4},{6,7},{7,6},{8,9},{9,8},{10,11... | collective-permute-start | bytes 49160 | tf_op jit(solution)/shard_map/ppermute | solution.py:208
  42.1 3.5 %collective-permute-start.17 = (f32[4,8,128]{2,1,0:T(8,128)S(1)}, f32[4,8,128]{2,1,0:T(8,128)S(1)}, u32[]{:S(2)}, u32[]{:S(2)}) collective-permute-start(f32[4,8,128]{2,1,0:T(8,128)S(1)} %get-tuple-element.38), channel_id=1, source_target_pairs={{0,48},{16,32},{32,16},{48,0},{64,112},{80,96},{96,80},{112,64},{1... | collective-permute-start | bytes 49160 | tf_op jit(solution)/shard_map/ppermute | solution.py:208
